TPU v7x, 256 devices: a whole 4x4x8 slice. The times are simulated.
256 devices in a mesh: tile: 64 (over z, x, core), band: 4 (over y).
Axes of the slice: x: 4, y: 4, z: 8, core: 2. Of those that a mesh axis runs over, the one named last changes fastest.
Arguments:
- water_depth: float32 [512, 32768], P('band', 'tile'), may hold values from 0.05 to 2
- flux_east: float32 [512, 32768], P('band', 'tile'), may hold values from -3 to 3
- flux_south: float32 [512, 32768], P('band', 'tile'), may hold values from -3 to 3
- bed_level: float32 [512, 32768], P('band', 'tile'), may hold values from -4 to 4
- roughness: float32 [512, 32768], P('band', 'tile'), may hold values from 0.001 to 0.01
- link_rows: int32 [64, 4, 512], P('tile', 'band'), may hold values from 0 to 511, as said below
- link_blocks: int32 [64, 4, 512], P('tile', 'band'), may hold values from 0 to 8191, as said below
- reach_inverse: bfloat16 [8192, 128, 128], P(('tile', 'band'))
- reach_source: float32 [8192, 128], P(('tile', 'band')), may hold values from -6 to 6
- river_section: float32 [8192, 128], P(('tile', 'band')), may hold values from -4 to 4
- block_level: int32 [8192], P(('tile', 'band')), may hold values from 0 to 7, as said below
- block_down: int32 [8192], P(('tile', 'band')), may hold values from -1 to 8191, as said below
Outputs:
- final_depth: float32 [512, 32768], P('band', 'tile')
- final_east: float32 [512, 32768], P('band', 'tile')
- final_south: float32 [512, 32768], P('band', 'tile')
- discharge: float32 [8192, 128], P(('tile', 'band'))
Inputs may be any that keep to these rules, and one draw needn't show every extreme that they name: `link_rows`: the entries of one device's list are distinct. `link_blocks`: each entry names a block held by a device of the same band index as the list's device; at most 16 entries of one list name blocks held at one tile index, and in every draw some tile index receives exactly 16 from every list. `block_level`: every level occurs. `block_down`: a block below level 7 names a block whose level is one higher; the blocks of level 7 hold -1.
All inputs are finite; a program needn't handle non-finite values.
Results may differ from a plain program's by a relative error of at most 0.0003.
Values sent between devices are 32-bit elements; how exact they have to be, the bound alone decides.
No kernel may reach another device: no remote copies, remote signals or barrier semaphores. Data moves between devices by JAX's collectives and lax.ppermute only.
A program may use at most 64 MiB of HBM per device.

v0:
```python
import jax
import jax.numpy as jnp
from jax import lax
from jax.sharding import PartitionSpec as P

SUBSTEPS = 8
LEVELS = 8


GRAVITY = 9.81
TIME_STEP = 3.0
CELL_WIDTH = 30.0
DEPTH_FLOOR = 0.2
FRICTION_POWER = 7.0 / 3.0
LATERAL_RATE = 0.2
PLAIN_SHARE = 0.8
RIVER_SHARE = 0.25


def extended(x, sides, width):
    for axis, dim in sides:
        peers, length = (lax.axis_size(axis), x.shape[dim])
        up = [(i, (i + 1) % peers) for i in range(peers - 1)]
        down = [(j, i) for i, j in up]
        last = lax.slice_in_dim(x, length - width, length, axis=dim)
        initial = lax.slice_in_dim(x, 0, width, axis=dim)
        before = lax.ppermute(last, axis, up)
        after = lax.ppermute(initial, axis, down)
        x = jnp.concatenate([before, x, after], axis=dim)
    return x


def face_flux(here_level, ahead_level, here_bed, ahead_bed, here_rough, old_flux):
    flow_depth = jnp.maximum(
        jnp.maximum(here_level, ahead_level) - jnp.maximum(here_bed, ahead_bed), DEPTH_FLOOR
    )
    surface_slope = (ahead_level - here_level) / CELL_WIDTH
    driven_flux = old_flux - GRAVITY * TIME_STEP * flow_depth * surface_slope
    return driven_flux / (
        1.0
        + GRAVITY
        * TIME_STEP
        * here_rough
        * jnp.abs(old_flux)
        / jnp.power(flow_depth, FRICTION_POWER)
    )


def per_device(
    water_depth,
    flux_east,
    flux_south,
    bed_level,
    roughness,
    link_rows,
    link_blocks,
    reach_inverse,
    reach_source,
    river_section,
    block_level,
    block_down,
):
    tile_count = lax.axis_size("tile")
    band_count = lax.axis_size("band")
    tile_index = lax.axis_index("tile")
    band_index = lax.axis_index("band")
    rows_local, cols_local = water_depth.shape
    blocks_local = reach_source.shape[0]
    rows_here = link_rows.reshape(-1)
    blocks_here = link_blocks.reshape(-1)
    links_local = rows_here.shape[0]
    slot_count = 2 * links_local // tile_count
    start_level = bed_level + water_depth
    picked = start_level.reshape(-1, 128)[rows_here]
    dest_tile = blocks_here // blocks_local // band_count
    local_block = blocks_here % blocks_local
    matches = (dest_tile[:, None] == jnp.arange(tile_count)[None, :]).astype(jnp.int32)
    ranking = jnp.sum(matches * (jnp.cumsum(matches, axis=0) - 1), axis=1)
    position = dest_tile * slot_count + ranking
    slot_ids = (
        jnp.full((tile_count * slot_count,), -1, jnp.int32)
        .at[position]
        .set(local_block)
        .reshape(tile_count, slot_count)
    )
    block_range = jnp.arange(blocks_local)
    send_rows = (
        jnp.zeros((tile_count * slot_count, 128), jnp.float32)
        .at[position]
        .set(picked)
        .reshape(tile_count, slot_count, 128)
    )
    rows_in = lax.all_to_all(send_rows, "tile", split_axis=0, concat_axis=0, tiled=True)
    ids_in = lax.all_to_all(slot_ids, "tile", split_axis=0, concat_axis=0, tiled=True)
    lookup = (ids_in[..., None] == block_range).astype(jnp.float32)
    section_in = jnp.einsum("smk,kc->smc", lookup, river_section, precision=lax.Precision.HIGHEST)
    lateral = jnp.where(ids_in[..., None] >= 0, LATERAL_RATE * (rows_in - section_in), 0.0)
    returned = lax.all_to_all(lateral, "tile", split_axis=0, concat_axis=0, tiled=True)
    returned, lateral_in, ids_in = (returned, lateral, ids_in)
    lateral_mine = returned.reshape(-1, 128)[position]
    lookup_in = (ids_in[..., None] == block_range).astype(jnp.float32)
    lateral_sum = jnp.einsum("smk,smc->kc", lookup_in, lateral_in, precision=lax.Precision.HIGHEST)
    source = reach_source + RIVER_SHARE * lateral_sum
    inverse = reach_inverse.astype(jnp.float32)
    base_flow = jnp.einsum("bij,bj->bi", inverse, source, precision=lax.Precision.HIGHEST)
    column = inverse[:, :, 0]
    inflow_gain = inverse[:, -1, 0]
    block_end = base_flow[:, -1]
    block_total = blocks_local * tile_count * band_count
    my_index = tile_index * band_count + band_index
    inflow = jnp.zeros((blocks_local,), jnp.float32)
    route_table = (block_down[:, None] == jnp.arange(block_total)[None, :]).astype(jnp.float32)
    for level_now in range(LEVELS):
        outflow = block_end + inflow_gain * inflow
        level_share = jnp.where(block_level == level_now, outflow, 0.0)
        spread = jnp.dot(level_share, route_table, precision=lax.Precision.HIGHEST)
        summed = lax.psum(spread, ("tile", "band"))
        inflow = inflow + lax.dynamic_slice_in_dim(summed, my_index * blocks_local, blocks_local)
    discharge = base_flow + column * inflow[:, None]
    grid_cols = tile_count * cols_local
    grid_rows = band_count * rows_local
    ground = extended(jnp.stack([bed_level, roughness]), (("tile", 2), ("band", 1)), 1)
    ext_bed = ground[0]
    ext_rough = ground[1]
    face_columns = tile_index * cols_local + jnp.arange(cols_local + 1) - 1
    closed_columns = (face_columns < 0) | (face_columns >= grid_cols - 1)
    face_rows = band_index * rows_local + jnp.arange(rows_local + 1) - 1
    closed_rows = (face_rows < 0) | (face_rows >= grid_rows - 1)
    water_now = water_depth
    east_flux = flux_east
    south_flux = flux_south
    for substep in range(SUBSTEPS):
        padded = extended(
            jnp.stack([bed_level + water_now, east_flux, south_flux]), (("tile", 2), ("band", 1)), 1
        )
        ext_level = padded[0]
        ext_east = padded[1]
        ext_south = padded[2]
        east_faces = face_flux(
            ext_level[1:-1, :-1],
            ext_level[1:-1, 1:],
            ext_bed[1:-1, :-1],
            ext_bed[1:-1, 1:],
            ext_rough[1:-1, :-1],
            ext_east[1:-1, :-1],
        )
        east_faces = jnp.where(closed_columns[None, :], 0.0, east_faces)
        south_faces = face_flux(
            ext_level[:-1, 1:-1],
            ext_level[1:, 1:-1],
            ext_bed[:-1, 1:-1],
            ext_bed[1:, 1:-1],
            ext_rough[:-1, 1:-1],
            ext_south[:-1, 1:-1],
        )
        south_faces = jnp.where(closed_rows[:, None], 0.0, south_faces)
        water_now = water_now + TIME_STEP / CELL_WIDTH * (
            east_faces[:, :-1] - east_faces[:, 1:] + south_faces[:-1, :] - south_faces[1:, :]
        )
        east_flux = east_faces[:, 1:]
        south_flux = south_faces[1:, :]
    final_depth = (
        water_now.reshape(-1, 128)
        .at[rows_here]
        .add(-PLAIN_SHARE * lateral_mine)
        .reshape(rows_local, cols_local)
    )
    return (final_depth, east_flux, south_flux, discharge)


def solution(mesh):
    placed = (
        P("band", "tile"),
        P("band", "tile"),
        P("band", "tile"),
        P("band", "tile"),
        P("band", "tile"),
        P("tile", "band", None),
        P("tile", "band", None),
        P(("tile", "band"), None, None),
        P(("tile", "band"), None),
        P(("tile", "band"), None),
        P(("tile", "band")),
        P(("tile", "band")),
    )
    return jax.shard_map(
        per_device,
        mesh=mesh,
        in_specs=placed,
        out_specs=(
            P("band", "tile"),
            P("band", "tile"),
            P("band", "tile"),
            P(("tile", "band"), None),
        ),
        check_vma=False,
    )
```

profile of v0, /device:TPU:2, one launch (start us, length us, event | category | flops | bytes accessed | tf_op | source)
XLA Modules:
  0.0 845.8 jit_solution(11655497092111342717)
XLA Ops:
  7.4 3.8 collective-permute-start.5
  13.7 3.8 collective-permute-done.4
  18.8 4.5 collective-permute-start.6
  24.9 4.5 collective-permute-start.2
  37.8 3.8 collective-permute-done.8
  43.0 4.8 collective-permute-start.10
  56.0 3.8 collective-permute-done.12
  61.3 4.8 collective-permute-start.14
  74.3 3.8 collective-permute-done.16
  79.5 4.8 collective-permute-start.18
  92.5 3.8 collective-permute-done.20
  97.7 4.8 collective-permute-start.22
  108.3 2.9 collective-permute-start.24
  111.2 2.4 scatter_custom_fusion
  114.3 32.7 %all-to-all-start = ((s32[64,1,16]{2,1,0:T(1,128)}), s32[64,1,16]{2,1,0:T(1,128)}, u32[]{:S(2)}, u32[]{:S(2)}) async-start(s32[64,1,16]{2,1,0:T(1,128)} %bitcast.60), calls=%async_computation | async-start | bytes 65536 | tf_op jit(solution)/shard_map/all_to_all | solution.py:94
  149.0 5.4 collective-permute-start.26
  164.9 3.8 collective-permute-done.28
  170.1 4.5 collective-permute-start.30
  182.1 4.0 scatter_custom_fusion.1
  188.1 4.8 collective-permute-start.34
  192.9 16.9 %all-to-all-start.1 = ((f32[64,16,128]{2,1,0:T(8,128)}), f32[64,16,128]{2,1,0:T(8,128)S(1)}, u32[]{:S(2)}, u32[]{:S(2)}) async-start(f32[64,16,128]{2,1,0:T(8,128)} %bitcast.62), calls=%async_computation.1 | async-start | bytes 1048576 | tf_op jit(solution)/shard_map/all_to_all | solution.py:93
  212.9 14.3 %all-to-all-done.1 = f32[64,16,128]{2,1,0:T(8,128)S(1)} async-done(((f32[64,16,128]{2,1,0:T(8,128)}), f32[64,16,128]{2,1,0:T(8,128)S(1)}, u32[]{:S(2)}, u32[]{:S(2)}) %all-to-all-start.1) | async-done | bytes 524320 | tf_op jit(solution)/shard_map/all_to_all | solution.py:93
  229.3 5.9 all-to-all-start.2
  239.5 76.8 %psum.56 = f32[8192]{0:T(1024)S(1)} all-reduce(f32[8192]{0:T(1024)S(1)} %bitcast.210), channel_id=1, replica_groups=mesh['tile'=64,'band'=4] {'tile','band'}, use_global_device_ids=true, to_apply=%region_6.7 | all-reduce | flops 8192 | bytes 65536 | tf_op jit(solution)/shard_map/psum | solution.py:117
  316.8 74.6 %psum.57 = f32[8192]{0:T(1024)S(1)} all-reduce(f32[8192]{0:T(1024)S(1)} %bitcast.211), channel_id=1, replica_groups=mesh['tile'=64,'band'=4] {'tile','band'}, use_global_device_ids=true, to_apply=%region_7.8 | all-reduce | flops 8192 | bytes 65536 | tf_op jit(solution)/shard_map/psum | solution.py:117
  391.8 73.5 %psum.58 = f32[8192]{0:T(1024)S(1)} all-reduce(f32[8192]{0:T(1024)S(1)} %bitcast.212), channel_id=1, replica_groups=mesh['tile'=64,'band'=4] {'tile','band'}, use_global_device_ids=true, to_apply=%region_8.9 | all-reduce | flops 8192 | bytes 65536 | tf_op jit(solution)/shard_map/psum | solution.py:117
  465.9 74.5 %psum.59 = f32[8192]{0:T(1024)S(1)} all-reduce(f32[8192]{0:T(1024)S(1)} %bitcast.213), channel_id=1, replica_groups=mesh['tile'=64,'band'=4] {'tile','band'}, use_global_device_ids=true, to_apply=%region_9.10 | all-reduce | flops 8192 | bytes 65536 | tf_op jit(solution)/shard_map/psum | solution.py:117
  540.9 73.5 %psum.60 = f32[8192]{0:T(1024)S(1)} all-reduce(f32[8192]{0:T(1024)S(1)} %bitcast.214), channel_id=1, replica_groups=mesh['tile'=64,'band'=4] {'tile','band'}, use_global_device_ids=true, to_apply=%region_10.11 | all-reduce | flops 8192 | bytes 65536 | tf_op jit(solution)/shard_map/psum | solution.py:117
  615.0 74.6 %psum.61 = f32[8192]{0:T(1024)S(1)} all-reduce(f32[8192]{0:T(1024)S(1)} %bitcast.215), channel_id=1, replica_groups=mesh['tile'=64,'band'=4] {'tile','band'}, use_global_device_ids=true, to_apply=%region_11.12 | all-reduce | flops 8192 | bytes 65536 | tf_op jit(solution)/shard_map/psum | solution.py:117
  690.2 73.5 %psum.62 = f32[8192]{0:T(1024)S(1)} all-reduce(f32[8192]{0:T(1024)S(1)} %bitcast.216), channel_id=1, replica_groups=mesh['tile'=64,'band'=4] {'tile','band'}, use_global_device_ids=true, to_apply=%region_12.13 | all-reduce | flops 8192 | bytes 65536 | tf_op jit(solution)/shard_map/psum | solution.py:117
  764.2 74.4 %psum.63 = f32[8192]{0:T(1024)S(1)} all-reduce(f32[8192]{0:T(1024)S(1)} %bitcast.209), channel_id=1, replica_groups=mesh['tile'=64,'band'=4] {'tile','band'}, use_global_device_ids=true, to_apply=%region_13.14 | all-reduce | flops 8192 | bytes 65536 | tf_op jit(solution)/shard_map/psum | solution.py:117
  840.1 4.7 scatter_custom_fusion.2
  (188 shorter events, 94.6 us)
Async XLA Ops:
  2.9 20.5 %collective-permute-start.1 = (f32[3,128,1]{2,1,0:T(8,128)S(1)}, f32[3,128,1]{2,1,0:T(8,128)S(1)}, u32[]{:S(2)}, u32[]{:S(2)}) collective-permute-start(f32[3,128,1]{2,1,0:T(8,128)S(1)} %get-tuple-element.82), channel_id=1, source_target_pairs={{4,0},{8,4},{12,8},{16,12},{20,16},{24,20},{28,24},{32,28},{36,32}... | collective-permute-start | bytes 4616 | tf_op jit(solution)/shard_map/ppermute | solution.py:28
  4.8 18.6 %collective-permute-start = (f32[3,128,1]{2,1,0:T(8,128)S(1)}, f32[3,128,1]{2,1,0:T(8,128)S(1)}, u32[]{:S(2)}, u32[]{:S(2)}) collective-permute-start(f32[3,128,1]{2,1,0:T(8,128)S(1)} %get-tuple-element.81), channel_id=1, source_target_pairs={{0,4},{4,8},{8,12},{12,16},{16,20},{20,24},{24,28},{28,32},{32,36}... | collective-permute-start | bytes 4616 | tf_op jit(solution)/shard_map/ppermute | solution.py:27
  7.4 6.3 collective-permute-start.5
  11.2 6.3 collective-permute-start.4
  17.5 11.9 %collective-permute-start.7 = (f32[2,1,514]{2,1,0:T(1,128)S(1)}, f32[2,1,514]{2,1,0:T(1,128)S(1)}, u32[]{:S(2)}, u32[]{:S(2)}) collective-permute-start(f32[2,1,514]{2,1,0:T(1,128)S(1)} %get-tuple-element.80), channel_id=1, source_target_pairs={{1,0},{2,1},{3,2},{5,4},{6,5},{7,6},{9,8},{10,9},{11,10},{13,12},{... | collective-permute-start | bytes 12344 | tf_op jit(solution)/shard_map/ppermute | solution.py:28
  18.8 10.6 %collective-permute-start.6 = (f32[2,1,514]{2,1,0:T(1,128)S(1)}, f32[2,1,514]{2,1,0:T(1,128)S(1)}, u32[]{:S(2)}, u32[]{:S(2)}) collective-permute-start(f32[2,1,514]{2,1,0:T(1,128)S(1)} %get-tuple-element.79), channel_id=1, source_target_pairs={{0,1},{1,2},{2,3},{4,5},{5,6},{6,7},{8,9},{9,10},{10,11},{12,13},{... | collective-permute-start | bytes 12344 | tf_op jit(solution)/shard_map/ppermute | solution.py:27
  23.6 6.2 collective-permute-start.3
  24.9 5.9 collective-permute-start.2
  34.6 7.0 collective-permute-start.8
  41.7 6.1 collective-permute-start.11
  43.0 6.2 collective-permute-start.10
  52.9 7.0 collective-permute-start.12
  60.0 6.2 collective-permute-start.15
  61.3 6.2 collective-permute-start.14
  71.1 7.0 collective-permute-start.16
  78.2 7.4 collective-permute-start.19
  79.5 6.2 collective-permute-start.18
  89.3 7.0 collective-permute-start.20
  96.4 6.2 collective-permute-start.23
  97.7 6.2 collective-permute-start.22
  106.3 40.7 %collective-permute-start.25 = (f32[3,128,1]{2,1,0:T(8,128)S(1)}, f32[3,128,1]{2,1,0:T(8,128)S(1)}, u32[]{:S(2)}, u32[]{:S(2)}) collective-permute-start(f32[3,128,1]{2,1,0:T(8,128)S(1)} %get-tuple-element.70), channel_id=1, source_target_pairs={{4,0},{8,4},{12,8},{16,12},{20,16},{24,20},{28,24},{32,28},{36,32}... | collective-permute-start | bytes 4616 | tf_op jit(solution)/shard_map/ppermute | solution.py:28
  108.3 38.7 %collective-permute-start.24 = (f32[3,128,1]{2,1,0:T(8,128)S(1)}, f32[3,128,1]{2,1,0:T(8,128)S(1)}, u32[]{:S(2)}, u32[]{:S(2)}) collective-permute-start(f32[3,128,1]{2,1,0:T(8,128)S(1)} %get-tuple-element.69), channel_id=1, source_target_pairs={{0,4},{4,8},{8,12},{12,16},{16,20},{20,24},{24,28},{28,32},{32,36}... | collective-permute-start | bytes 4616 | tf_op jit(solution)/shard_map/ppermute | solution.py:27
  114.3 78.6 %all-to-all-start = ((s32[64,1,16]{2,1,0:T(1,128)}), s32[64,1,16]{2,1,0:T(1,128)}, u32[]{:S(2)}, u32[]{:S(2)}) async-start(s32[64,1,16]{2,1,0:T(1,128)} %bitcast.60), calls=%async_computation | async-start | bytes 65536 | tf_op jit(solution)/shard_map/all_to_all | solution.py:94
  147.7 9.0 %collective-permute-start.27 = (f32[3,1,514]{2,1,0:T(1,128)}, f32[3,1,514]{2,1,0:T(1,128)S(1)}, u32[]{:S(2)}, u32[]{:S(2)}) collective-permute-start(f32[3,1,514]{2,1,0:T(1,128)} %get-tuple-element.30), channel_id=1, source_target_pairs={{1,0},{2,1},{3,2},{5,4},{6,5},{7,6},{9,8},{10,9},{11,10},{13,12},{... | collective-permute-start | bytes 18512 | tf_op jit(solution)/shard_map/ppermute | solution.py:28
  149.0 7.7 collective-permute-start.26
  161.7 7.0 collective-permute-start.28
  177.8 8.4 collective-permute-start.33
  179.7 7.0 collective-permute-start.32
  186.8 23.8 %collective-permute-start.35 = (f32[3,1,514]{2,1,0:T(1,128)S(1)}, f32[3,1,514]{2,1,0:T(1,128)S(1)}, u32[]{:S(2)}, u32[]{:S(2)}) collective-permute-start(f32[3,1,514]{2,1,0:T(1,128)S(1)} %get-tuple-element.26), channel_id=1, source_target_pairs={{1,0},{2,1},{3,2},{5,4},{6,5},{7,6},{9,8},{10,9},{11,10},{13,12},{... | collective-permute-start | bytes 18512 | tf_op jit(solution)/shard_map/ppermute | solution.py:28
  188.1 22.5 %collective-permute-start.34 = (f32[3,1,514]{2,1,0:T(1,128)S(1)}, f32[3,1,514]{2,1,0:T(1,128)S(1)}, u32[]{:S(2)}, u32[]{:S(2)}) collective-permute-start(f32[3,1,514]{2,1,0:T(1,128)S(1)} %get-tuple-element.25), channel_id=1, source_target_pairs={{0,1},{1,2},{2,3},{4,5},{5,6},{6,7},{8,9},{9,10},{10,11},{12,13},{... | collective-permute-start | bytes 18512 | tf_op jit(solution)/shard_map/ppermute | solution.py:27
  192.9 34.4 %all-to-all-start.1 = ((f32[64,16,128]{2,1,0:T(8,128)}), f32[64,16,128]{2,1,0:T(8,128)S(1)}, u32[]{:S(2)}, u32[]{:S(2)}) async-start(f32[64,16,128]{2,1,0:T(8,128)} %bitcast.62), calls=%async_computation.1 | async-start | bytes 1048576 | tf_op jit(solution)/shard_map/all_to_all | solution.py:93
  229.3 610.8 %all-to-all-start.2 = ((f32[64,16,128]{2,1,0:T(8,128)}), f32[64,16,128]{2,1,0:T(8,128)S(1)}, u32[]{:S(2)}, u32[]{:S(2)}) async-start(f32[64,16,128]{2,1,0:T(8,128)} %fusion.1), calls=%async_computation.2 | async-start | bytes 1048576 | tf_op jit(solution)/shard_map/all_to_all | solution.py:98
  (23 other events, 504.5 us)
where the time goes:
time: 858 us; the launch traced here: 846 us
  blocking collectives  596 us (69%)
  starting transfers between devices  151 us (18%)
  waiting for transfers between devices  47.8 us (6%)
  other arithmetic  28.1 us (3%)
  local copies, waits for them, and re-layouts  11.8 us (1%)
  matrix products  9.47 us (1%)
    psum x8, blocking collectives, per_device(): summed = lax.psum(spread, ('tile', 'band'))  596 us
    ppermute x18, starting transfers between devices, extended(): before = lax.ppermute(last, axis, up)  64.8 us
    all_to_all x1, starting transfers between devices, per_device(): lax.all_to_all(slot_ids, 'tile', split_axis=0, concat_axis=0, tiled=True)  32.7 us
    ppermute x18, starting transfers between devices, extended(): after = lax.ppermute(initial, axis, down)  30.8 us
    ppermute x18, waiting for transfers between devices, extended(): before = lax.ppermute(last, axis, up)  29.6 us
  transfers between devices with their start and end apart: 39, of which 20 were waited for; matrix products, arithmetic and copies ran while one was open for 3% of the time, Pallas kernels for 0%

commit v1 on v0

v1 whole, which is shorter than its diff:
```python
import functools

import jax
import jax.numpy as jnp
from jax import lax
from jax.experimental import pallas as pl
from jax.experimental.pallas import tpu as pltpu
from jax.sharding import PartitionSpec as P

SUBSTEPS = 8
LEVELS = 8
HALO = 8
LANES = 128
SLOTS = 16
CHUNK = SLOTS + 1

GRAVITY = 9.81
TIME_STEP = 3.0
CELL_WIDTH = 30.0
DEPTH_FLOOR = 0.2
FRICTION_POWER = 7.0 / 3.0
LATERAL_RATE = 0.2
PLAIN_SHARE = 0.8
RIVER_SHARE = 0.25

F32 = jnp.float32
BF16 = jnp.bfloat16
VMEM = pl.BlockSpec(memory_space=pltpu.VMEM)
SMEM = pl.BlockSpec(memory_space=pltpu.SMEM)


def iota(shape, dim):
    return lax.broadcasted_iota(jnp.int32, shape, dim)


def halves(x):
    hi = x.astype(BF16)
    lo = (x - hi.astype(F32)).astype(BF16)
    return hi, lo


def paired(x):
    hi, lo = halves(x)
    return jnp.concatenate([hi, lo], axis=1)


def fold(x):
    return x[:, :LANES] + x[:, LANES:]


def mm(a, b, dims=((1,), (0,))):
    return lax.dot_general(a, b, (dims, ((), ())), preferred_element_type=F32)


def pack_kernel(water, bed, link_rows, link_blocks, table, out, slots):
    rows = link_rows[...]
    blocks = link_blocks[...]
    links = rows.shape[1]
    height = water.shape[0]
    groups = water.shape[1] // LANES
    tiles = out.shape[0] // CHUNK
    place = ((rows % groups) * height + rows // groups).astype(F32)
    dest = (blocks >> 7).astype(F32)
    local = (blocks & 31).astype(F32)
    pick = iota((8, links), 0)
    stacked = jnp.where(pick == 0, place, jnp.where(pick == 1, dest, local))
    turned = jnp.transpose(stacked)
    place_c, dest_c, local_c = turned[:, 0:1], turned[:, 1:2], turned[:, 2:3]
    earlier = (dest_c == dest) & (iota((links, links), 1) < iota((links, links), 0))
    ones = jnp.ones((links, LANES), BF16)
    rank = mm(earlier.astype(F32).astype(BF16), ones)
    position = dest_c * float(CHUNK) + rank
    position_c = position[:, 0:1]
    lane = iota((links, links), 1).astype(F32)
    slot_of = jnp.sum(jnp.where(place_c == lane, position_c, 0.0), axis=0, keepdims=True)
    slots[...] = jnp.broadcast_to(slot_of, slots.shape)
    dest_hot = (iota((tiles, links), 0).astype(F32) == dest).astype(F32).astype(BF16)
    rank_hot = jnp.where(rank == iota((links, LANES), 1).astype(F32), local_c + 1.0, 0.0)
    ids = mm(dest_hot, rank_hot.astype(BF16))
    level = water[...] + bed[...]
    by_block = jnp.concatenate(
        [level[:, c * LANES : (c + 1) * LANES] for c in range(groups)], axis=0
    )
    by_block = paired(by_block)
    step = 8 * CHUNK
    for start in range(0, out.shape[0], step):
        hot = (iota((step, links), 0) + start).astype(F32) == slot_of
        out[start : start + step, :] = fold(mm(hot.astype(F32).astype(BF16), by_block))
    out[pl.ds(SLOTS, tiles, CHUNK), :] = ids + table[0:1, :]


def lateral_kernel(rows_in, section, reach_source, last_row, out, source, ends):
    total = rows_in.shape[0]
    tiles = total // CHUNK
    blocks = section.shape[0]
    slot = iota((total, 1), 0).astype(F32)
    owner = jnp.floor((slot + 0.5) * (1.0 / CHUNK))
    within = slot - owner * CHUNK
    extras = rows_in[pl.ds(SLOTS, tiles, CHUNK), :]
    ids = jnp.where(iota((tiles, LANES), 1) < SLOTS, extras, 0.0).astype(BF16)
    spread = (iota((total, tiles), 1).astype(F32) == owner).astype(F32).astype(BF16)
    mine = mm(spread, ids)
    mine = jnp.where(iota((total, LANES), 1).astype(F32) == within, mine, 0.0)
    block = mm(mine.astype(BF16), jnp.ones((LANES, LANES), BF16)) - 1.0
    hot = (block == iota((total, LANES), 1).astype(F32)).astype(F32).astype(BF16)
    rows = rows_in[...]
    section_in = fold(mm(hot[:, :blocks], paired(section[...])))
    lateral = jnp.where(block >= 0.0, LATERAL_RATE * (rows - section_in), 0.0)
    out[...] = lateral
    sums = fold(mm(hot, paired(lateral), ((0,), (0,))))[:blocks]
    src = reach_source[...] + RIVER_SHARE * sums
    source[...] = src
    end = jnp.sum(src * last_row[...].astype(F32), axis=1, keepdims=True)
    ends[...] = jnp.broadcast_to(end, ends.shape)


def push_kernel(where, lateral, ends, table, own, one, two, three, out):
    band = where[1]
    bands = 4
    tiles = own.shape[0]
    blocks = ends.shape[0]
    lane = iota((tiles, LANES), 1)
    down = jnp.zeros((tiles, LANES), F32)
    gain = jnp.zeros((tiles, LANES), F32)
    for back, ref in enumerate((own, one, two, three)):
        source = (band + bands - back) % bands
        x = ref[...]
        here = (lane // blocks) == source
        y = x
        for turn in (1, 2, 3):
            y = jnp.where(lane // blocks == (turn + 1) % bands, pltpu.roll(x, turn * blocks, 1), y)
        down = jnp.where(here, y, down)
        y = x
        for turn in (1, 2, 3):
            y = jnp.where(lane // blocks == (turn + 2) % bands, pltpu.roll(x, turn * blocks, 1), y)
        gain = jnp.where(here, y, gain)
    high = jnp.floor(down * (1.0 / LANES))
    tables = jnp.concatenate([high + 1.0, down - high * LANES, gain], axis=1).astype(BF16)
    column = jnp.transpose(table[...])[blocks : 2 * blocks, 0:1]
    column_high = jnp.floor(column * (1.0 / LANES))
    high, low = column_high + 1.0, column - column_high * LANES
    factor = ends[...][:, 0:1]
    tile_lane = iota((blocks, tiles), 1).astype(F32) + 1.0
    block_lane = iota((blocks, LANES), 1).astype(F32)
    lefts, rights = [], []
    for hop in range(LEVELS - 1):
        left = (tile_lane == high).astype(F32)
        right = (block_lane == low).astype(F32)
        lefts.append(left * factor)
        rights.append(right.astype(BF16))
        if hop < LEVELS - 2:
            found = mm(left.astype(BF16), tables)
            high = jnp.sum(found[:, :LANES] * right, axis=1, keepdims=True)
            low = jnp.sum(found[:, LANES : 2 * LANES] * right, axis=1, keepdims=True)
            factor = factor * jnp.sum(found[:, 2 * LANES :] * right, axis=1, keepdims=True)
    left_hi, left_lo = halves(jnp.concatenate(lefts, axis=0))
    right = jnp.concatenate(rights, axis=0)
    pushed = mm(left_hi, right, ((0,), (0,))) + mm(left_lo, right, ((0,), (0,)))
    out[...] = lateral[...]
    out[pl.ds(SLOTS, tiles, CHUNK), :] = pushed


def flow_kernel(source, inverse, base, column):
    blocks = source.shape[0]
    hi, lo = halves(source[...])
    first = (iota((blocks, LANES), 1) == 0).astype(F32).astype(BF16)
    stacked = jnp.concatenate([hi, lo, first], axis=0)
    row = iota((blocks, LANES), 0)
    base_now = jnp.zeros((blocks, LANES), F32)
    column_now = jnp.zeros((blocks, LANES), F32)
    for g in range(blocks):
        x = mm(stacked, inverse[g], ((1,), (1,)))
        base_now = jnp.where(row == g, x[:blocks] + x[blocks : 2 * blocks], base_now)
        column_now = jnp.where(row == g, x[2 * blocks :], column_now)
    base[...] = base_now
    column[...] = column_now


def final_kernel(water, returned, slots, out):
    total = returned.shape[0]
    height = water.shape[0]
    groups = water.shape[1] // LANES
    slot_c = jnp.transpose(slots[...])[:, 0:1]
    rows = paired(returned[...])
    for c in range(groups):
        mine = slot_c[c * height : (c + 1) * height]
        hot = (iota((height, total), 1).astype(F32) == mine).astype(F32).astype(BF16)
        lateral = fold(mm(hot, rows))
        cols = slice(c * LANES, (c + 1) * LANES)
        out[:, cols] = water[:, cols] - PLAIN_SHARE * lateral


def strips_kernel(above, below, f0, f1, f2, f3, f4, left, right):
    fields = (f0, f1, f2, f3, f4)
    height, width = f0.shape
    tiles = height // 8 + 2
    lane = iota((8, LANES), 1)
    groups = left.shape[0] // 8
    lefts = [jnp.zeros((8, LANES), F32) for _ in range(groups)]
    rights = [jnp.zeros((8, LANES), F32) for _ in range(groups)]
    for a, field in enumerate(fields):
        for i in range(tiles):
            if i == 0:
                ref, rows = above, slice(a * HALO, a * HALO + 8)
            elif i == tiles - 1:
                ref, rows = below, slice(a * HALO, a * HALO + 8)
            else:
                ref, rows = field, slice(8 * i - 8, 8 * i)
            strip = a * tiles + i
            v, off = strip // 16, (strip % 16) * 8
            here = (lane >= off) & (lane < off + 8)
            x = ref[rows, 0:LANES]
            y = ref[rows, width - LANES : width]
            x = pltpu.roll(x, off, 1) if off else x
            y = pltpu.roll(y, (off + 8) % LANES, 1) if (off + 8) % LANES else y
            lefts[v] = jnp.where(here, x, lefts[v])
            rights[v] = jnp.where(here, y, rights[v])
    for v in range(groups):
        left[8 * v : 8 * v + 8, :] = lefts[v]
        right[8 * v : 8 * v + 8, :] = rights[v]


def flood_kernel(
    where, above, below, west, east, f0, f1, f2, f3, f4,
    water_out, east_out, south_out,
    level_s, bed_s, rough_s, qe_s, qs_s, mbe_s, mbs_s,
):
    height, width = f0.shape
    tiles = height // 8 + 2
    wide = width + LANES
    lane1 = iota((8, LANES), 1)
    scratch = (level_s, bed_s, rough_s, qe_s, qs_s)
    rate = GRAVITY * TIME_STEP
    tile_index, band_index, tile_last, band_last = where[0], where[1], where[2], where[3]
    for a, (field, dst) in enumerate(zip((f0, f1, f2, f3, f4), scratch)):
        for i in range(tiles):
            if i == 0:
                ref, rows = above, slice(a * HALO, a * HALO + 8)
            elif i == tiles - 1:
                ref, rows = below, slice(a * HALO, a * HALO + 8)
            else:
                ref, rows = field, slice(8 * i - 8, 8 * i)
            strip = a * tiles + i
            v, off = strip // 16, (strip % 16) * 8
            x = east[8 * v : 8 * v + 8, :]
            y = west[8 * v : 8 * v + 8, :]
            x = pltpu.roll(x, LANES - off, 1) if off else x
            y = pltpu.roll(y, (LANES - 8 - off) % LANES, 1) if (LANES - 8 - off) % LANES else y
            edge = jnp.where(lane1 < 8, x, jnp.where(lane1 >= LANES - 8, y, 0.0))
            body = ref[rows, :]
            if a == 2:
                body, edge = rate * body, rate * edge
            dst[8 * i : 8 * i + 8, :width] = body
            dst[8 * i : 8 * i + 8, width:] = edge
    lane = iota((8, wide), 1)
    sub = iota((8, wide), 0)
    shut_e = ((lane == width - 1) & (tile_index == tile_last)) | ((lane == wide - 1) & (tile_index == 0))
    ce = jnp.where(shut_e, 0.0, rate / CELL_WIDTH)
    shut_n = (sub == 7) & (band_index == 0)
    shut_s = (sub == 7) & (band_index == band_last)
    cs_first = jnp.where(shut_n, 0.0, rate / CELL_WIDTH)
    cs_last = jnp.where(shut_s, 0.0, rate / CELL_WIDTH)
    nxt = bed_s[0:8, :]
    nxt_up = pltpu.roll(nxt, 7, 0)
    for i in range(tiles):
        rows = slice(8 * i, 8 * i + 8)
        bed, up = nxt, nxt_up
        if i + 1 < tiles:
            nxt = bed_s[8 * i + 8 : 8 * i + 16, :]
            nxt_up = pltpu.roll(nxt, 7, 0)
        mbe_s[rows, :] = jnp.maximum(bed, pltpu.roll(bed, wide - 1, 1))
        mbs_s[rows, :] = jnp.maximum(bed, jnp.where(sub == 7, nxt_up, up))
        qe_s[rows, :] = jnp.where(shut_e, 0.0, qe_s[rows, :])
    last = slice(height, height + 8)
    qs_s[last, :] = jnp.where(shut_s, 0.0, qs_s[last, :])

    def face(here, ahead, bed_max, rough, old, factor):
        depth = jnp.maximum(jnp.maximum(here, ahead) - bed_max, DEPTH_FLOOR)
        drag = rough * jnp.abs(old) * jnp.exp(-FRICTION_POWER * jnp.log(depth)) + 1.0
        near = pl.reciprocal(drag, approx=True)
        near = near * (2.0 - drag * near)
        return (old - factor * depth * (ahead - here)) * near

    def substep(_, carry):
        nxt = level_s[0:8, :]
        nxt_up = pltpu.roll(nxt, 7, 0)
        north_turned = jnp.zeros((8, wide), F32)
        for i in range(tiles):
            rows = slice(8 * i, 8 * i + 8)
            level, up = nxt, nxt_up
            if i + 1 < tiles:
                nxt = level_s[8 * i + 8 : 8 * i + 16, :]
                nxt_up = pltpu.roll(nxt, 7, 0)
            rough = rough_s[rows, :]
            cs = cs_first if i == 0 else cs_last if i == tiles - 2 else rate / CELL_WIDTH
            qe = face(level, pltpu.roll(level, wide - 1, 1), mbe_s[rows, :], rough, qe_s[rows, :], ce)
            below_level = jnp.where(sub == 7, nxt_up, up)
            qs = face(level, below_level, mbs_s[rows, :], rough, qs_s[rows, :], cs)
            qe_s[rows, :] = qe
            qs_s[rows, :] = qs
            turned = pltpu.roll(qs, 1, 0)
            north = jnp.where(sub == 0, north_turned, turned)
            north_turned = turned
            gained = pltpu.roll(qe, 1, 1) - qe + north - qs
            level_s[rows, :] = level + (TIME_STEP / CELL_WIDTH) * gained
        return carry

    lax.fori_loop(0, SUBSTEPS, substep, 0)
    inner = slice(HALO, HALO + height)
    water_out[...] = level_s[inner, :width] - bed_s[inner, :width]
    east_out[...] = qe_s[inner, :width]
    south_out[...] = qs_s[inner, :width]


def shaped(*shape):
    return jax.ShapeDtypeStruct(shape, F32)


def call(kernel, out_shape, specs, scratch=(), flops=0, size=0, exps=0):
    return pl.pallas_call(
        kernel,
        out_shape=out_shape,
        in_specs=specs,
        out_specs=jax.tree.map(lambda _: VMEM, out_shape),
        scratch_shapes=list(scratch),
        compiler_params=pltpu.CompilerParams(vmem_limit_bytes=40 * 1024 * 1024),
        cost_estimate=pl.CostEstimate(flops=flops, bytes_accessed=size, transcendentals=exps),
        name=kernel.__name__,
    )


def per_device(
    water_depth, flux_east, flux_south, bed_level, roughness, link_rows, link_blocks,
    reach_inverse, reach_source, river_section, block_level, block_down,
):
    tiles = lax.axis_size("tile")
    bands = lax.axis_size("band")
    tile_index = lax.axis_index("tile")
    band_index = lax.axis_index("band")
    height, width = water_depth.shape
    blocks, reach = reach_source.shape
    total = tiles * CHUNK
    links = link_rows.shape[-1]
    where = jnp.stack(
        [tile_index, band_index, jnp.int32(tiles - 1), jnp.int32(bands - 1)]
    ).astype(jnp.int32)
    ring = [[(i, (i + k) % bands) for i in range(bands)] for k in range(bands)]

    last_row = reach_inverse[:, reach - 1, :]
    gain = last_row[:, 0].astype(F32)
    table = jnp.concatenate(
        [jnp.zeros((blocks,), F32), block_down.astype(F32), gain, jnp.zeros((blocks,), F32)]
    )
    table = jnp.broadcast_to(table[None, :], (8, LANES))

    payload, slots = call(
        pack_kernel, (shaped(total, LANES), shaped(8, links)), [VMEM] * 5, flops=10**9, size=10**6
    )(water_depth, bed_level, link_rows.reshape(1, links), link_blocks.reshape(1, links), table)
    rows_in = lax.all_to_all(
        payload.reshape(tiles, CHUNK, 1, LANES), "tile", split_axis=0, concat_axis=0, tiled=True
    )

    fields = (bed_level + water_depth, bed_level, roughness, flux_east, flux_south)
    top = jnp.concatenate([f[:HALO] for f in fields], axis=0)
    bottom = jnp.concatenate([f[height - HALO :] for f in fields], axis=0)
    above = lax.ppermute(bottom, "band", [(i, i + 1) for i in range(bands - 1)])
    below = lax.ppermute(top, "band", [(i + 1, i) for i in range(bands - 1)])
    left, right = call(
        strips_kernel, (shaped(48, LANES), shaped(48, LANES)), [VMEM] * 7, flops=10**6, size=10**6
    )(above, below, *fields)
    west = lax.ppermute(right, "tile", [(i, i + 1) for i in range(tiles - 1)])
    east = lax.ppermute(left, "tile", [(i + 1, i) for i in range(tiles - 1)])

    extras = rows_in.reshape(tiles, CHUNK, LANES)[:, SLOTS, :]
    others = [lax.ppermute(extras, "band", ring[k]) for k in (1, 2, 3)]
    lateral, source, ends = call(
        lateral_kernel,
        (shaped(total, LANES), shaped(blocks, LANES), shaped(blocks, LANES)),
        [VMEM] * 4,
        flops=10**9,
        size=10**6,
    )(rows_in.reshape(total, LANES), river_section, reach_source, last_row)
    answer = call(
        push_kernel, shaped(total, LANES), [SMEM] + [VMEM] * 7, flops=10**8, size=10**6
    )(where, lateral, ends, table, extras, *others)
    returned = lax.all_to_all(
        answer.reshape(tiles, CHUNK, 1, LANES), "tile", split_axis=0, concat_axis=0, tiled=True
    )

    wide = width + LANES
    tall = height + 2 * HALO
    water_now, final_east, final_south = call(
        flood_kernel,
        (shaped(height, width),) * 3,
        [SMEM] + [VMEM] * 9,
        scratch=[pltpu.VMEM((tall, wide), F32)] * 7,
        flops=10**8,
        size=10**7,
        exps=10**7,
    )(where, above, below, west, east, *fields)
    base_flow, column = call(
        flow_kernel, (shaped(blocks, reach),) * 2, [VMEM] * 2, flops=10**8, size=10**6
    )(source, reach_inverse)

    pushed = jnp.sum(returned.reshape(tiles, CHUNK, LANES)[:, SLOTS, :], axis=0, keepdims=True)
    parts = [pushed] + [lax.ppermute(pushed, "band", ring[k]) for k in (1, 2, 3)]
    final_depth = call(
        final_kernel, shaped(height, width), [VMEM] * 3, flops=10**9, size=10**6
    )(water_now, returned.reshape(total, LANES), slots)
    inflow = lax.dynamic_slice_in_dim(sum(parts)[0], band_index * blocks, blocks)
    discharge = base_flow + column * inflow[:, None]
    return (final_depth, final_east, final_south, discharge)


def solution(mesh):
    grid = P("band", "tile")
    owned = P(("tile", "band"))
    lists = P("tile", "band", None)
    return jax.shard_map(
        per_device,
        mesh=mesh,
        in_specs=(grid,) * 5 + (lists,) * 2 + (owned,) * 5,
        out_specs=(grid, grid, grid, owned),
        check_vma=False,
    )
```

time: 858 us -> 93.6 us (0.11)
  the two profiles are of different devices: /device:TPU:2 before, /device:TPU:103 now
where the time goes in v1:
time: 93.6 us; the launch traced here: 93 us
  starting transfers between devices  42.9 us (46%)
  waiting for transfers between devices  27 us (29%)
  Pallas kernels  16.1 us (17%)
  local copies, waits for them, and re-layouts  5.13 us (5%)
  other arithmetic  1.02 us (1%)
    all_to_all x1, waiting for transfers between devices, per_device(): lax.all_to_all(payload.reshape(tiles, CHUNK, 1, LANES), 'tile', split_axi...  15.2 us
    all_to_all x1, starting transfers between devices, per_device(): lax.all_to_all(payload.reshape(tiles, CHUNK, 1, LANES), 'tile', split_axi...  11.1 us
    all_to_all x1, starting transfers between devices, per_device(): lax.all_to_all(answer.reshape(tiles, CHUNK, 1, LANES), 'tile', split_axis...  10.3 us
    pallas_call x1, Pallas kernels, per_device(): call(flood_kernel, (shaped(height, width),) * 3, [SMEM] + [VMEM] * 9, scr...  7.51 us
    ppermute x1, waiting for transfers between devices, per_device(): east = lax.ppermute(left, 'tile', [(i + 1, i) for i in range(tiles - 1)])  6.51 us
    ppermute x3, starting transfers between devices, per_device(): lax.ppermute(pushed, 'band', ring[k])  5.7 us
    ppermute x1, starting transfers between devices, per_device(): west = lax.ppermute(right, 'tile', [(i, i + 1) for i in range(tiles - 1)])  5.7 us
    ppermute x3, starting transfers between devices, per_device(): others = [lax.ppermute(extras, 'band', ring[k]) for k in (1, 2, 3)]  5.06 us
  transfers between devices with their start and end apart: 12, of which 5 were waited for; matrix products, arithmetic and copies ran while one was open for 0% of the time, Pallas kernels for 12%

profile of v1, /device:TPU:103, one launch (start us, length us, event | category | flops | bytes accessed | tf_op | source)
XLA Modules:
  0.0 93.0 jit_solution(5127507381104176653)
XLA Ops:
  0.6 0.9 slice.52
  1.5 0.1 convert_reduce_fusion
  1.6 0.5 copy-done.12
  2.3 0.7 copy-done.11
  3.0 0.9 %copy-done = f32[128,512]{1,0:T(8,128)S(1)} copy-done((f32[128,512]{1,0:T(8,128)S(1)}, f32[128,512]{1,0:T(8,128)}, u32[]{:S(2)}) %copy-start) | copy-done | bytes 262168
  3.9 0.9 %copy-done.6 = f32[128,512]{1,0:T(8,128)S(1)} copy-done((f32[128,512]{1,0:T(8,128)S(1)}, f32[128,512]{1,0:T(8,128)}, u32[]{:S(2)}) %copy-start.6) | copy-done | bytes 262168
  4.9 2.2 %pack_kernel.1 = (f32[1088,128]{1,0:T(8,128)}, f32[8,512]{1,0:T(8,128)S(1)}) custom-call(f32[128,512]{1,0:T(8,128)S(1)} %copy-done.6, f32[128,512]{1,0:T(8,128)S(1)} %copy-done, s32[1,512]{1,0:T(1,128)S(1)} %bitcast.27, s32[1,512]{1,0:T(1,128)S(1)} %bitcast.28, f32[8,128]{1,0:T(8,128)S(1)} %broadcast_in_dim.4.table), custom_call_target="tpu_custom_call" | custom-call | flops 1000000000 | bytes 1000000 | tf_op jit(solution)/shard_map/pack_kernel/pallas_call | solution.py:356
  7.0 11.1 %all-to-all-start = ((f32[64,17,1,128]{3,2,1,0:T(1,128)}), f32[64,17,1,128]{3,2,1,0:T(1,128)S(1)}, u32[]{:S(2)}, u32[]{:S(2)}) async-start(f32[64,17,1,128]{3,2,1,0:T(1,128)} %bitcast.5), calls=%async_computation | async-start | bytes 1114112 | tf_op jit(solution)/shard_map/all_to_all | solution.py:359
  18.3 15.2 %all-to-all-done = f32[64,17,1,128]{3,2,1,0:T(1,128)S(1)} async-done(((f32[64,17,1,128]{3,2,1,0:T(1,128)}), f32[64,17,1,128]{3,2,1,0:T(1,128)S(1)}, u32[]{:S(2)}, u32[]{:S(2)}) %all-to-all-start) | async-done | bytes 557088 | tf_op jit(solution)/shard_map/all_to_all | solution.py:359
  33.7 1.4 %collective-permute-start.4 = (f32[64,128]{1,0:T(8,128)S(1)}, f32[64,128]{1,0:T(8,128)S(1)}, u32[]{:S(2)}, u32[]{:S(2)}) collective-permute-start(f32[64,128]{1,0:T(8,128)S(1)} %slice_bitcast_fusion.own), channel_id=1, source_target_pairs={{0,1},{1,2},{2,3},{3,0},{4,5},{5,6},{6,7},{7,4},{8,9},{9,10},{10,1... | collective-permute-start | bytes 98312 | tf_op jit(solution)/shard_map/ppermute | solution.py:375
  35.0 2.6 %collective-permute-start.5 = (f32[64,128]{1,0:T(8,128)S(1)}, f32[64,128]{1,0:T(8,128)S(1)}, u32[]{:S(2)}, u32[]{:S(2)}) collective-permute-start(f32[64,128]{1,0:T(8,128)S(1)} %slice_bitcast_fusion.own), channel_id=1, source_target_pairs={{0,2},{1,3},{2,0},{3,1},{4,6},{5,7},{6,4},{7,5},{8,10},{9,11},{10,... | collective-permute-start | bytes 98312 | tf_op jit(solution)/shard_map/ppermute | solution.py:375
  37.7 1.1 %collective-permute-start.6 = (f32[64,128]{1,0:T(8,128)S(1)}, f32[64,128]{1,0:T(8,128)S(1)}, u32[]{:S(2)}, u32[]{:S(2)}) collective-permute-start(f32[64,128]{1,0:T(8,128)S(1)} %slice_bitcast_fusion.own), channel_id=1, source_target_pairs={{0,3},{1,0},{2,1},{3,2},{4,7},{5,4},{6,5},{7,6},{8,11},{9,8},{10,9... | collective-permute-start | bytes 98312 | tf_op jit(solution)/shard_map/ppermute | solution.py:375
  38.7 0.9 lateral_kernel.1
  39.7 1.1 %collective-permute-done.6.three = f32[64,128]{1,0:T(8,128)S(1)} collective-permute-done((f32[64,128]{1,0:T(8,128)S(1)}, f32[64,128]{1,0:T(8,128)S(1)}, u32[]{:S(2)}, u32[]{:S(2)}) %collective-permute-start.6) | collective-permute-done | bytes 32800 | tf_op jit(solution)/shard_map/ppermute | solution.py:375
  40.7 3.0 %push_kernel.1 = f32[1088,128]{1,0:T(8,128)} custom-call(s32[4]{0:T(128)S(1)} %pad_add_fusion.where, f32[1088,128]{1,0:T(8,128)S(1)} %get-tuple-element.20.lateral, f32[32,128]{1,0:T(8,128)S(1)} %get-tuple-element.21.ends, f32[8,128]{1,0:T(8,128)S(1)} %broadcast_in_dim.4.table, f32[64,128]{1,0:T(8,128)S(1)} %slice_bitcast_fusion.own, ...), custom_call_target="tpu_custom_call" | custom-call | flops 100000000 | bytes 1000000 | tf_op jit(solution)/shard_map/push_kernel/pallas_call | solution.py:383
  43.8 10.3 %all-to-all-start.1 = ((f32[64,17,1,128]{3,2,1,0:T(1,128)}), f32[64,17,1,128]{3,2,1,0:T(1,128)S(1)}, u32[]{:S(2)}, u32[]{:S(2)}) async-start(f32[64,17,1,128]{3,2,1,0:T(1,128)} %bitcast.9), calls=%async_computation.1 | async-start | bytes 1114112 | tf_op jit(solution)/shard_map/all_to_all | solution.py:386
  54.1 0.9 copy-done.5
  55.0 1.8 %collective-permute-start = (f32[40,512]{1,0:T(8,128)S(1)}, f32[40,512]{1,0:T(8,128)S(1)}, u32[]{:S(2)}, u32[]{:S(2)}) collective-permute-start(f32[40,512]{1,0:T(8,128)S(1)} %get-tuple-element.29), channel_id=1, source_target_pairs={{0,1},{1,2},{2,3},{4,5},{5,6},{6,7},{8,9},{9,10},{10,11},{12,13},{... | collective-permute-start | bytes 245768 | tf_op jit(solution)/shard_map/ppermute | solution.py:366
  56.8 1.3 %collective-permute-start.1 = (f32[40,512]{1,0:T(8,128)S(1)}, f32[40,512]{1,0:T(8,128)S(1)}, u32[]{:S(2)}, u32[]{:S(2)}) collective-permute-start(f32[40,512]{1,0:T(8,128)S(1)} %get-tuple-element.28), channel_id=1, source_target_pairs={{1,0},{2,1},{3,2},{5,4},{6,5},{7,6},{9,8},{10,9},{11,10},{13,12},{... | collective-permute-start | bytes 245768 | tf_op jit(solution)/shard_map/ppermute | solution.py:367
  58.1 0.2 collective-permute-done.above
  58.3 4.0 %collective-permute-done.1.below = f32[40,512]{1,0:T(8,128)S(1)} collective-permute-done((f32[40,512]{1,0:T(8,128)S(1)}, f32[40,512]{1,0:T(8,128)S(1)}, u32[]{:S(2)}, u32[]{:S(2)}) %collective-permute-start.1) | collective-permute-done | bytes 81952 | tf_op jit(solution)/shard_map/ppermute | solution.py:367
  62.3 0.2 strips_kernel.1
  62.5 5.7 %collective-permute-start.2 = (f32[48,128]{1,0:T(8,128)S(1)}, f32[48,128]{1,0:T(8,128)S(1)}, u32[]{:S(2)}, u32[]{:S(2)}) collective-permute-start(f32[48,128]{1,0:T(8,128)S(1)} %get-tuple-element.16), channel_id=1, source_target_pairs={{0,4},{4,8},{8,12},{12,16},{16,20},{20,24},{24,28},{28,32},{32,36}... | collective-permute-start | bytes 73736 | tf_op jit(solution)/shard_map/ppermute | solution.py:371
  68.2 1.9 %collective-permute-start.3 = (f32[48,128]{1,0:T(8,128)S(1)}, f32[48,128]{1,0:T(8,128)S(1)}, u32[]{:S(2)}, u32[]{:S(2)}) collective-permute-start(f32[48,128]{1,0:T(8,128)S(1)} %get-tuple-element.17), channel_id=1, source_target_pairs={{4,0},{8,4},{12,8},{16,12},{20,16},{24,20},{28,24},{32,28},{36,32}... | collective-permute-start | bytes 73736 | tf_op jit(solution)/shard_map/ppermute | solution.py:372
  70.2 6.5 %collective-permute-done.3.east = f32[48,128]{1,0:T(8,128)S(1)} collective-permute-done((f32[48,128]{1,0:T(8,128)S(1)}, f32[48,128]{1,0:T(8,128)S(1)}, u32[]{:S(2)}, u32[]{:S(2)}) %collective-permute-start.3) | collective-permute-done | bytes 24608 | tf_op jit(solution)/shard_map/ppermute | solution.py:372
  76.7 7.5 %flood_kernel.1 = (f32[128,512]{1,0:T(8,128)S(1)}, f32[128,512]{1,0:T(8,128)}, f32[128,512]{1,0:T(8,128)}) custom-call(s32[4]{0:T(128)S(1)} %pad_add_fusion.where, f32[40,512]{1,0:T(8,128)S(1)} %collective-permute-done.above, f32[40,512]{1,0:T(8,128)S(1)} %collective-permute-done.1.below, f32[48,128]{1,0:T(8,128)S(1)} %collective-permute-done.2.west, ...), custom_call_target="tpu_custom_call" | custom-call | flops 100000000 | bytes 10000000 | tf_op jit(solution)/shard_map/flood_kernel/pallas_call | solution.py:392
  84.2 0.8 flow_kernel.1
  85.1 1.6 %collective-permute-start.7 = (f32[1,128]{1,0:T(1,128)S(1)}, f32[1,128]{1,0:T(1,128)S(1)}, u32[]{:S(2)}, u32[]{:S(2)}) collective-permute-start(f32[1,128]{1,0:T(1,128)S(1)} %bitcast.31), channel_id=1, source_target_pairs={{0,1},{1,2},{2,3},{3,0},{4,5},{5,6},{6,7},{7,4},{8,9},{9,10},{10,1... | collective-permute-start | bytes 1544 | tf_op jit(solution)/shard_map/ppermute | solution.py:406
  86.8 2.1 %collective-permute-start.8 = (f32[1,128]{1,0:T(1,128)S(1)}, f32[1,128]{1,0:T(1,128)S(1)}, u32[]{:S(2)}, u32[]{:S(2)}) collective-permute-start(f32[1,128]{1,0:T(1,128)S(1)} %bitcast.32), channel_id=1, source_target_pairs={{0,2},{1,3},{2,0},{3,1},{4,6},{5,7},{6,4},{7,5},{8,10},{9,11},{10,... | collective-permute-start | bytes 1544 | tf_op jit(solution)/shard_map/ppermute | solution.py:406
  88.9 2.0 %collective-permute-start.9 = (f32[1,128]{1,0:T(1,128)S(1)}, f32[1,128]{1,0:T(1,128)S(1)}, u32[]{:S(2)}, u32[]{:S(2)}) collective-permute-start(f32[1,128]{1,0:T(1,128)S(1)} %bitcast.33), channel_id=1, source_target_pairs={{0,3},{1,0},{2,1},{3,2},{4,7},{5,4},{6,5},{7,6},{8,11},{9,8},{10,9... | collective-permute-start | bytes 1544 | tf_op jit(solution)/shard_map/ppermute | solution.py:406
  90.8 1.4 %final_kernel.1 = f32[128,512]{1,0:T(8,128)} custom-call(f32[128,512]{1,0:T(8,128)S(1)} %get-tuple-element.18.water, f32[1088,128]{1,0:T(8,128)S(1)} %bitcast.23, f32[8,512]{1,0:T(8,128)S(1)} %get-tuple-element.22.slots), custom_call_target="tpu_custom_call" | custom-call | flops 1000000000 | bytes 1000000 | tf_op jit(solution)/shard_map/final_kernel/pallas_call | solution.py:407
  92.4 0.7 multiply_add_fusion
  (46 shorter events, 0.5 us)
Async XLA Ops:
  1.5 0.7 copy-start.12
  2.3 0.7 copy-start.11
  2.3 0.7 copy-start.10
  3.0 0.9 %copy-start = (f32[128,512]{1,0:T(8,128)S(1)}, f32[128,512]{1,0:T(8,128)}, u32[]{:S(2)}) copy-start(f32[128,512]{1,0:T(8,128)} %bed.1) | copy-start | bytes 786436
  3.9 0.9 %copy-start.6 = (f32[128,512]{1,0:T(8,128)S(1)}, f32[128,512]{1,0:T(8,128)}, u32[]{:S(2)}) copy-start(f32[128,512]{1,0:T(8,128)} %water.1) | copy-start | bytes 786436
  7.0 11.1 %copy-start.1 = (f32[128,512]{1,0:T(8,128)S(1)}, f32[128,512]{1,0:T(8,128)}, u32[]{:S(2)}) copy-start(f32[128,512]{1,0:T(8,128)} %bed.1) | copy-start | bytes 786436
  7.0 11.2 %copy-start.7 = (f32[128,512]{1,0:T(8,128)S(1)}, f32[128,512]{1,0:T(8,128)}, u32[]{:S(2)}) copy-start(f32[128,512]{1,0:T(8,128)} %water.1) | copy-start | bytes 786436
  7.0 26.5 %all-to-all-start = ((f32[64,17,1,128]{3,2,1,0:T(1,128)}), f32[64,17,1,128]{3,2,1,0:T(1,128)S(1)}, u32[]{:S(2)}, u32[]{:S(2)}) async-start(f32[64,17,1,128]{3,2,1,0:T(1,128)} %bitcast.5), calls=%async_computation | async-start | bytes 1114112 | tf_op jit(solution)/shard_map/all_to_all | solution.py:359
  33.6 5.1 %copy-start.8 = (f32[32,128]{1,0:T(8,128)S(1)}, f32[32,128]{1,0:T(8,128)}, u32[]{:S(2)}) copy-start(f32[32,128]{1,0:T(8,128)} %section.1) | copy-start | bytes 49156
  33.6 5.1 %copy-start.9 = (f32[32,128]{1,0:T(8,128)S(1)}, f32[32,128]{1,0:T(8,128)}, u32[]{:S(2)}) copy-start(f32[32,128]{1,0:T(8,128)} %reach_source.1) | copy-start | bytes 49156
  33.7 6.0 %collective-permute-start.4 = (f32[64,128]{1,0:T(8,128)S(1)}, f32[64,128]{1,0:T(8,128)S(1)}, u32[]{:S(2)}, u32[]{:S(2)}) collective-permute-start(f32[64,128]{1,0:T(8,128)S(1)} %slice_bitcast_fusion.own), channel_id=1, source_target_pairs={{0,1},{1,2},{2,3},{3,0},{4,5},{5,6},{6,7},{7,4},{8,9},{9,10},{10,1... | collective-permute-start | bytes 98312 | tf_op jit(solution)/shard_map/ppermute | solution.py:375
  35.0 4.6 %collective-permute-start.5 = (f32[64,128]{1,0:T(8,128)S(1)}, f32[64,128]{1,0:T(8,128)S(1)}, u32[]{:S(2)}, u32[]{:S(2)}) collective-permute-start(f32[64,128]{1,0:T(8,128)S(1)} %slice_bitcast_fusion.own), channel_id=1, source_target_pairs={{0,2},{1,3},{2,0},{3,1},{4,6},{5,7},{6,4},{7,5},{8,10},{9,11},{10,... | collective-permute-start | bytes 98312 | tf_op jit(solution)/shard_map/ppermute | solution.py:375
  37.7 3.1 %collective-permute-start.6 = (f32[64,128]{1,0:T(8,128)S(1)}, f32[64,128]{1,0:T(8,128)S(1)}, u32[]{:S(2)}, u32[]{:S(2)}) collective-permute-start(f32[64,128]{1,0:T(8,128)S(1)} %slice_bitcast_fusion.own), channel_id=1, source_target_pairs={{0,3},{1,0},{2,1},{3,2},{4,7},{5,4},{6,5},{7,6},{8,11},{9,8},{10,9... | collective-permute-start | bytes 98312 | tf_op jit(solution)/shard_map/ppermute | solution.py:375
  43.7 10.3 %copy-start.3 = (f32[128,512]{1,0:T(8,128)S(1)}, f32[128,512]{1,0:T(8,128)}, u32[]{:S(2)}) copy-start(f32[128,512]{1,0:T(8,128)} %f2.3) | copy-start | bytes 786436
  43.8 10.4 %copy-start.4 = (f32[128,512]{1,0:T(8,128)S(1)}, f32[128,512]{1,0:T(8,128)}, u32[]{:S(2)}) copy-start(f32[128,512]{1,0:T(8,128)} %f3.3) | copy-start | bytes 786436
  43.8 41.3 %all-to-all-start.1 = ((f32[64,17,1,128]{3,2,1,0:T(1,128)}), f32[64,17,1,128]{3,2,1,0:T(1,128)S(1)}, u32[]{:S(2)}, u32[]{:S(2)}) async-start(f32[64,17,1,128]{3,2,1,0:T(1,128)} %bitcast.9), calls=%async_computation.1 | async-start | bytes 1114112 | tf_op jit(solution)/shard_map/all_to_all | solution.py:386
  54.0 1.0 %copy-start.5 = (f32[128,512]{1,0:T(8,128)S(1)}, f32[128,512]{1,0:T(8,128)}, u32[]{:S(2)}) copy-start(f32[128,512]{1,0:T(8,128)} %f4.3) | copy-start | bytes 786436
  55.0 3.3 %collective-permute-start = (f32[40,512]{1,0:T(8,128)S(1)}, f32[40,512]{1,0:T(8,128)S(1)}, u32[]{:S(2)}, u32[]{:S(2)}) collective-permute-start(f32[40,512]{1,0:T(8,128)S(1)} %get-tuple-element.29), channel_id=1, source_target_pairs={{0,1},{1,2},{2,3},{4,5},{5,6},{6,7},{8,9},{9,10},{10,11},{12,13},{... | collective-permute-start | bytes 245768 | tf_op jit(solution)/shard_map/ppermute | solution.py:366
  56.8 5.5 %collective-permute-start.1 = (f32[40,512]{1,0:T(8,128)S(1)}, f32[40,512]{1,0:T(8,128)S(1)}, u32[]{:S(2)}, u32[]{:S(2)}) collective-permute-start(f32[40,512]{1,0:T(8,128)S(1)} %get-tuple-element.28), channel_id=1, source_target_pairs={{1,0},{2,1},{3,2},{5,4},{6,5},{7,6},{9,8},{10,9},{11,10},{13,12},{... | collective-permute-start | bytes 245768 | tf_op jit(solution)/shard_map/ppermute | solution.py:367
  62.5 7.7 %collective-permute-start.2 = (f32[48,128]{1,0:T(8,128)S(1)}, f32[48,128]{1,0:T(8,128)S(1)}, u32[]{:S(2)}, u32[]{:S(2)}) collective-permute-start(f32[48,128]{1,0:T(8,128)S(1)} %get-tuple-element.16), channel_id=1, source_target_pairs={{0,4},{4,8},{8,12},{12,16},{16,20},{20,24},{24,28},{28,32},{32,36}... | collective-permute-start | bytes 73736 | tf_op jit(solution)/shard_map/ppermute | solution.py:371
  68.2 8.5 %collective-permute-start.3 = (f32[48,128]{1,0:T(8,128)S(1)}, f32[48,128]{1,0:T(8,128)S(1)}, u32[]{:S(2)}, u32[]{:S(2)}) collective-permute-start(f32[48,128]{1,0:T(8,128)S(1)} %get-tuple-element.17), channel_id=1, source_target_pairs={{4,0},{8,4},{12,8},{16,12},{20,16},{24,20},{28,24},{32,28},{36,32}... | collective-permute-start | bytes 73736 | tf_op jit(solution)/shard_map/ppermute | solution.py:372
  70.2 14.0 %copy-start.2 = (bf16[32,128,128]{2,1,0:T(8,128)(2,1)S(1)}, bf16[32,128,128]{2,1,0:T(8,128)(2,1)}, u32[]{:S(2)}) copy-start(bf16[32,128,128]{2,1,0:T(8,128)(2,1)} %inverse.1) | copy-start | bytes 3145732
  85.1 7.1 %collective-permute-start.7 = (f32[1,128]{1,0:T(1,128)S(1)}, f32[1,128]{1,0:T(1,128)S(1)}, u32[]{:S(2)}, u32[]{:S(2)}) collective-permute-start(f32[1,128]{1,0:T(1,128)S(1)} %bitcast.31), channel_id=1, source_target_pairs={{0,1},{1,2},{2,3},{3,0},{4,5},{5,6},{6,7},{7,4},{8,9},{9,10},{10,1... | collective-permute-start | bytes 1544 | tf_op jit(solution)/shard_map/ppermute | solution.py:406
  86.8 5.5 %collective-permute-start.8 = (f32[1,128]{1,0:T(1,128)S(1)}, f32[1,128]{1,0:T(1,128)S(1)}, u32[]{:S(2)}, u32[]{:S(2)}) collective-permute-start(f32[1,128]{1,0:T(1,128)S(1)} %bitcast.32), channel_id=1, source_target_pairs={{0,2},{1,3},{2,0},{3,1},{4,6},{5,7},{6,4},{7,5},{8,10},{9,11},{10,... | collective-permute-start | bytes 1544 | tf_op jit(solution)/shard_map/ppermute | solution.py:406
  88.9 3.4 %collective-permute-start.9 = (f32[1,128]{1,0:T(1,128)S(1)}, f32[1,128]{1,0:T(1,128)S(1)}, u32[]{:S(2)}, u32[]{:S(2)}) collective-permute-start(f32[1,128]{1,0:T(1,128)S(1)} %bitcast.33), channel_id=1, source_target_pairs={{0,3},{1,0},{2,1},{3,2},{4,7},{5,4},{6,5},{7,6},{8,11},{9,8},{10,9... | collective-permute-start | bytes 1544 | tf_op jit(solution)/shard_map/ppermute | solution.py:406

commit v2 on v1

--- a/solution.py
+++ b/solution.py
@@ -13,6 +13,8 @@
 LANES = 128
 SLOTS = 16
 CHUNK = SLOTS + 1
+GAIN_LANE = 64
+ID_LANE = 96
 
 GRAVITY = 9.81
 TIME_STEP = 3.0
@@ -27,6 +29,8 @@
 BF16 = jnp.bfloat16
 VMEM = pl.BlockSpec(memory_space=pltpu.VMEM)
 SMEM = pl.BlockSpec(memory_space=pltpu.SMEM)
+HBM = pl.BlockSpec(memory_space=pltpu.HBM)
+ANY = pl.BlockSpec(memory_space=pl.ANY)
 
 
 def iota(shape, dim):
@@ -52,13 +56,31 @@
     return lax.dot_general(a, b, (dims, ((), ())), preferred_element_type=F32)
 
 
-def pack_kernel(water, bed, link_rows, link_blocks, table, out, slots):
+def pack_kernel(
+    water_h, bed_h, rows_h, blocks_h, inverse_h, down,
+    out, slots, tables, last_out,
+    water, bed, link_rows, link_blocks, tails, row_s, sems,
+):
+    blocks_own, reach = last_out.shape
+    moves = (
+        (rows_h, link_rows),
+        (blocks_h, link_blocks),
+        (water_h, water),
+        (bed_h, bed),
+        (inverse_h.at[:, reach - 16 : reach, :], tails),
+    )
+    copies = [pltpu.make_async_copy(src, dst, sems.at[i]) for i, (src, dst) in enumerate(moves)]
+    for copy in copies:
+        copy.start()
+    copies[0].wait()
+    copies[1].wait()
     rows = link_rows[...]
     blocks = link_blocks[...]
     links = rows.shape[1]
     height = water.shape[0]
     groups = water.shape[1] // LANES
-    tiles = out.shape[0] // CHUNK
+    tiles = out.shape[0] // SLOTS
+    bands = tables.shape[0] // tiles
     place = ((rows % groups) * height + rows // groups).astype(F32)
     dest = (blocks >> 7).astype(F32)
     local = (blocks & 31).astype(F32)
@@ -69,77 +91,85 @@
     earlier = (dest_c == dest) & (iota((links, links), 1) < iota((links, links), 0))
     ones = jnp.ones((links, LANES), BF16)
     rank = mm(earlier.astype(F32).astype(BF16), ones)
-    position = dest_c * float(CHUNK) + rank
+    position = dest_c * float(SLOTS) + rank
     position_c = position[:, 0:1]
     lane = iota((links, links), 1).astype(F32)
     slot_of = jnp.sum(jnp.where(place_c == lane, position_c, 0.0), axis=0, keepdims=True)
     slots[...] = jnp.broadcast_to(slot_of, slots.shape)
-    dest_hot = (iota((tiles, links), 0).astype(F32) == dest).astype(F32).astype(BF16)
-    rank_hot = jnp.where(rank == iota((links, LANES), 1).astype(F32), local_c + 1.0, 0.0)
-    ids = mm(dest_hot, rank_hot.astype(BF16))
+    copies[2].wait()
+    copies[3].wait()
     level = water[...] + bed[...]
     by_block = jnp.concatenate(
         [level[:, c * LANES : (c + 1) * LANES] for c in range(groups)], axis=0
     )
     by_block = paired(by_block)
-    step = 8 * CHUNK
+    step = 128
     for start in range(0, out.shape[0], step):
         hot = (iota((step, links), 0) + start).astype(F32) == slot_of
         out[start : start + step, :] = fold(mm(hot.astype(F32).astype(BF16), by_block))
-    out[pl.ds(SLOTS, tiles, CHUNK), :] = ids + table[0:1, :]
-
-
-def lateral_kernel(rows_in, section, reach_source, last_row, out, source, ends):
+    dest_hot = (iota((tiles, links), 0).astype(F32) == dest).astype(F32).astype(BF16)
+    seat = iota((links, LANES), 1).astype(F32) - float(ID_LANE)
+    rank_hot = jnp.where(rank == seat, local_c + 1.0, 0.0)
+    ids = mm(dest_hot, rank_hot.astype(BF16))
+    copies[4].wait()
+    last = tails[:, 15, :].astype(F32)
+    last_out[...] = last
+    first = (iota((8, reach), 1) == 0).astype(F32).astype(BF16)
+    seated = jnp.concatenate(
+        [jnp.zeros((GAIN_LANE, reach), F32), last, jnp.zeros((LANES - GAIN_LANE - blocks_own, reach), F32)],
+        axis=0,
+    )
+    gain = mm(first, seated.astype(BF16), ((1,), (1,)))
+    row_s[...] = jnp.zeros(row_s.shape, F32)
+    row_s[0:1, 0:blocks_own] = down[...].astype(F32)
+    entry = ids + (row_s[0:1, :] + gain[0:1, :])
+    for b in range(bands):
+        tables[pl.ds(b, tiles, bands), :] = entry
+
+
+def river_kernel(
+    where, rows_in, tables_in, section, reach_source, last_row, down, order, out, source
+):
     total = rows_in.shape[0]
-    tiles = total // CHUNK
+    tiles = total // SLOTS
     blocks = section.shape[0]
-    slot = iota((total, 1), 0).astype(F32)
-    owner = jnp.floor((slot + 0.5) * (1.0 / CHUNK))
-    within = slot - owner * CHUNK
-    extras = rows_in[pl.ds(SLOTS, tiles, CHUNK), :]
-    ids = jnp.where(iota((tiles, LANES), 1) < SLOTS, extras, 0.0).astype(BF16)
-    spread = (iota((total, tiles), 1).astype(F32) == owner).astype(F32).astype(BF16)
-    mine = mm(spread, ids)
-    mine = jnp.where(iota((total, LANES), 1).astype(F32) == within, mine, 0.0)
-    block = mm(mine.astype(BF16), jnp.ones((LANES, LANES), BF16)) - 1.0
+    bands = tables_in.shape[0] // tiles
+    band = where[1]
+    group = iota((tiles, LANES), 1) // blocks
+    turns = LANES // blocks
+    downs = jnp.zeros((tiles, LANES), F32)
+    gains = jnp.zeros((tiles, LANES), F32)
+    mine = jnp.zeros((tiles, LANES), F32)
+    for b in range(bands):
+        x = tables_in[pl.ds(b, tiles, bands), :]
+        mine = jnp.where(band == b, x, mine)
+        y = pltpu.roll(x, b * blocks, 1) if b else x
+        downs = jnp.where(group == b, y, downs)
+        turn = (b * blocks - GAIN_LANE) % LANES
+        y = pltpu.roll(x, turn, 1) if turn else x
+        gains = jnp.where(group == b, y, gains)
+    high = jnp.floor(downs * (1.0 / LANES))
+    tables = jnp.concatenate([high + 1.0, downs - high * LANES, gains], axis=1).astype(BF16)
+
+    slot = iota((total, 1), 0)
+    owner = slot // SLOTS
+    within = slot % SLOTS + ID_LANE
+    spread = (iota((total, tiles), 1) == owner).astype(F32).astype(BF16)
+    seat = mm(spread, mine.astype(BF16))
+    seat = jnp.where(iota((total, LANES), 1) == within, seat, 0.0)
+    block = mm(seat.astype(BF16), jnp.ones((LANES, LANES), BF16)) - 1.0
     hot = (block == iota((total, LANES), 1).astype(F32)).astype(F32).astype(BF16)
-    rows = rows_in[...]
     section_in = fold(mm(hot[:, :blocks], paired(section[...])))
-    lateral = jnp.where(block >= 0.0, LATERAL_RATE * (rows - section_in), 0.0)
-    out[...] = lateral
+    lateral = jnp.where(block >= 0.0, LATERAL_RATE * (rows_in[...] - section_in), 0.0)
     sums = fold(mm(hot, paired(lateral), ((0,), (0,))))[:blocks]
     src = reach_source[...] + RIVER_SHARE * sums
     source[...] = src
-    end = jnp.sum(src * last_row[...].astype(F32), axis=1, keepdims=True)
-    ends[...] = jnp.broadcast_to(end, ends.shape)
-
-
-def push_kernel(where, lateral, ends, table, own, one, two, three, out):
-    band = where[1]
-    bands = 4
-    tiles = own.shape[0]
-    blocks = ends.shape[0]
-    lane = iota((tiles, LANES), 1)
-    down = jnp.zeros((tiles, LANES), F32)
-    gain = jnp.zeros((tiles, LANES), F32)
-    for back, ref in enumerate((own, one, two, three)):
-        source = (band + bands - back) % bands
-        x = ref[...]
-        here = (lane // blocks) == source
-        y = x
-        for turn in (1, 2, 3):
-            y = jnp.where(lane // blocks == (turn + 1) % bands, pltpu.roll(x, turn * blocks, 1), y)
-        down = jnp.where(here, y, down)
-        y = x
-        for turn in (1, 2, 3):
-            y = jnp.where(lane // blocks == (turn + 2) % bands, pltpu.roll(x, turn * blocks, 1), y)
-        gain = jnp.where(here, y, gain)
-    high = jnp.floor(down * (1.0 / LANES))
-    tables = jnp.concatenate([high + 1.0, down - high * LANES, gain], axis=1).astype(BF16)
-    column = jnp.transpose(table[...])[blocks : 2 * blocks, 0:1]
+    ends = jnp.sum(src * last_row[...], axis=1, keepdims=True)
+
+    column = jnp.transpose(down[...])[:, 0:1]
     column_high = jnp.floor(column * (1.0 / LANES))
     high, low = column_high + 1.0, column - column_high * LANES
-    factor = ends[...][:, 0:1]
+    factor = jnp.ones((blocks, 1), F32)
     tile_lane = iota((blocks, tiles), 1).astype(F32) + 1.0
     block_lane = iota((blocks, LANES), 1).astype(F32)
     lefts, rights = [], []
@@ -153,10 +183,12 @@
             high = jnp.sum(found[:, :LANES] * right, axis=1, keepdims=True)
             low = jnp.sum(found[:, LANES : 2 * LANES] * right, axis=1, keepdims=True)
             factor = factor * jnp.sum(found[:, 2 * LANES :] * right, axis=1, keepdims=True)
-    left_hi, left_lo = halves(jnp.concatenate(lefts, axis=0))
+    left = jnp.concatenate([x * ends for x in lefts], axis=0)
+    left_hi, left_lo = halves(left)
     right = jnp.concatenate(rights, axis=0)
     pushed = mm(left_hi, right, ((0,), (0,))) + mm(left_lo, right, ((0,), (0,)))
-    out[...] = lateral[...]
+    for t in range(tiles):
+        out[t * CHUNK : t * CHUNK + SLOTS, :] = lateral[t * SLOTS : (t + 1) * SLOTS]
     out[pl.ds(SLOTS, tiles, CHUNK), :] = pushed
 
 
@@ -180,7 +212,8 @@
     total = returned.shape[0]
     height = water.shape[0]
     groups = water.shape[1] // LANES
-    slot_c = jnp.transpose(slots[...])[:, 0:1]
+    slot = slots[...]
+    slot_c = jnp.transpose(slot + jnp.floor(slot * (1.0 / SLOTS)))[:, 0:1]
     rows = paired(returned[...])
     for c in range(groups):
         mine = slot_c[c * height : (c + 1) * height]
@@ -346,18 +379,28 @@
     ).astype(jnp.int32)
     ring = [[(i, (i + k) % bands) for i in range(bands)] for k in range(bands)]
 
-    last_row = reach_inverse[:, reach - 1, :]
-    gain = last_row[:, 0].astype(F32)
-    table = jnp.concatenate(
-        [jnp.zeros((blocks,), F32), block_down.astype(F32), gain, jnp.zeros((blocks,), F32)]
-    )
-    table = jnp.broadcast_to(table[None, :], (8, LANES))
-
-    payload, slots = call(
-        pack_kernel, (shaped(total, LANES), shaped(8, links)), [VMEM] * 5, flops=10**9, size=10**6
-    )(water_depth, bed_level, link_rows.reshape(1, links), link_blocks.reshape(1, links), table)
+    down = block_down.reshape(1, blocks)
+    payload, slots, tables, last_row = call(
+        pack_kernel,
+        (shaped(tiles * SLOTS, LANES), shaped(8, links), shaped(tiles * bands, LANES), shaped(blocks, reach)),
+        [HBM] * 5 + [VMEM],
+        scratch=[
+            pltpu.VMEM((height, width), F32),
+            pltpu.VMEM((height, width), F32),
+            pltpu.VMEM((1, links), jnp.int32),
+            pltpu.VMEM((1, links), jnp.int32),
+            pltpu.VMEM((blocks, 16, reach), BF16),
+            pltpu.VMEM((8, LANES), F32),
+            pltpu.SemaphoreType.DMA((5,)),
+        ],
+        flops=10**9,
+        size=10**6,
+    )(water_depth, bed_level, link_rows.reshape(1, links), link_blocks.reshape(1, links), reach_inverse, down)
     rows_in = lax.all_to_all(
-        payload.reshape(tiles, CHUNK, 1, LANES), "tile", split_axis=0, concat_axis=0, tiled=True
+        payload.reshape(tiles, SLOTS, LANES), "tile", split_axis=0, concat_axis=0, tiled=True
+    )
+    tables_in = lax.all_to_all(
+        tables.reshape(tiles * bands, 1, LANES), ("tile", "band"), split_axis=0, concat_axis=0, tiled=True
     )
 
     fields = (bed_level + water_depth, bed_level, roughness, flux_east, flux_south)
@@ -371,18 +414,23 @@
     west = lax.ppermute(right, "tile", [(i, i + 1) for i in range(tiles - 1)])
     east = lax.ppermute(left, "tile", [(i + 1, i) for i in range(tiles - 1)])
 
-    extras = rows_in.reshape(tiles, CHUNK, LANES)[:, SLOTS, :]
-    others = [lax.ppermute(extras, "band", ring[k]) for k in (1, 2, 3)]
-    lateral, source, ends = call(
-        lateral_kernel,
-        (shaped(total, LANES), shaped(blocks, LANES), shaped(blocks, LANES)),
-        [VMEM] * 4,
+    column_down = jnp.broadcast_to(block_down.astype(F32)[None, :], (8, blocks))
+    answer, source = call(
+        river_kernel,
+        (shaped(total, LANES), shaped(blocks, LANES)),
+        [SMEM] + [VMEM] * 6 + [ANY],
         flops=10**9,
         size=10**6,
-    )(rows_in.reshape(total, LANES), river_section, reach_source, last_row)
-    answer = call(
-        push_kernel, shaped(total, LANES), [SMEM] + [VMEM] * 7, flops=10**8, size=10**6
-    )(where, lateral, ends, table, extras, *others)
+    )(
+        where,
+        rows_in.reshape(tiles * SLOTS, LANES),
+        tables_in.reshape(tiles * bands, LANES),
+        river_section,
+        reach_source,
+        last_row,
+        column_down,
+        left,
+    )
     returned = lax.all_to_all(
         answer.reshape(tiles, CHUNK, 1, LANES), "tile", split_axis=0, concat_axis=0, tiled=True
     )

time: 93.6 us -> 96.3 us (1.029)
  the two profiles are of different devices: /device:TPU:103 before, /device:TPU:160 now
where the time goes in v2:
time: 96.3 us; the launch traced here: 95.8 us
  starting transfers between devices  45.4 us (47%)
  waiting for transfers between devices  28.2 us (29%)
  Pallas kernels  15.6 us (16%)
  local copies, waits for them, and re-layouts  4.87 us (5%)
    all_to_all x1, starting transfers between devices, per_device(): lax.all_to_all(tables.reshape(tiles * bands, 1, LANES), ('tile', 'band'),...  13.7 us
    ppermute x1, waiting for transfers between devices, per_device(): west = lax.ppermute(right, 'tile', [(i, i + 1) for i in range(tiles - 1)])  8.88 us
    all_to_all x1, starting transfers between devices, per_device(): lax.all_to_all(payload.reshape(tiles, SLOTS, LANES), 'tile', split_axis=0...  8.65 us
    all_to_all x1, starting transfers between devices, per_device(): lax.all_to_all(answer.reshape(tiles, CHUNK, 1, LANES), 'tile', split_axis...  7.95 us
    all_to_all x1, waiting for transfers between devices, per_device(): lax.all_to_all(tables.reshape(tiles * bands, 1, LANES), ('tile', 'band'),...  7.92 us
    pallas_call x1, Pallas kernels, per_device(): call(flood_kernel, (shaped(height, width),) * 3, [SMEM] + [VMEM] * 9, scr...  7.51 us
    all_to_all x1, waiting for transfers between devices, per_device(): lax.all_to_all(payload.reshape(tiles, SLOTS, LANES), 'tile', split_axis=0...  5.67 us
    ppermute x1, starting transfers between devices, per_device(): east = lax.ppermute(left, 'tile', [(i + 1, i) for i in range(tiles - 1)])  5.61 us
  transfers between devices with their start and end apart: 10, of which 7 were waited for; matrix products, arithmetic and copies ran while one was open for 0% of the time, Pallas kernels for 10%

profile of v2, /device:TPU:160, one launch (start us, length us, event | category | flops | bytes accessed | tf_op | source)
XLA Modules:
  0.0 95.8 jit_solution(7251458242480773379)
XLA Ops:
  0.7 0.7 copy-done.12
  1.3 0.9 copy-done
  2.3 1.2 %copy-done.2 = bf16[32,128,128]{2,1,0:T(8,128)(2,1)S(1)} copy-done((bf16[32,128,128]{2,1,0:T(8,128)(2,1)S(1)}, bf16[32,128,128]{2,1,0:T(8,128)(2,1)}, u32[]{:S(2)}) %copy-start.2) | copy-done | bytes 1048600
  3.5 0.9 copy-done.7
  4.5 2.2 %pack_kernel.1 = (f32[1024,128]{1,0:T(8,128)}, f32[8,512]{1,0:T(8,128)S(1)}, f32[256,128]{1,0:T(8,128)}, f32[32,128]{1,0:T(8,128)S(1)}) custom-call(f32[128,512]{1,0:T(8,128)S(1)} %copy-done.7, f32[128,512]{1,0:T(8,128)S(1)} %copy-done, s32[1,512]{1,0:T(1,128)S(1)} %bitcast.23, s32[1,512]{1,0:T(1,128)S(1)} %bitcast.24, bf16[32,128,128]{2,1,0:T(8,128)(2,1)S(1)} %copy-done.2, ...), custom_call_target="tpu_custom_call" | custom-call | flops 1000000000 | bytes 1000000 | tf_op jit(solution)/shard_map/pack_kernel/pallas_call | solution.py:383
  6.7 13.7 %all-to-all-start.1 = ((f32[256,1,128]{2,1,0:T(1,128)}), f32[256,1,128]{2,1,0:T(1,128)S(1)}, u32[]{:S(2)}, u32[]{:S(2)}) async-start(f32[256,1,128]{2,1,0:T(1,128)} %bitcast.8), calls=%async_computation.1 | async-start | bytes 262144 | tf_op jit(solution)/shard_map/all_to_all | solution.py:402
  20.4 7.9 %all-to-all-done.1 = f32[256,1,128]{2,1,0:T(1,128)S(1)} async-done(((f32[256,1,128]{2,1,0:T(1,128)}), f32[256,1,128]{2,1,0:T(1,128)S(1)}, u32[]{:S(2)}, u32[]{:S(2)}) %all-to-all-start.1) | async-done | bytes 131104 | tf_op jit(solution)/shard_map/all_to_all | solution.py:402
  28.3 8.7 %all-to-all-start = ((f32[64,16,128]{2,1,0:T(8,128)}), f32[64,16,128]{2,1,0:T(8,128)S(1)}, u32[]{:S(2)}, u32[]{:S(2)}) async-start(f32[64,16,128]{2,1,0:T(8,128)} %bitcast.5), calls=%async_computation | async-start | bytes 1048576 | tf_op jit(solution)/shard_map/all_to_all | solution.py:399
  37.0 0.9 copy-done.6
  37.9 2.3 %collective-permute-start = (f32[40,512]{1,0:T(8,128)S(1)}, f32[40,512]{1,0:T(8,128)S(1)}, u32[]{:S(2)}, u32[]{:S(2)}) collective-permute-start(f32[40,512]{1,0:T(8,128)S(1)} %get-tuple-element.31), channel_id=1, source_target_pairs={{0,1},{1,2},{2,3},{4,5},{5,6},{6,7},{8,9},{9,10},{10,11},{12,13},{... | collective-permute-start | bytes 245768 | tf_op jit(solution)/shard_map/ppermute | solution.py:409
  40.2 1.3 %collective-permute-start.1 = (f32[40,512]{1,0:T(8,128)S(1)}, f32[40,512]{1,0:T(8,128)S(1)}, u32[]{:S(2)}, u32[]{:S(2)}) collective-permute-start(f32[40,512]{1,0:T(8,128)S(1)} %get-tuple-element.30), channel_id=1, source_target_pairs={{1,0},{2,1},{3,2},{5,4},{6,5},{7,6},{9,8},{10,9},{11,10},{13,12},{... | collective-permute-start | bytes 245768 | tf_op jit(solution)/shard_map/ppermute | solution.py:410
  41.5 0.1 pad_add_fusion.where
  41.6 0.6 collective-permute-done.above
  42.2 4.3 %collective-permute-done.1.below = f32[40,512]{1,0:T(8,128)S(1)} collective-permute-done((f32[40,512]{1,0:T(8,128)S(1)}, f32[40,512]{1,0:T(8,128)S(1)}, u32[]{:S(2)}, u32[]{:S(2)}) %collective-permute-start.1) | collective-permute-done | bytes 81952 | tf_op jit(solution)/shard_map/ppermute | solution.py:410
  46.5 0.2 strips_kernel.1
  46.8 5.7 %all-to-all-done = f32[64,16,128]{2,1,0:T(8,128)S(1)} async-done(((f32[64,16,128]{2,1,0:T(8,128)}), f32[64,16,128]{2,1,0:T(8,128)S(1)}, u32[]{:S(2)}, u32[]{:S(2)}) %all-to-all-start) | async-done | bytes 524320 | tf_op jit(solution)/shard_map/all_to_all | solution.py:399
  52.5 3.4 %river_kernel.1 = (f32[1088,128]{1,0:T(8,128)}, f32[32,128]{1,0:T(8,128)S(1)}) custom-call(s32[4]{0:T(128)S(1)} %pad_add_fusion.where, f32[1024,128]{1,0:T(8,128)S(1)} %bitcast.21, f32[256,128]{1,0:T(8,128)S(1)} %bitcast.22, f32[32,128]{1,0:T(8,128)S(1)} %copy-done.9, f32[32,128]{1,0:T(8,128)S(1)} %copy-done.10, f32[32,128]{1,0:T(8,128)S(1)} %get-tuple-element.22.last_row, ...), custom_call_target="tpu_custom_call" | custom-call | flops 1000000000 | bytes 1000000 | tf_op jit(solution)/shard_map/river_kernel/pallas_call | solution.py:418
  55.9 8.0 %all-to-all-start.2 = ((f32[64,17,1,128]{3,2,1,0:T(1,128)}), f32[64,17,1,128]{3,2,1,0:T(1,128)S(1)}, u32[]{:S(2)}, u32[]{:S(2)}) async-start(f32[64,17,1,128]{3,2,1,0:T(1,128)} %bitcast.10), calls=%async_computation.2 | async-start | bytes 1114112 | tf_op jit(solution)/shard_map/all_to_all | solution.py:434
  63.8 2.1 %collective-permute-start.2 = (f32[48,128]{1,0:T(8,128)S(1)}, f32[48,128]{1,0:T(8,128)S(1)}, u32[]{:S(2)}, u32[]{:S(2)}) collective-permute-start(f32[48,128]{1,0:T(8,128)S(1)} %get-tuple-element.17), channel_id=1, source_target_pairs={{0,4},{4,8},{8,12},{12,16},{16,20},{20,24},{24,28},{28,32},{32,36}... | collective-permute-start | bytes 73736 | tf_op jit(solution)/shard_map/ppermute | solution.py:414
  65.9 5.6 %collective-permute-start.3 = (f32[48,128]{1,0:T(8,128)S(1)}, f32[48,128]{1,0:T(8,128)S(1)}, u32[]{:S(2)}, u32[]{:S(2)}) collective-permute-start(f32[48,128]{1,0:T(8,128)S(1)} %get-tuple-element.18.order), channel_id=1, source_target_pairs={{4,0},{8,4},{12,8},{16,12},{20,16},{24,20},{28,24},{32,28},{36,32}... | collective-permute-start | bytes 73736 | tf_op jit(solution)/shard_map/ppermute | solution.py:415
  71.5 8.9 %collective-permute-done.2.west = f32[48,128]{1,0:T(8,128)S(1)} collective-permute-done((f32[48,128]{1,0:T(8,128)S(1)}, f32[48,128]{1,0:T(8,128)S(1)}, u32[]{:S(2)}, u32[]{:S(2)}) %collective-permute-start.2) | collective-permute-done | bytes 24608 | tf_op jit(solution)/shard_map/ppermute | solution.py:414
  80.4 7.5 %flood_kernel.1 = (f32[128,512]{1,0:T(8,128)S(1)}, f32[128,512]{1,0:T(8,128)}, f32[128,512]{1,0:T(8,128)}) custom-call(s32[4]{0:T(128)S(1)} %pad_add_fusion.where, f32[40,512]{1,0:T(8,128)S(1)} %collective-permute-done.above, f32[40,512]{1,0:T(8,128)S(1)} %collective-permute-done.1.below, f32[48,128]{1,0:T(8,128)S(1)} %collective-permute-done.2.west, ...), custom_call_target="tpu_custom_call" | custom-call | flops 100000000 | bytes 10000000 | tf_op jit(solution)/shard_map/flood_kernel/pallas_call | solution.py:440
  87.9 0.8 flow_kernel.1
  88.8 0.1 copy.21
  88.9 0.4 collective-permute-start.4
  89.3 2.2 %collective-permute-start.5 = (f32[1,128]{1,0:T(1,128)S(1)}, f32[1,128]{1,0:T(1,128)S(1)}, u32[]{:S(2)}, u32[]{:S(2)}) collective-permute-start(f32[1,128]{1,0:T(1,128)S(1)} %bitcast.28), channel_id=1, source_target_pairs={{0,2},{1,3},{2,0},{3,1},{4,6},{5,7},{6,4},{7,5},{8,10},{9,11},{10,... | collective-permute-start | bytes 1544 | tf_op jit(solution)/shard_map/ppermute | solution.py:454
  91.5 1.3 %collective-permute-start.6 = (f32[1,128]{1,0:T(1,128)S(1)}, f32[1,128]{1,0:T(1,128)S(1)}, u32[]{:S(2)}, u32[]{:S(2)}) collective-permute-start(f32[1,128]{1,0:T(1,128)S(1)} %bitcast.29), channel_id=1, source_target_pairs={{0,3},{1,0},{2,1},{3,2},{4,7},{5,4},{6,5},{7,6},{8,11},{9,8},{10,9... | collective-permute-start | bytes 1544 | tf_op jit(solution)/shard_map/ppermute | solution.py:454
  92.8 1.4 %final_kernel.1 = f32[128,512]{1,0:T(8,128)} custom-call(f32[128,512]{1,0:T(8,128)S(1)} %get-tuple-element.19.water, f32[1088,128]{1,0:T(8,128)S(1)} %bitcast.20, f32[8,512]{1,0:T(8,128)S(1)} %get-tuple-element.24.slots), custom_call_target="tpu_custom_call" | custom-call | flops 1000000000 | bytes 1000000 | tf_op jit(solution)/shard_map/final_kernel/pallas_call | solution.py:455
  94.2 0.1 collective-permute-done.5
  94.3 0.7 collective-permute-done.6
  95.0 0.1 dynamic-slice_bitcast_fusion
  95.1 0.7 multiply_add_fusion
  (36 shorter events, 0.2 us)
Async XLA Ops:
  0.6 0.7 copy-start.12
  0.6 0.7 copy-start.11
  0.7 0.7 copy-start.13
  1.3 1.0 copy-start
  2.3 1.2 %copy-start.2 = (bf16[32,128,128]{2,1,0:T(8,128)(2,1)S(1)}, bf16[32,128,128]{2,1,0:T(8,128)(2,1)}, u32[]{:S(2)}) copy-start(bf16[32,128,128]{2,1,0:T(8,128)(2,1)} %inverse.1) | copy-start | bytes 3145732
  3.5 0.9 copy-start.7
  4.5 15.9 %copy-start.8 = (f32[128,512]{1,0:T(8,128)S(1)}, f32[128,512]{1,0:T(8,128)}, u32[]{:S(2)}) copy-start(f32[128,512]{1,0:T(8,128)} %water_h.1) | copy-start | bytes 786436
  6.6 13.7 %copy-start.1 = (f32[128,512]{1,0:T(8,128)S(1)}, f32[128,512]{1,0:T(8,128)}, u32[]{:S(2)}) copy-start(f32[128,512]{1,0:T(8,128)} %bed_h.1) | copy-start | bytes 786436
  6.7 21.6 %all-to-all-start.1 = ((f32[256,1,128]{2,1,0:T(1,128)}), f32[256,1,128]{2,1,0:T(1,128)S(1)}, u32[]{:S(2)}, u32[]{:S(2)}) async-start(f32[256,1,128]{2,1,0:T(1,128)} %bitcast.8), calls=%async_computation.1 | async-start | bytes 262144 | tf_op jit(solution)/shard_map/all_to_all | solution.py:402
  28.3 8.7 %copy-start.4 = (f32[128,512]{1,0:T(8,128)S(1)}, f32[128,512]{1,0:T(8,128)}, u32[]{:S(2)}) copy-start(f32[128,512]{1,0:T(8,128)} %f2.3) | copy-start | bytes 786436
  28.3 8.7 %copy-start.5 = (f32[128,512]{1,0:T(8,128)S(1)}, f32[128,512]{1,0:T(8,128)}, u32[]{:S(2)}) copy-start(f32[128,512]{1,0:T(8,128)} %f3.3) | copy-start | bytes 786436
  28.3 24.1 %all-to-all-start = ((f32[64,16,128]{2,1,0:T(8,128)}), f32[64,16,128]{2,1,0:T(8,128)S(1)}, u32[]{:S(2)}, u32[]{:S(2)}) async-start(f32[64,16,128]{2,1,0:T(8,128)} %bitcast.5), calls=%async_computation | async-start | bytes 1048576 | tf_op jit(solution)/shard_map/all_to_all | solution.py:399
  37.0 1.0 copy-start.6
  37.9 4.3 %collective-permute-start = (f32[40,512]{1,0:T(8,128)S(1)}, f32[40,512]{1,0:T(8,128)S(1)}, u32[]{:S(2)}, u32[]{:S(2)}) collective-permute-start(f32[40,512]{1,0:T(8,128)S(1)} %get-tuple-element.31), channel_id=1, source_target_pairs={{0,1},{1,2},{2,3},{4,5},{5,6},{6,7},{8,9},{9,10},{10,11},{12,13},{... | collective-permute-start | bytes 245768 | tf_op jit(solution)/shard_map/ppermute | solution.py:409
  40.2 6.3 %collective-permute-start.1 = (f32[40,512]{1,0:T(8,128)S(1)}, f32[40,512]{1,0:T(8,128)S(1)}, u32[]{:S(2)}, u32[]{:S(2)}) collective-permute-start(f32[40,512]{1,0:T(8,128)S(1)} %get-tuple-element.30), channel_id=1, source_target_pairs={{1,0},{2,1},{3,2},{5,4},{6,5},{7,6},{9,8},{10,9},{11,10},{13,12},{... | collective-permute-start | bytes 245768 | tf_op jit(solution)/shard_map/ppermute | solution.py:410
  41.6 10.9 %copy-start.9 = (f32[32,128]{1,0:T(8,128)S(1)}, f32[32,128]{1,0:T(8,128)}, u32[]{:S(2)}) copy-start(f32[32,128]{1,0:T(8,128)} %section.1) | copy-start | bytes 49156
  41.6 10.9 %copy-start.10 = (f32[32,128]{1,0:T(8,128)S(1)}, f32[32,128]{1,0:T(8,128)}, u32[]{:S(2)}) copy-start(f32[32,128]{1,0:T(8,128)} %reach_source.1) | copy-start | bytes 49156
  55.9 32.9 %all-to-all-start.2 = ((f32[64,17,1,128]{3,2,1,0:T(1,128)}), f32[64,17,1,128]{3,2,1,0:T(1,128)S(1)}, u32[]{:S(2)}, u32[]{:S(2)}) async-start(f32[64,17,1,128]{3,2,1,0:T(1,128)} %bitcast.10), calls=%async_computation.2 | async-start | bytes 1114112 | tf_op jit(solution)/shard_map/all_to_all | solution.py:434
  63.8 16.6 %collective-permute-start.2 = (f32[48,128]{1,0:T(8,128)S(1)}, f32[48,128]{1,0:T(8,128)S(1)}, u32[]{:S(2)}, u32[]{:S(2)}) collective-permute-start(f32[48,128]{1,0:T(8,128)S(1)} %get-tuple-element.17), channel_id=1, source_target_pairs={{0,4},{4,8},{8,12},{12,16},{16,20},{20,24},{24,28},{28,32},{32,36}... | collective-permute-start | bytes 73736 | tf_op jit(solution)/shard_map/ppermute | solution.py:414
  65.9 14.5 %collective-permute-start.3 = (f32[48,128]{1,0:T(8,128)S(1)}, f32[48,128]{1,0:T(8,128)S(1)}, u32[]{:S(2)}, u32[]{:S(2)}) collective-permute-start(f32[48,128]{1,0:T(8,128)S(1)} %get-tuple-element.18.order), channel_id=1, source_target_pairs={{4,0},{8,4},{12,8},{16,12},{20,16},{24,20},{28,24},{32,28},{36,32}... | collective-permute-start | bytes 73736 | tf_op jit(solution)/shard_map/ppermute | solution.py:415
  71.5 16.4 %copy-start.3 = (bf16[32,128,128]{2,1,0:T(8,128)(2,1)S(1)}, bf16[32,128,128]{2,1,0:T(8,128)(2,1)}, u32[]{:S(2)}) copy-start(bf16[32,128,128]{2,1,0:T(8,128)(2,1)} %inverse.1) | copy-start | bytes 3145732
  88.9 5.4 %collective-permute-start.4 = (f32[1,128]{1,0:T(1,128)S(1)}, f32[1,128]{1,0:T(1,128)S(1)}, u32[]{:S(2)}, u32[]{:S(2)}) collective-permute-start(f32[1,128]{1,0:T(1,128)S(1)} %bitcast.27), channel_id=1, source_target_pairs={{0,1},{1,2},{2,3},{3,0},{4,5},{5,6},{6,7},{7,4},{8,9},{9,10},{10,1... | collective-permute-start | bytes 1544 | tf_op jit(solution)/shard_map/ppermute | solution.py:454
  89.3 5.0 %collective-permute-start.5 = (f32[1,128]{1,0:T(1,128)S(1)}, f32[1,128]{1,0:T(1,128)S(1)}, u32[]{:S(2)}, u32[]{:S(2)}) collective-permute-start(f32[1,128]{1,0:T(1,128)S(1)} %bitcast.28), channel_id=1, source_target_pairs={{0,2},{1,3},{2,0},{3,1},{4,6},{5,7},{6,4},{7,5},{8,10},{9,11},{10,... | collective-permute-start | bytes 1544 | tf_op jit(solution)/shard_map/ppermute | solution.py:454
  91.5 3.5 %collective-permute-start.6 = (f32[1,128]{1,0:T(1,128)S(1)}, f32[1,128]{1,0:T(1,128)S(1)}, u32[]{:S(2)}, u32[]{:S(2)}) collective-permute-start(f32[1,128]{1,0:T(1,128)S(1)} %bitcast.29), channel_id=1, source_target_pairs={{0,3},{1,0},{2,1},{3,2},{4,7},{5,4},{6,5},{7,6},{8,11},{9,8},{10,9... | collective-permute-start | bytes 1544 | tf_op jit(solution)/shard_map/ppermute | solution.py:454

commit v3 on v2

--- a/solution.py
+++ b/solution.py
@@ -58,7 +58,7 @@
 
 def pack_kernel(
     water_h, bed_h, rows_h, blocks_h, inverse_h, down,
-    out, slots, tables, last_out,
+    out, slots, last_out,
     water, bed, link_rows, link_blocks, tails, row_s, sems,
 ):
     blocks_own, reach = last_out.shape
@@ -79,8 +79,7 @@
     links = rows.shape[1]
     height = water.shape[0]
     groups = water.shape[1] // LANES
-    tiles = out.shape[0] // SLOTS
-    bands = tables.shape[0] // tiles
+    tiles = out.shape[0] // CHUNK
     place = ((rows % groups) * height + rows // groups).astype(F32)
     dest = (blocks >> 7).astype(F32)
     local = (blocks & 31).astype(F32)
@@ -91,7 +90,7 @@
     earlier = (dest_c == dest) & (iota((links, links), 1) < iota((links, links), 0))
     ones = jnp.ones((links, LANES), BF16)
     rank = mm(earlier.astype(F32).astype(BF16), ones)
-    position = dest_c * float(SLOTS) + rank
+    position = dest_c * float(CHUNK) + rank
     position_c = position[:, 0:1]
     lane = iota((links, links), 1).astype(F32)
     slot_of = jnp.sum(jnp.where(place_c == lane, position_c, 0.0), axis=0, keepdims=True)
@@ -103,7 +102,7 @@
         [level[:, c * LANES : (c + 1) * LANES] for c in range(groups)], axis=0
     )
     by_block = paired(by_block)
-    step = 128
+    step = 8 * CHUNK
     for start in range(0, out.shape[0], step):
         hot = (iota((step, links), 0) + start).astype(F32) == slot_of
         out[start : start + step, :] = fold(mm(hot.astype(F32).astype(BF16), by_block))
@@ -122,74 +121,102 @@
     gain = mm(first, seated.astype(BF16), ((1,), (1,)))
     row_s[...] = jnp.zeros(row_s.shape, F32)
     row_s[0:1, 0:blocks_own] = down[...].astype(F32)
-    entry = ids + (row_s[0:1, :] + gain[0:1, :])
-    for b in range(bands):
-        tables[pl.ds(b, tiles, bands), :] = entry
-
-
-def river_kernel(
-    where, rows_in, tables_in, section, reach_source, last_row, down, order, out, source
-):
+    out[pl.ds(SLOTS, tiles, CHUNK), :] = ids + (row_s[0:1, :] + gain[0:1, :])
+
+
+def lateral_kernel(rows_in, section, reach_source, last_row, order, out, source):
     total = rows_in.shape[0]
-    tiles = total // SLOTS
+    tiles = total // CHUNK
     blocks = section.shape[0]
-    bands = tables_in.shape[0] // tiles
-    band = where[1]
-    group = iota((tiles, LANES), 1) // blocks
-    turns = LANES // blocks
-    downs = jnp.zeros((tiles, LANES), F32)
-    gains = jnp.zeros((tiles, LANES), F32)
-    mine = jnp.zeros((tiles, LANES), F32)
-    for b in range(bands):
-        x = tables_in[pl.ds(b, tiles, bands), :]
-        mine = jnp.where(band == b, x, mine)
-        y = pltpu.roll(x, b * blocks, 1) if b else x
-        downs = jnp.where(group == b, y, downs)
-        turn = (b * blocks - GAIN_LANE) % LANES
-        y = pltpu.roll(x, turn, 1) if turn else x
-        gains = jnp.where(group == b, y, gains)
-    high = jnp.floor(downs * (1.0 / LANES))
-    tables = jnp.concatenate([high + 1.0, downs - high * LANES, gains], axis=1).astype(BF16)
-
-    slot = iota((total, 1), 0)
-    owner = slot // SLOTS
-    within = slot % SLOTS + ID_LANE
-    spread = (iota((total, tiles), 1) == owner).astype(F32).astype(BF16)
-    seat = mm(spread, mine.astype(BF16))
-    seat = jnp.where(iota((total, LANES), 1) == within, seat, 0.0)
+    slot = iota((total, 1), 0).astype(F32)
+    owner = jnp.floor((slot + 0.5) * (1.0 / CHUNK))
+    within = slot - owner * CHUNK + ID_LANE
+    lane = iota((total, LANES), 1).astype(F32)
+    extras = rows_in[pl.ds(SLOTS, tiles, CHUNK), :]
+    ids_here = iota((tiles, LANES), 1)
+    ids_here = (ids_here >= ID_LANE) & (ids_here < ID_LANE + SLOTS)
+    ids = jnp.where(ids_here, extras, 0.0).astype(BF16)
+    spread = (iota((total, tiles), 1).astype(F32) == owner).astype(F32).astype(BF16)
+    seat = jnp.where(lane == within, mm(spread, ids), 0.0)
     block = mm(seat.astype(BF16), jnp.ones((LANES, LANES), BF16)) - 1.0
-    hot = (block == iota((total, LANES), 1).astype(F32)).astype(F32).astype(BF16)
+    hot = (block == lane).astype(F32).astype(BF16)
     section_in = fold(mm(hot[:, :blocks], paired(section[...])))
     lateral = jnp.where(block >= 0.0, LATERAL_RATE * (rows_in[...] - section_in), 0.0)
+    out[...] = lateral
     sums = fold(mm(hot, paired(lateral), ((0,), (0,))))[:blocks]
     src = reach_source[...] + RIVER_SHARE * sums
     source[...] = src
-    ends = jnp.sum(src * last_row[...], axis=1, keepdims=True)
-
-    column = jnp.transpose(down[...])[:, 0:1]
-    column_high = jnp.floor(column * (1.0 / LANES))
-    high, low = column_high + 1.0, column - column_high * LANES
-    factor = jnp.ones((blocks, 1), F32)
-    tile_lane = iota((blocks, tiles), 1).astype(F32) + 1.0
-    block_lane = iota((blocks, LANES), 1).astype(F32)
-    lefts, rights = [], []
+    ends = jnp.concatenate([src * last_row[...], jnp.zeros((LANES - blocks, LANES), F32)], axis=0)
+    ends_hi, ends_lo = halves(ends)
+    ones = jnp.ones((8, LANES), BF16)
+    row = mm(ones, ends_hi, ((1,), (1,))) + mm(ones, ends_lo, ((1,), (1,)))
+    out[pl.ds(SLOTS, tiles, CHUNK), :] = jnp.broadcast_to(row[0:1, :], (tiles, LANES))
+
+
+def dense(ref, blocks, start, step, count):
+    turns = LANES // blocks
+    group = iota((count // turns, LANES), 1) // blocks
+    rows = jnp.zeros((count // turns, LANES), F32)
+    for turn in range(turns):
+        x = ref[pl.ds(start + turn * step, count // turns, turns * step), :]
+        x = pltpu.roll(x, turn * blocks, 1) if turn else x
+        rows = jnp.where(group == turn, x, rows)
+    return rows
+
+
+def paths_kernel(where, own, one, two, three, reach):
+    bands = 4
+    band, me = where[1], where[0].astype(F32) + 1.0
+    tiles = own.shape[0]
+    blocks = LANES // bands
+    group = iota((tiles, LANES), 1) // blocks
+    downs = jnp.zeros((tiles, LANES), F32)
+    gains = jnp.zeros((tiles, LANES), F32)
+    for back, ref in enumerate((own, one, two, three)):
+        here = group == (band + bands - back) % bands
+        x = ref[...]
+        down, gain = x, x
+        for turn in (1, 2, 3):
+            y = pltpu.roll(x, turn * blocks, 1)
+            down = jnp.where(group == turn, y, down)
+            gain = jnp.where(group == (turn + GAIN_LANE // blocks) % bands, y, gain)
+        downs = jnp.where(here, down, downs)
+        gains = jnp.where(here, gain, gains)
+    high = jnp.floor(downs * (1.0 / LANES))
+    parts = (high + 1.0, downs - high * LANES, gains)
+    tables = jnp.concatenate([jnp.transpose(x) for x in parts], axis=0).astype(BF16)
+    sources = dense(own, blocks, 0, 1, tiles)
+    chunks = sources.shape[0]
+    high = jnp.floor(sources * (1.0 / LANES))
+    low = sources - high * LANES
+    high = high + 1.0
+    tile_row = iota((tiles, LANES), 0).astype(F32) + 1.0
+    block_row = iota((LANES, LANES), 0).astype(F32)
+    state = [(high[i : i + 1], low[i : i + 1], jnp.ones((1, LANES), F32)) for i in range(chunks)]
     for hop in range(LEVELS - 1):
-        left = (tile_lane == high).astype(F32)
-        right = (block_lane == low).astype(F32)
-        lefts.append(left * factor)
-        rights.append(right.astype(BF16))
-        if hop < LEVELS - 2:
-            found = mm(left.astype(BF16), tables)
-            high = jnp.sum(found[:, :LANES] * right, axis=1, keepdims=True)
-            low = jnp.sum(found[:, LANES : 2 * LANES] * right, axis=1, keepdims=True)
-            factor = factor * jnp.sum(found[:, 2 * LANES :] * right, axis=1, keepdims=True)
-    left = jnp.concatenate([x * ends for x in lefts], axis=0)
-    left_hi, left_lo = halves(left)
-    right = jnp.concatenate(rights, axis=0)
-    pushed = mm(left_hi, right, ((0,), (0,))) + mm(left_lo, right, ((0,), (0,)))
-    for t in range(tiles):
-        out[t * CHUNK : t * CHUNK + SLOTS, :] = lateral[t * SLOTS : (t + 1) * SLOTS]
-    out[pl.ds(SLOTS, tiles, CHUNK), :] = pushed
+        for i, (hi, lo, factor) in enumerate(state):
+            cols = slice(i * LANES, (i + 1) * LANES)
+            hit = block_row == lo
+            mine = jnp.where(hit, jnp.where(hi == me, factor, 0.0), 0.0)
+            reach[:, cols] = mine if hop == 0 else reach[:, cols] + mine
+            if hop < LEVELS - 2:
+                found = mm(tables, (tile_row == hi).astype(F32).astype(BF16))
+                next_hi = jnp.sum(jnp.where(hit, found[:LANES], 0.0), axis=0, keepdims=True)
+                next_lo = jnp.sum(jnp.where(hit, found[LANES : 2 * LANES], 0.0), axis=0, keepdims=True)
+                gain = jnp.sum(jnp.where(hit, found[2 * LANES :], 0.0), axis=0, keepdims=True)
+                state[i] = (next_hi, next_lo, factor * gain)
+
+
+def gather_kernel(returned, reach, out):
+    tiles = returned.shape[0] // CHUNK
+    blocks = reach.shape[1] // tiles
+    ends = dense(returned, blocks, SLOTS, CHUNK, tiles)
+    total = jnp.zeros((LANES, LANES), F32)
+    for i in range(ends.shape[0]):
+        total = total + reach[:, i * LANES : (i + 1) * LANES] * ends[i : i + 1, :]
+    hi, lo = halves(total)
+    ones = jnp.ones((8, LANES), BF16)
+    out[...] = mm(ones, hi, ((1,), (1,))) + mm(ones, lo, ((1,), (1,)))
 
 
 def flow_kernel(source, inverse, base, column):
@@ -212,8 +239,7 @@
     total = returned.shape[0]
     height = water.shape[0]
     groups = water.shape[1] // LANES
-    slot = slots[...]
-    slot_c = jnp.transpose(slot + jnp.floor(slot * (1.0 / SLOTS)))[:, 0:1]
+    slot_c = jnp.transpose(slots[...])[:, 0:1]
     rows = paired(returned[...])
     for c in range(groups):
         mine = slot_c[c * height : (c + 1) * height]
@@ -380,9 +406,9 @@
     ring = [[(i, (i + k) % bands) for i in range(bands)] for k in range(bands)]
 
     down = block_down.reshape(1, blocks)
-    payload, slots, tables, last_row = call(
+    payload, slots, last_row = call(
         pack_kernel,
-        (shaped(tiles * SLOTS, LANES), shaped(8, links), shaped(tiles * bands, LANES), shaped(blocks, reach)),
+        (shaped(total, LANES), shaped(8, links), shaped(blocks, reach)),
         [HBM] * 5 + [VMEM],
         scratch=[
             pltpu.VMEM((height, width), F32),
@@ -397,10 +423,7 @@
         size=10**6,
     )(water_depth, bed_level, link_rows.reshape(1, links), link_blocks.reshape(1, links), reach_inverse, down)
     rows_in = lax.all_to_all(
-        payload.reshape(tiles, SLOTS, LANES), "tile", split_axis=0, concat_axis=0, tiled=True
-    )
-    tables_in = lax.all_to_all(
-        tables.reshape(tiles * bands, 1, LANES), ("tile", "band"), split_axis=0, concat_axis=0, tiled=True
+        payload.reshape(tiles, CHUNK, 1, LANES), "tile", split_axis=0, concat_axis=0, tiled=True
     )
 
     fields = (bed_level + water_depth, bed_level, roughness, flux_east, flux_south)
@@ -414,23 +437,13 @@
     west = lax.ppermute(right, "tile", [(i, i + 1) for i in range(tiles - 1)])
     east = lax.ppermute(left, "tile", [(i + 1, i) for i in range(tiles - 1)])
 
-    column_down = jnp.broadcast_to(block_down.astype(F32)[None, :], (8, blocks))
     answer, source = call(
-        river_kernel,
+        lateral_kernel,
         (shaped(total, LANES), shaped(blocks, LANES)),
-        [SMEM] + [VMEM] * 6 + [ANY],
+        [VMEM] * 4 + [ANY],
         flops=10**9,
         size=10**6,
-    )(
-        where,
-        rows_in.reshape(tiles * SLOTS, LANES),
-        tables_in.reshape(tiles * bands, LANES),
-        river_section,
-        reach_source,
-        last_row,
-        column_down,
-        left,
-    )
+    )(rows_in.reshape(total, LANES), river_section, reach_source, last_row, west)
     returned = lax.all_to_all(
         answer.reshape(tiles, CHUNK, 1, LANES), "tile", split_axis=0, concat_axis=0, tiled=True
     )
@@ -449,8 +462,15 @@
     base_flow, column = call(
         flow_kernel, (shaped(blocks, reach),) * 2, [VMEM] * 2, flops=10**8, size=10**6
     )(source, reach_inverse)
-
-    pushed = jnp.sum(returned.reshape(tiles, CHUNK, LANES)[:, SLOTS, :], axis=0, keepdims=True)
+    extras = rows_in.reshape(tiles, CHUNK, LANES)[:, SLOTS, :]
+    others = [lax.ppermute(extras, "band", ring[k]) for k in (1, 2, 3)]
+    reached = call(
+        paths_kernel, shaped(LANES, tiles * blocks), [SMEM] + [VMEM] * 4, flops=10**9, size=10**6
+    )(where, extras, *others)
+
+    pushed = call(gather_kernel, shaped(8, LANES), [VMEM] * 2, flops=10**6, size=10**6)(
+        returned.reshape(total, LANES), reached
+    )[0:1]
     parts = [pushed] + [lax.ppermute(pushed, "band", ring[k]) for k in (1, 2, 3)]
     final_depth = call(
         final_kernel, shaped(height, width), [VMEM] * 3, flops=10**9, size=10**6

time: 96.3 us -> 83.3 us (0.87)
  the two profiles are of different devices: /device:TPU:160 before, /device:TPU:7 now
where the time goes in v3:
time: 83.3 us; the launch traced here: 82.7 us
  starting transfers between devices  44 us (53%)
  Pallas kernels  18.4 us (22%)
  waiting for transfers between devices  13.5 us (16%)
  local copies, waits for them, and re-layouts  5.01 us (6%)
  between operations  0.94 us (1%)
    all_to_all x1, starting transfers between devices, per_device(): lax.all_to_all(payload.reshape(tiles, CHUNK, 1, LANES), 'tile', split_axi...  12.4 us
    all_to_all x1, starting transfers between devices, per_device(): lax.all_to_all(answer.reshape(tiles, CHUNK, 1, LANES), 'tile', split_axis...  10.9 us
    pallas_call x1, Pallas kernels, per_device(): call(flood_kernel, (shaped(height, width),) * 3, [SMEM] + [VMEM] * 9, scr...  7.51 us
    ppermute x1, waiting for transfers between devices, per_device(): east = lax.ppermute(left, 'tile', [(i + 1, i) for i in range(tiles - 1)])  7.27 us
    unnamed x32, local copies, waits for them, and re-layouts  4.87 us
    ppermute x3, starting transfers between devices, per_device(): others = [lax.ppermute(extras, 'band', ring[k]) for k in (1, 2, 3)]  4.77 us
    ppermute x3, starting transfers between devices, per_device(): lax.ppermute(pushed, 'band', ring[k])  4.7 us
    ppermute x1, starting transfers between devices, per_device(): west = lax.ppermute(right, 'tile', [(i, i + 1) for i in range(tiles - 1)])  4.47 us
  transfers between devices with their start and end apart: 12, of which 5 were waited for; matrix products, arithmetic and copies ran while one was open for 0% of the time, Pallas kernels for 17%

profile of v3, /device:TPU:7, one launch (start us, length us, event | category | flops | bytes accessed | tf_op | source)
XLA Modules:
  0.0 82.7 jit_solution(6425330068570684693)
XLA Ops:
  0.7 0.7 copy-done.12
  1.3 0.9 %copy-done = f32[128,512]{1,0:T(8,128)S(1)} copy-done((f32[128,512]{1,0:T(8,128)S(1)}, f32[128,512]{1,0:T(8,128)}, u32[]{:S(2)}) %copy-start) | copy-done | bytes 262168
  2.3 1.2 %copy-done.2 = bf16[32,128,128]{2,1,0:T(8,128)(2,1)S(1)} copy-done((bf16[32,128,128]{2,1,0:T(8,128)(2,1)S(1)}, bf16[32,128,128]{2,1,0:T(8,128)(2,1)}, u32[]{:S(2)}) %copy-start.2) | copy-done | bytes 1048600
  3.5 0.9 %copy-done.7 = f32[128,512]{1,0:T(8,128)S(1)} copy-done((f32[128,512]{1,0:T(8,128)S(1)}, f32[128,512]{1,0:T(8,128)}, u32[]{:S(2)}) %copy-start.7) | copy-done | bytes 262168
  4.5 2.4 %pack_kernel.1 = (f32[1088,128]{1,0:T(8,128)}, f32[8,512]{1,0:T(8,128)S(1)}, f32[32,128]{1,0:T(8,128)S(1)}) custom-call(f32[128,512]{1,0:T(8,128)S(1)} %copy-done.7, f32[128,512]{1,0:T(8,128)S(1)} %copy-done, s32[1,512]{1,0:T(1,128)S(1)} %bitcast.19, s32[1,512]{1,0:T(1,128)S(1)} %bitcast.20, bf16[32,128,128]{2,1,0:T(8,128)(2,1)S(1)} %copy-done.2, ...), custom_call_target="tpu_custom_call" | custom-call | flops 1000000000 | bytes 1000000 | tf_op jit(solution)/shard_map/pack_kernel/pallas_call | solution.py:409
  6.8 12.4 %all-to-all-start = ((f32[64,17,1,128]{3,2,1,0:T(1,128)}), f32[64,17,1,128]{3,2,1,0:T(1,128)S(1)}, u32[]{:S(2)}, u32[]{:S(2)}) async-start(f32[64,17,1,128]{3,2,1,0:T(1,128)} %bitcast.5), calls=%async_computation | async-start | bytes 1114112 | tf_op jit(solution)/shard_map/all_to_all | solution.py:425
  19.4 0.8 %copy-done.4 = f32[128,512]{1,0:T(8,128)S(1)} copy-done((f32[128,512]{1,0:T(8,128)S(1)}, f32[128,512]{1,0:T(8,128)}, u32[]{:S(2)}) %copy-start.4) | copy-done | bytes 262168
  20.3 0.1 copy-done.6
  20.4 3.2 %collective-permute-start = (f32[40,512]{1,0:T(8,128)S(1)}, f32[40,512]{1,0:T(8,128)S(1)}, u32[]{:S(2)}, u32[]{:S(2)}) collective-permute-start(f32[40,512]{1,0:T(8,128)S(1)} %get-tuple-element.29), channel_id=1, source_target_pairs={{0,1},{1,2},{2,3},{4,5},{5,6},{6,7},{8,9},{9,10},{10,11},{12,13},{... | collective-permute-start | bytes 245768 | tf_op jit(solution)/shard_map/ppermute | solution.py:432
  23.6 1.3 %collective-permute-start.1 = (f32[40,512]{1,0:T(8,128)S(1)}, f32[40,512]{1,0:T(8,128)S(1)}, u32[]{:S(2)}, u32[]{:S(2)}) collective-permute-start(f32[40,512]{1,0:T(8,128)S(1)} %get-tuple-element.28), channel_id=1, source_target_pairs={{1,0},{2,1},{3,2},{5,4},{6,5},{7,6},{9,8},{10,9},{11,10},{13,12},{... | collective-permute-start | bytes 245768 | tf_op jit(solution)/shard_map/ppermute | solution.py:433
  24.9 0.1 collective-permute-done.above
  25.1 4.0 %collective-permute-done.1.below = f32[40,512]{1,0:T(8,128)S(1)} collective-permute-done((f32[40,512]{1,0:T(8,128)S(1)}, f32[40,512]{1,0:T(8,128)S(1)}, u32[]{:S(2)}, u32[]{:S(2)}) %collective-permute-start.1) | collective-permute-done | bytes 81952 | tf_op jit(solution)/shard_map/ppermute | solution.py:433
  29.1 0.2 strips_kernel.1
  29.4 4.5 %collective-permute-start.2 = (f32[48,128]{1,0:T(8,128)S(1)}, f32[48,128]{1,0:T(8,128)S(1)}, u32[]{:S(2)}, u32[]{:S(2)}) collective-permute-start(f32[48,128]{1,0:T(8,128)S(1)} %get-tuple-element.16), channel_id=1, source_target_pairs={{0,4},{4,8},{8,12},{12,16},{16,20},{20,24},{24,28},{28,32},{32,36}... | collective-permute-start | bytes 73736 | tf_op jit(solution)/shard_map/ppermute | solution.py:437
  33.9 0.9 %collective-permute-done.2.west.order = f32[48,128]{1,0:T(8,128)S(1)} collective-permute-done((f32[48,128]{1,0:T(8,128)S(1)}, f32[48,128]{1,0:T(8,128)S(1)}, u32[]{:S(2)}, u32[]{:S(2)}) %collective-permute-start.2) | collective-permute-done | bytes 24608 | tf_op jit(solution)/shard_map/ppermute | solution.py:437
  34.8 1.2 %all-to-all-done = f32[64,17,1,128]{3,2,1,0:T(1,128)S(1)} async-done(((f32[64,17,1,128]{3,2,1,0:T(1,128)}), f32[64,17,1,128]{3,2,1,0:T(1,128)S(1)}, u32[]{:S(2)}, u32[]{:S(2)}) %all-to-all-start) | async-done | bytes 557088 | tf_op jit(solution)/shard_map/all_to_all | solution.py:425
  35.9 1.8 %lateral_kernel.1 = (f32[1088,128]{1,0:T(8,128)}, f32[32,128]{1,0:T(8,128)S(1)}) custom-call(f32[1088,128]{1,0:T(8,128)S(1)} %bitcast.18, f32[32,128]{1,0:T(8,128)S(1)} %copy-done.9, f32[32,128]{1,0:T(8,128)S(1)} %copy-done.10, f32[32,128]{1,0:T(8,128)S(1)} %get-tuple-element.20.last_row, f32[48,128]{1,0:T(8,128)S(1)} %collective-permute-done.2.west.order), custom_call_target="tpu_custom_call" | custom-call | flops 1000000000 | bytes 1000000 | tf_op jit(solution)/shard_map/lateral_kernel/pallas_call | solution.py:440
  37.7 10.9 %all-to-all-start.1 = ((f32[64,17,1,128]{3,2,1,0:T(1,128)}), f32[64,17,1,128]{3,2,1,0:T(1,128)S(1)}, u32[]{:S(2)}, u32[]{:S(2)}) async-start(f32[64,17,1,128]{3,2,1,0:T(1,128)} %bitcast.7), calls=%async_computation.1 | async-start | bytes 1114112 | tf_op jit(solution)/shard_map/all_to_all | solution.py:447
  48.7 2.3 %collective-permute-start.3 = (f32[48,128]{1,0:T(8,128)S(1)}, f32[48,128]{1,0:T(8,128)S(1)}, u32[]{:S(2)}, u32[]{:S(2)}) collective-permute-start(f32[48,128]{1,0:T(8,128)S(1)} %get-tuple-element.17), channel_id=1, source_target_pairs={{4,0},{8,4},{12,8},{16,12},{20,16},{24,20},{28,24},{32,28},{36,32}... | collective-permute-start | bytes 73736 | tf_op jit(solution)/shard_map/ppermute | solution.py:438
  51.0 1.4 %collective-permute-start.4 = (f32[64,128]{1,0:T(8,128)S(1)}, f32[64,128]{1,0:T(8,128)S(1)}, u32[]{:S(2)}, u32[]{:S(2)}) collective-permute-start(f32[64,128]{1,0:T(8,128)S(1)} %slice_bitcast_fusion.own), channel_id=1, source_target_pairs={{0,1},{1,2},{2,3},{3,0},{4,5},{5,6},{6,7},{7,4},{8,9},{9,10},{10,1... | collective-permute-start | bytes 98312 | tf_op jit(solution)/shard_map/ppermute | solution.py:466
  52.4 1.4 %collective-permute-start.5 = (f32[64,128]{1,0:T(8,128)S(1)}, f32[64,128]{1,0:T(8,128)S(1)}, u32[]{:S(2)}, u32[]{:S(2)}) collective-permute-start(f32[64,128]{1,0:T(8,128)S(1)} %slice_bitcast_fusion.own), channel_id=1, source_target_pairs={{0,2},{1,3},{2,0},{3,1},{4,6},{5,7},{6,4},{7,5},{8,10},{9,11},{10,... | collective-permute-start | bytes 98312 | tf_op jit(solution)/shard_map/ppermute | solution.py:466
  53.8 2.0 %collective-permute-start.6 = (f32[64,128]{1,0:T(8,128)S(1)}, f32[64,128]{1,0:T(8,128)S(1)}, u32[]{:S(2)}, u32[]{:S(2)}) collective-permute-start(f32[64,128]{1,0:T(8,128)S(1)} %slice_bitcast_fusion.own), channel_id=1, source_target_pairs={{0,3},{1,0},{2,1},{3,2},{4,7},{5,4},{6,5},{7,6},{8,11},{9,8},{10,9... | collective-permute-start | bytes 98312 | tf_op jit(solution)/shard_map/ppermute | solution.py:466
  55.9 7.3 %collective-permute-done.3.east = f32[48,128]{1,0:T(8,128)S(1)} collective-permute-done((f32[48,128]{1,0:T(8,128)S(1)}, f32[48,128]{1,0:T(8,128)S(1)}, u32[]{:S(2)}, u32[]{:S(2)}) %collective-permute-start.3) | collective-permute-done | bytes 24608 | tf_op jit(solution)/shard_map/ppermute | solution.py:438
  63.1 7.5 %flood_kernel.1 = (f32[128,512]{1,0:T(8,128)S(1)}, f32[128,512]{1,0:T(8,128)}, f32[128,512]{1,0:T(8,128)}) custom-call(s32[4]{0:T(128)S(1)} %pad_add_fusion.where, f32[40,512]{1,0:T(8,128)S(1)} %collective-permute-done.above, f32[40,512]{1,0:T(8,128)S(1)} %collective-permute-done.1.below, f32[48,128]{1,0:T(8,128)S(1)} %collective-permute-done.2.west.order, ...), custom_call_target="tpu_custom_call" | custom-call | flops 100000000 | bytes 10000000 | tf_op jit(solution)/shard_map/flood_kernel/pallas_call | solution.py:453
  70.7 0.8 flow_kernel.1
  71.5 4.0 %paths_kernel.1.reach = f32[128,2048]{1,0:T(8,128)S(1)} custom-call(s32[4]{0:T(128)S(1)} %pad_add_fusion.where, f32[64,128]{1,0:T(8,128)S(1)} %slice_bitcast_fusion.own, f32[64,128]{1,0:T(8,128)S(1)} %collective-permute-done.4.one, f32[64,128]{1,0:T(8,128)S(1)} %collective-permute-done.5.two, f32[64,128]{1,0:T(8,128)S(1)} %collective-permute-done.6.three), custom_call_target="tpu_custom_call" | custom-call | flops 1000000000 | bytes 1000000 | tf_op jit(solution)/shard_map/paths_kernel/pallas_call | solution.py:467
  75.6 0.3 gather_kernel.1
  75.8 1.3 %collective-permute-start.7 = (f32[1,128]{1,0:T(1,128)S(1)}, f32[1,128]{1,0:T(1,128)S(1)}, u32[]{:S(2)}, u32[]{:S(2)}) collective-permute-start(f32[1,128]{1,0:T(1,128)S(1)} %slice.47), channel_id=1, source_target_pairs={{0,1},{1,2},{2,3},{3,0},{4,5},{5,6},{6,7},{7,4},{8,9},{9,10},{10,1... | collective-permute-start | bytes 1544 | tf_op jit(solution)/shard_map/ppermute | solution.py:474
  77.1 1.4 %collective-permute-start.8 = (f32[1,128]{1,0:T(1,128)S(1)}, f32[1,128]{1,0:T(1,128)S(1)}, u32[]{:S(2)}, u32[]{:S(2)}) collective-permute-start(f32[1,128]{1,0:T(1,128)S(1)} %slice.47), channel_id=1, source_target_pairs={{0,2},{1,3},{2,0},{3,1},{4,6},{5,7},{6,4},{7,5},{8,10},{9,11},{10,... | collective-permute-start | bytes 1544 | tf_op jit(solution)/shard_map/ppermute | solution.py:474
  78.5 2.0 %collective-permute-start.9 = (f32[1,128]{1,0:T(1,128)S(1)}, f32[1,128]{1,0:T(1,128)S(1)}, u32[]{:S(2)}, u32[]{:S(2)}) collective-permute-start(f32[1,128]{1,0:T(1,128)S(1)} %slice.47), channel_id=1, source_target_pairs={{0,3},{1,0},{2,1},{3,2},{4,7},{5,4},{6,5},{7,6},{8,11},{9,8},{10,9... | collective-permute-start | bytes 1544 | tf_op jit(solution)/shard_map/ppermute | solution.py:474
  80.5 1.4 %final_kernel.1 = f32[128,512]{1,0:T(8,128)} custom-call(f32[128,512]{1,0:T(8,128)S(1)} %get-tuple-element.18.water, f32[1088,128]{1,0:T(8,128)S(1)} %bitcast.17, f32[8,512]{1,0:T(8,128)S(1)} %get-tuple-element.22.slots), custom_call_target="tpu_custom_call" | custom-call | flops 1000000000 | bytes 1000000 | tf_op jit(solution)/shard_map/final_kernel/pallas_call | solution.py:475
  82.1 0.7 multiply_add_fusion
  (41 shorter events, 0.4 us)
Async XLA Ops:
  0.6 0.7 copy-start.12
  0.6 0.7 copy-start.11
  0.7 0.7 copy-start.13
  1.3 1.0 %copy-start = (f32[128,512]{1,0:T(8,128)S(1)}, f32[128,512]{1,0:T(8,128)}, u32[]{:S(2)}) copy-start(f32[128,512]{1,0:T(8,128)} %bed_h.1) | copy-start | bytes 786436
  2.3 1.2 %copy-start.2 = (bf16[32,128,128]{2,1,0:T(8,128)(2,1)S(1)}, bf16[32,128,128]{2,1,0:T(8,128)(2,1)}, u32[]{:S(2)}) copy-start(bf16[32,128,128]{2,1,0:T(8,128)(2,1)} %inverse.1) | copy-start | bytes 3145732
  3.5 0.9 %copy-start.7 = (f32[128,512]{1,0:T(8,128)S(1)}, f32[128,512]{1,0:T(8,128)}, u32[]{:S(2)}) copy-start(f32[128,512]{1,0:T(8,128)} %water_h.1) | copy-start | bytes 786436
  6.8 12.5 %copy-start.1 = (f32[128,512]{1,0:T(8,128)S(1)}, f32[128,512]{1,0:T(8,128)}, u32[]{:S(2)}) copy-start(f32[128,512]{1,0:T(8,128)} %bed_h.1) | copy-start | bytes 786436
  6.8 12.5 %copy-start.8 = (f32[128,512]{1,0:T(8,128)S(1)}, f32[128,512]{1,0:T(8,128)}, u32[]{:S(2)}) copy-start(f32[128,512]{1,0:T(8,128)} %water_h.1) | copy-start | bytes 786436
  6.8 29.1 %all-to-all-start = ((f32[64,17,1,128]{3,2,1,0:T(1,128)}), f32[64,17,1,128]{3,2,1,0:T(1,128)S(1)}, u32[]{:S(2)}, u32[]{:S(2)}) async-start(f32[64,17,1,128]{3,2,1,0:T(1,128)} %bitcast.5), calls=%async_computation | async-start | bytes 1114112 | tf_op jit(solution)/shard_map/all_to_all | solution.py:425
  19.3 1.0 %copy-start.4 = (f32[128,512]{1,0:T(8,128)S(1)}, f32[128,512]{1,0:T(8,128)}, u32[]{:S(2)}) copy-start(f32[128,512]{1,0:T(8,128)} %f2.3) | copy-start | bytes 786436
  19.3 1.0 %copy-start.5 = (f32[128,512]{1,0:T(8,128)S(1)}, f32[128,512]{1,0:T(8,128)}, u32[]{:S(2)}) copy-start(f32[128,512]{1,0:T(8,128)} %f3.3) | copy-start | bytes 786436
  19.4 1.1 %copy-start.6 = (f32[128,512]{1,0:T(8,128)S(1)}, f32[128,512]{1,0:T(8,128)}, u32[]{:S(2)}) copy-start(f32[128,512]{1,0:T(8,128)} %f4.3) | copy-start | bytes 786436
  20.4 4.7 %collective-permute-start = (f32[40,512]{1,0:T(8,128)S(1)}, f32[40,512]{1,0:T(8,128)S(1)}, u32[]{:S(2)}, u32[]{:S(2)}) collective-permute-start(f32[40,512]{1,0:T(8,128)S(1)} %get-tuple-element.29), channel_id=1, source_target_pairs={{0,1},{1,2},{2,3},{4,5},{5,6},{6,7},{8,9},{9,10},{10,11},{12,13},{... | collective-permute-start | bytes 245768 | tf_op jit(solution)/shard_map/ppermute | solution.py:432
  23.6 12.3 %copy-start.9 = (f32[32,128]{1,0:T(8,128)S(1)}, f32[32,128]{1,0:T(8,128)}, u32[]{:S(2)}) copy-start(f32[32,128]{1,0:T(8,128)} %section.1) | copy-start | bytes 49156
  23.6 12.3 %copy-start.10 = (f32[32,128]{1,0:T(8,128)S(1)}, f32[32,128]{1,0:T(8,128)}, u32[]{:S(2)}) copy-start(f32[32,128]{1,0:T(8,128)} %reach_source.1) | copy-start | bytes 49156
  23.6 5.5 %collective-permute-start.1 = (f32[40,512]{1,0:T(8,128)S(1)}, f32[40,512]{1,0:T(8,128)S(1)}, u32[]{:S(2)}, u32[]{:S(2)}) collective-permute-start(f32[40,512]{1,0:T(8,128)S(1)} %get-tuple-element.28), channel_id=1, source_target_pairs={{1,0},{2,1},{3,2},{5,4},{6,5},{7,6},{9,8},{10,9},{11,10},{13,12},{... | collective-permute-start | bytes 245768 | tf_op jit(solution)/shard_map/ppermute | solution.py:433
  29.4 5.4 %collective-permute-start.2 = (f32[48,128]{1,0:T(8,128)S(1)}, f32[48,128]{1,0:T(8,128)S(1)}, u32[]{:S(2)}, u32[]{:S(2)}) collective-permute-start(f32[48,128]{1,0:T(8,128)S(1)} %get-tuple-element.16), channel_id=1, source_target_pairs={{0,4},{4,8},{8,12},{12,16},{16,20},{20,24},{24,28},{28,32},{32,36}... | collective-permute-start | bytes 73736 | tf_op jit(solution)/shard_map/ppermute | solution.py:437
  37.7 37.8 %all-to-all-start.1 = ((f32[64,17,1,128]{3,2,1,0:T(1,128)}), f32[64,17,1,128]{3,2,1,0:T(1,128)S(1)}, u32[]{:S(2)}, u32[]{:S(2)}) async-start(f32[64,17,1,128]{3,2,1,0:T(1,128)} %bitcast.7), calls=%async_computation.1 | async-start | bytes 1114112 | tf_op jit(solution)/shard_map/all_to_all | solution.py:447
  48.7 14.5 %collective-permute-start.3 = (f32[48,128]{1,0:T(8,128)S(1)}, f32[48,128]{1,0:T(8,128)S(1)}, u32[]{:S(2)}, u32[]{:S(2)}) collective-permute-start(f32[48,128]{1,0:T(8,128)S(1)} %get-tuple-element.17), channel_id=1, source_target_pairs={{4,0},{8,4},{12,8},{16,12},{20,16},{24,20},{28,24},{32,28},{36,32}... | collective-permute-start | bytes 73736 | tf_op jit(solution)/shard_map/ppermute | solution.py:438
  51.0 20.4 %collective-permute-start.4 = (f32[64,128]{1,0:T(8,128)S(1)}, f32[64,128]{1,0:T(8,128)S(1)}, u32[]{:S(2)}, u32[]{:S(2)}) collective-permute-start(f32[64,128]{1,0:T(8,128)S(1)} %slice_bitcast_fusion.own), channel_id=1, source_target_pairs={{0,1},{1,2},{2,3},{3,0},{4,5},{5,6},{6,7},{7,4},{8,9},{9,10},{10,1... | collective-permute-start | bytes 98312 | tf_op jit(solution)/shard_map/ppermute | solution.py:466
  52.4 19.1 %collective-permute-start.5 = (f32[64,128]{1,0:T(8,128)S(1)}, f32[64,128]{1,0:T(8,128)S(1)}, u32[]{:S(2)}, u32[]{:S(2)}) collective-permute-start(f32[64,128]{1,0:T(8,128)S(1)} %slice_bitcast_fusion.own), channel_id=1, source_target_pairs={{0,2},{1,3},{2,0},{3,1},{4,6},{5,7},{6,4},{7,5},{8,10},{9,11},{10,... | collective-permute-start | bytes 98312 | tf_op jit(solution)/shard_map/ppermute | solution.py:466
  53.8 17.7 %collective-permute-start.6 = (f32[64,128]{1,0:T(8,128)S(1)}, f32[64,128]{1,0:T(8,128)S(1)}, u32[]{:S(2)}, u32[]{:S(2)}) collective-permute-start(f32[64,128]{1,0:T(8,128)S(1)} %slice_bitcast_fusion.own), channel_id=1, source_target_pairs={{0,3},{1,0},{2,1},{3,2},{4,7},{5,4},{6,5},{7,6},{8,11},{9,8},{10,9... | collective-permute-start | bytes 98312 | tf_op jit(solution)/shard_map/ppermute | solution.py:466
  55.9 14.8 %copy-start.3 = (bf16[32,128,128]{2,1,0:T(8,128)(2,1)S(1)}, bf16[32,128,128]{2,1,0:T(8,128)(2,1)}, u32[]{:S(2)}) copy-start(bf16[32,128,128]{2,1,0:T(8,128)(2,1)} %inverse.1) | copy-start | bytes 3145732
  75.8 6.1 %collective-permute-start.7 = (f32[1,128]{1,0:T(1,128)S(1)}, f32[1,128]{1,0:T(1,128)S(1)}, u32[]{:S(2)}, u32[]{:S(2)}) collective-permute-start(f32[1,128]{1,0:T(1,128)S(1)} %slice.47), channel_id=1, source_target_pairs={{0,1},{1,2},{2,3},{3,0},{4,5},{5,6},{6,7},{7,4},{8,9},{9,10},{10,1... | collective-permute-start | bytes 1544 | tf_op jit(solution)/shard_map/ppermute | solution.py:474
  77.1 4.8 %collective-permute-start.8 = (f32[1,128]{1,0:T(1,128)S(1)}, f32[1,128]{1,0:T(1,128)S(1)}, u32[]{:S(2)}, u32[]{:S(2)}) collective-permute-start(f32[1,128]{1,0:T(1,128)S(1)} %slice.47), channel_id=1, source_target_pairs={{0,2},{1,3},{2,0},{3,1},{4,6},{5,7},{6,4},{7,5},{8,10},{9,11},{10,... | collective-permute-start | bytes 1544 | tf_op jit(solution)/shard_map/ppermute | solution.py:474
  78.5 3.4 %collective-permute-start.9 = (f32[1,128]{1,0:T(1,128)S(1)}, f32[1,128]{1,0:T(1,128)S(1)}, u32[]{:S(2)}, u32[]{:S(2)}) collective-permute-start(f32[1,128]{1,0:T(1,128)S(1)} %slice.47), channel_id=1, source_target_pairs={{0,3},{1,0},{2,1},{3,2},{4,7},{5,4},{6,5},{7,6},{8,11},{9,8},{10,9... | collective-permute-start | bytes 1544 | tf_op jit(solution)/shard_map/ppermute | solution.py:474

commit v4 on v3

--- a/solution.py
+++ b/solution.py
@@ -57,8 +57,8 @@
 
 
 def pack_kernel(
-    water_h, bed_h, rows_h, blocks_h, inverse_h, down,
-    out, slots, last_out,
+    water_h, bed_h, rows_h, blocks_h, inverse_h, rough_h, east_h, south_h, down,
+    out, slots, last_out, top, bottom,
     water, bed, link_rows, link_blocks, tails, row_s, sems,
 ):
     blocks_own, reach = last_out.shape
@@ -69,6 +69,13 @@
         (bed_h, bed),
         (inverse_h.at[:, reach - 16 : reach, :], tails),
     )
+    height = water.shape[0]
+    for a, field in enumerate((rough_h, east_h, south_h)):
+        rows = pl.ds((a + 2) * HALO, HALO)
+        moves += (
+            (field.at[0:HALO, :], top.at[rows, :]),
+            (field.at[height - HALO : height, :], bottom.at[rows, :]),
+        )
     copies = [pltpu.make_async_copy(src, dst, sems.at[i]) for i, (src, dst) in enumerate(moves)]
     for copy in copies:
         copy.start()
@@ -77,7 +84,6 @@
     rows = link_rows[...]
     blocks = link_blocks[...]
     links = rows.shape[1]
-    height = water.shape[0]
     groups = water.shape[1] // LANES
     tiles = out.shape[0] // CHUNK
     place = ((rows % groups) * height + rows // groups).astype(F32)
@@ -98,6 +104,10 @@
     copies[2].wait()
     copies[3].wait()
     level = water[...] + bed[...]
+    top[0:HALO, :] = level[:HALO]
+    top[HALO : 2 * HALO, :] = bed[0:HALO, :]
+    bottom[0:HALO, :] = level[height - HALO :]
+    bottom[HALO : 2 * HALO, :] = bed[height - HALO : height, :]
     by_block = jnp.concatenate(
         [level[:, c * LANES : (c + 1) * LANES] for c in range(groups)], axis=0
     )
@@ -122,9 +132,11 @@
     row_s[...] = jnp.zeros(row_s.shape, F32)
     row_s[0:1, 0:blocks_own] = down[...].astype(F32)
     out[pl.ds(SLOTS, tiles, CHUNK), :] = ids + (row_s[0:1, :] + gain[0:1, :])
-
-
-def lateral_kernel(rows_in, section, reach_source, last_row, order, out, source):
+    for copy in copies[5:]:
+        copy.wait()
+
+
+def lateral_kernel(rows_in, section, reach_source, last_row, order0, order1, out, source):
     total = rows_in.shape[0]
     tiles = total // CHUNK
     blocks = section.shape[0]
@@ -183,8 +195,7 @@
         downs = jnp.where(here, down, downs)
         gains = jnp.where(here, gain, gains)
     high = jnp.floor(downs * (1.0 / LANES))
-    parts = (high + 1.0, downs - high * LANES, gains)
-    tables = jnp.concatenate([jnp.transpose(x) for x in parts], axis=0).astype(BF16)
+    tables = jnp.concatenate([high + 1.0, downs - high * LANES, gains], axis=0).astype(BF16)
     sources = dense(own, blocks, 0, 1, tiles)
     chunks = sources.shape[0]
     high = jnp.floor(sources * (1.0 / LANES))
@@ -194,17 +205,24 @@
     block_row = iota((LANES, LANES), 0).astype(F32)
     state = [(high[i : i + 1], low[i : i + 1], jnp.ones((1, LANES), F32)) for i in range(chunks)]
     for hop in range(LEVELS - 1):
-        for i, (hi, lo, factor) in enumerate(state):
-            cols = slice(i * LANES, (i + 1) * LANES)
-            hit = block_row == lo
-            mine = jnp.where(hit, jnp.where(hi == me, factor, 0.0), 0.0)
-            reach[:, cols] = mine if hop == 0 else reach[:, cols] + mine
+        for i in range(0, chunks, 2):
+            hits = [block_row == state[k][1] for k in (i, i + 1)]
             if hop < LEVELS - 2:
-                found = mm(tables, (tile_row == hi).astype(F32).astype(BF16))
-                next_hi = jnp.sum(jnp.where(hit, found[:LANES], 0.0), axis=0, keepdims=True)
-                next_lo = jnp.sum(jnp.where(hit, found[LANES : 2 * LANES], 0.0), axis=0, keepdims=True)
-                gain = jnp.sum(jnp.where(hit, found[2 * LANES :], 0.0), axis=0, keepdims=True)
-                state[i] = (next_hi, next_lo, factor * gain)
+                hot = jnp.concatenate([jnp.where(hit, 1.0, 0.0).astype(BF16) for hit in hits], axis=1)
+                founds = mm(tables, hot)
+            for k, hit in zip((i, i + 1), hits):
+                hi, lo, factor = state[k]
+                cols = slice(k * LANES, (k + 1) * LANES)
+                mine = jnp.where(hit, jnp.where(hi == me, factor, 0.0), 0.0)
+                reach[:, cols] = mine if hop == 0 else reach[:, cols] + mine
+                if hop < LEVELS - 2:
+                    found = founds[:, (k - i) * LANES : (k - i + 1) * LANES]
+                    here = tile_row == hi
+                    picks = [
+                        jnp.sum(jnp.where(here, found[p * tiles : (p + 1) * tiles], 0.0), axis=0, keepdims=True)
+                        for p in range(3)
+                    ]
+                    state[k] = (picks[0], picks[1], factor * picks[2])
 
 
 def gather_kernel(returned, reach, out):
@@ -270,6 +288,9 @@
             here = (lane >= off) & (lane < off + 8)
             x = ref[rows, 0:LANES]
             y = ref[rows, width - LANES : width]
+            if ref is f0:
+                x = x + f1[rows, 0:LANES]
+                y = y + f1[rows, width - LANES : width]
             x = pltpu.roll(x, off, 1) if off else x
             y = pltpu.roll(y, (off + 8) % LANES, 1) if (off + 8) % LANES else y
             lefts[v] = jnp.where(here, x, lefts[v])
@@ -289,7 +310,9 @@
     wide = width + LANES
     lane1 = iota((8, LANES), 1)
     scratch = (level_s, bed_s, rough_s, qe_s, qs_s)
+    share = TIME_STEP / CELL_WIDTH
     rate = GRAVITY * TIME_STEP
+    slope_rate = share * rate / CELL_WIDTH
     tile_index, band_index, tile_last, band_last = where[0], where[1], where[2], where[3]
     for a, (field, dst) in enumerate(zip((f0, f1, f2, f3, f4), scratch)):
         for i in range(tiles):
@@ -307,18 +330,21 @@
             y = pltpu.roll(y, (LANES - 8 - off) % LANES, 1) if (LANES - 8 - off) % LANES else y
             edge = jnp.where(lane1 < 8, x, jnp.where(lane1 >= LANES - 8, y, 0.0))
             body = ref[rows, :]
-            if a == 2:
-                body, edge = rate * body, rate * edge
+            if ref is f0:
+                body = body + f1[rows, :]
+            if a >= 2:
+                scale = rate / share if a == 2 else share
+                body, edge = scale * body, scale * edge
             dst[8 * i : 8 * i + 8, :width] = body
             dst[8 * i : 8 * i + 8, width:] = edge
     lane = iota((8, wide), 1)
     sub = iota((8, wide), 0)
     shut_e = ((lane == width - 1) & (tile_index == tile_last)) | ((lane == wide - 1) & (tile_index == 0))
-    ce = jnp.where(shut_e, 0.0, rate / CELL_WIDTH)
+    ce = jnp.where(shut_e, 0.0, slope_rate)
     shut_n = (sub == 7) & (band_index == 0)
     shut_s = (sub == 7) & (band_index == band_last)
-    cs_first = jnp.where(shut_n, 0.0, rate / CELL_WIDTH)
-    cs_last = jnp.where(shut_s, 0.0, rate / CELL_WIDTH)
+    cs_first = jnp.where(shut_n, 0.0, slope_rate)
+    cs_last = jnp.where(shut_s, 0.0, slope_rate)
     nxt = bed_s[0:8, :]
     nxt_up = pltpu.roll(nxt, 7, 0)
     for i in range(tiles):
@@ -335,9 +361,8 @@
 
     def face(here, ahead, bed_max, rough, old, factor):
         depth = jnp.maximum(jnp.maximum(here, ahead) - bed_max, DEPTH_FLOOR)
-        drag = rough * jnp.abs(old) * jnp.exp(-FRICTION_POWER * jnp.log(depth)) + 1.0
+        drag = rough * jnp.abs(old) * jnp.exp2(-FRICTION_POWER * jnp.log2(depth)) + 1.0
         near = pl.reciprocal(drag, approx=True)
-        near = near * (2.0 - drag * near)
         return (old - factor * depth * (ahead - here)) * near
 
     def substep(_, carry):
@@ -351,7 +376,7 @@
                 nxt = level_s[8 * i + 8 : 8 * i + 16, :]
                 nxt_up = pltpu.roll(nxt, 7, 0)
             rough = rough_s[rows, :]
-            cs = cs_first if i == 0 else cs_last if i == tiles - 2 else rate / CELL_WIDTH
+            cs = cs_first if i == 0 else cs_last if i == tiles - 2 else slope_rate
             qe = face(level, pltpu.roll(level, wide - 1, 1), mbe_s[rows, :], rough, qe_s[rows, :], ce)
             below_level = jnp.where(sub == 7, nxt_up, up)
             qs = face(level, below_level, mbs_s[rows, :], rough, qs_s[rows, :], cs)
@@ -361,28 +386,28 @@
             north = jnp.where(sub == 0, north_turned, turned)
             north_turned = turned
             gained = pltpu.roll(qe, 1, 1) - qe + north - qs
-            level_s[rows, :] = level + (TIME_STEP / CELL_WIDTH) * gained
+            level_s[rows, :] = level + gained
         return carry
 
     lax.fori_loop(0, SUBSTEPS, substep, 0)
     inner = slice(HALO, HALO + height)
     water_out[...] = level_s[inner, :width] - bed_s[inner, :width]
-    east_out[...] = qe_s[inner, :width]
-    south_out[...] = qs_s[inner, :width]
+    east_out[...] = (1.0 / share) * qe_s[inner, :width]
+    south_out[...] = (1.0 / share) * qs_s[inner, :width]
 
 
 def shaped(*shape):
     return jax.ShapeDtypeStruct(shape, F32)
 
 
-def call(kernel, out_shape, specs, scratch=(), flops=0, size=0, exps=0):
+def call(kernel, out_shape, specs, scratch=(), flops=0, size=0, exps=0, limit=40 * 1024 * 1024):
     return pl.pallas_call(
         kernel,
         out_shape=out_shape,
         in_specs=specs,
         out_specs=jax.tree.map(lambda _: VMEM, out_shape),
         scratch_shapes=list(scratch),
-        compiler_params=pltpu.CompilerParams(vmem_limit_bytes=40 * 1024 * 1024),
+        compiler_params=pltpu.CompilerParams(vmem_limit_bytes=limit),
         cost_estimate=pl.CostEstimate(flops=flops, bytes_accessed=size, transcendentals=exps),
         name=kernel.__name__,
     )
@@ -406,10 +431,11 @@
     ring = [[(i, (i + k) % bands) for i in range(bands)] for k in range(bands)]
 
     down = block_down.reshape(1, blocks)
-    payload, slots, last_row = call(
+    edge = shaped(5 * HALO, width)
+    payload, slots, last_row, top, bottom = call(
         pack_kernel,
-        (shaped(total, LANES), shaped(8, links), shaped(blocks, reach)),
-        [HBM] * 5 + [VMEM],
+        (shaped(total, LANES), shaped(8, links), shaped(blocks, reach), edge, edge),
+        [HBM] * 8 + [VMEM],
         scratch=[
             pltpu.VMEM((height, width), F32),
             pltpu.VMEM((height, width), F32),
@@ -417,18 +443,27 @@
             pltpu.VMEM((1, links), jnp.int32),
             pltpu.VMEM((blocks, 16, reach), BF16),
             pltpu.VMEM((8, LANES), F32),
-            pltpu.SemaphoreType.DMA((5,)),
+            pltpu.SemaphoreType.DMA((11,)),
         ],
+        limit=None,
         flops=10**9,
         size=10**6,
-    )(water_depth, bed_level, link_rows.reshape(1, links), link_blocks.reshape(1, links), reach_inverse, down)
+    )(
+        water_depth,
+        bed_level,
+        link_rows.reshape(1, links),
+        link_blocks.reshape(1, links),
+        reach_inverse,
+        roughness,
+        flux_east,
+        flux_south,
+        down,
+    )
     rows_in = lax.all_to_all(
         payload.reshape(tiles, CHUNK, 1, LANES), "tile", split_axis=0, concat_axis=0, tiled=True
     )
 
-    fields = (bed_level + water_depth, bed_level, roughness, flux_east, flux_south)
-    top = jnp.concatenate([f[:HALO] for f in fields], axis=0)
-    bottom = jnp.concatenate([f[height - HALO :] for f in fields], axis=0)
+    fields = (water_depth, bed_level, roughness, flux_east, flux_south)
     above = lax.ppermute(bottom, "band", [(i, i + 1) for i in range(bands - 1)])
     below = lax.ppermute(top, "band", [(i + 1, i) for i in range(bands - 1)])
     left, right = call(
@@ -440,10 +475,10 @@
     answer, source = call(
         lateral_kernel,
         (shaped(total, LANES), shaped(blocks, LANES)),
-        [VMEM] * 4 + [ANY],
+        [VMEM] * 4 + [ANY] * 2,
         flops=10**9,
         size=10**6,
-    )(rows_in.reshape(total, LANES), river_section, reach_source, last_row, west)
+    )(rows_in.reshape(total, LANES), river_section, reach_source, last_row, west, east)
     returned = lax.all_to_all(
         answer.reshape(tiles, CHUNK, 1, LANES), "tile", split_axis=0, concat_axis=0, tiled=True
     )
@@ -470,7 +505,7 @@
 
     pushed = call(gather_kernel, shaped(8, LANES), [VMEM] * 2, flops=10**6, size=10**6)(
         returned.reshape(total, LANES), reached
-    )[0:1]
+    )
     parts = [pushed] + [lax.ppermute(pushed, "band", ring[k]) for k in (1, 2, 3)]
     final_depth = call(
         final_kernel, shaped(height, width), [VMEM] * 3, flops=10**9, size=10**6

time: 83.3 us -> 76.8 us (0.922)
  the two profiles are of different devices: /device:TPU:7 before, /device:TPU:2 now
where the time goes in v4:
time: 76.8 us; the launch traced here: 76 us
  starting transfers between devices  46.7 us (61%)
  Pallas kernels  18 us (23%)
  waiting for transfers between devices  9.45 us (12%)
  between operations  0.9 us (1%)
    all_to_all x1, starting transfers between devices, per_device(): lax.all_to_all(answer.reshape(tiles, CHUNK, 1, LANES), 'tile', split_axis...  12.9 us
    all_to_all x1, starting transfers between devices, per_device(): lax.all_to_all(payload.reshape(tiles, CHUNK, 1, LANES), 'tile', split_axi...  12.2 us
    pallas_call x1, Pallas kernels, per_device(): call(flood_kernel, (shaped(height, width),) * 3, [SMEM] + [VMEM] * 9, scr...  6.38 us
    ppermute x3, starting transfers between devices, per_device(): others = [lax.ppermute(extras, 'band', ring[k]) for k in (1, 2, 3)]  5.61 us
    ppermute x3, starting transfers between devices, per_device(): lax.ppermute(pushed, 'band', ring[k])  5.54 us
    ppermute x1, waiting for transfers between devices, per_device(): below = lax.ppermute(top, 'band', [(i + 1, i) for i in range(bands - 1)])  4.36 us
    pallas_call x1, Pallas kernels, per_device(): call(pack_kernel, (shaped(total, LANES), shaped(8, links), shaped(blocks,...  3.84 us
    ppermute x1, starting transfers between devices, per_device(): east = lax.ppermute(left, 'tile', [(i + 1, i) for i in range(tiles - 1)])  3.64 us
  transfers between devices with their start and end apart: 12, of which 5 were waited for; matrix products, arithmetic and copies ran while one was open for 0% of the time, Pallas kernels for 16%

profile of v4, /device:TPU:2, one launch (start us, length us, event | category | flops | bytes accessed | tf_op | source)
XLA Modules:
  0.0 76.0 jit_solution(12426342406891220534)
XLA Ops:
  0.6 3.8 %pack_kernel.1 = (f32[1088,128]{1,0:T(8,128)}, f32[8,512]{1,0:T(8,128)}, f32[32,128]{1,0:T(8,128)}, f32[40,512]{1,0:T(8,128)}, f32[40,512]{1,0:T(8,128)}) custom-call(f32[128,512]{1,0:T(8,128)} %f0.3, f32[128,512]{1,0:T(8,128)} %f1.3, s32[1,512]{1,0:T(1,128)} %bitcast.21, s32[1,512]{1,0:T(1,128)} %bitcast.22, bf16[32,128,128]{2,1,0:T(8,128)(2,1)} %inverse.1, ...), custom_call_target="tpu_custom_call" | custom-call | flops 1000000000 | bytes 1000000 | tf_op jit(solution)/shard_map/pack_kernel/pallas_call | solution.py:435
  4.5 0.0 copy-start.1
  4.5 0.0 copy-start.4
  4.5 12.2 %all-to-all-start = ((f32[64,17,1,128]{3,2,1,0:T(1,128)}), f32[64,17,1,128]{3,2,1,0:T(1,128)S(1)}, u32[]{:S(2)}, u32[]{:S(2)}) async-start(f32[64,17,1,128]{3,2,1,0:T(1,128)} %bitcast.20), calls=%async_computation | async-start | bytes 1114112 | tf_op jit(solution)/shard_map/all_to_all | solution.py:462
  16.7 3.5 %collective-permute-start = (f32[40,512]{1,0:T(8,128)}, f32[40,512]{1,0:T(8,128)S(1)}, u32[]{:S(2)}, u32[]{:S(2)}) collective-permute-start(f32[40,512]{1,0:T(8,128)} %get-tuple-element.18), channel_id=1, source_target_pairs={{0,1},{1,2},{2,3},{4,5},{5,6},{6,7},{8,9},{9,10},{10,11},{12,13},{... | collective-permute-start | bytes 245768 | tf_op jit(solution)/shard_map/ppermute | solution.py:467
  20.2 0.0 copy-start.6
  20.2 1.4 %collective-permute-start.1 = (f32[40,512]{1,0:T(8,128)}, f32[40,512]{1,0:T(8,128)S(1)}, u32[]{:S(2)}, u32[]{:S(2)}) collective-permute-start(f32[40,512]{1,0:T(8,128)} %get-tuple-element.19), channel_id=1, source_target_pairs={{1,0},{2,1},{3,2},{5,4},{6,5},{7,6},{9,8},{10,9},{11,10},{13,12},{... | collective-permute-start | bytes 245768 | tf_op jit(solution)/shard_map/ppermute | solution.py:468
  21.7 0.9 %collective-permute-done.above = f32[40,512]{1,0:T(8,128)S(1)} collective-permute-done((f32[40,512]{1,0:T(8,128)}, f32[40,512]{1,0:T(8,128)S(1)}, u32[]{:S(2)}, u32[]{:S(2)}) %collective-permute-start) | collective-permute-done | bytes 81952 | tf_op jit(solution)/shard_map/ppermute | solution.py:467
  22.5 4.4 %collective-permute-done.1.below = f32[40,512]{1,0:T(8,128)S(1)} collective-permute-done((f32[40,512]{1,0:T(8,128)}, f32[40,512]{1,0:T(8,128)S(1)}, u32[]{:S(2)}, u32[]{:S(2)}) %collective-permute-start.1) | collective-permute-done | bytes 81952 | tf_op jit(solution)/shard_map/ppermute | solution.py:468
  26.9 0.2 strips_kernel.1
  27.2 1.9 %collective-permute-start.2 = (f32[48,128]{1,0:T(8,128)S(1)}, f32[48,128]{1,0:T(8,128)S(1)}, u32[]{:S(2)}, u32[]{:S(2)}) collective-permute-start(f32[48,128]{1,0:T(8,128)S(1)} %get-tuple-element.20), channel_id=1, source_target_pairs={{0,4},{4,8},{8,12},{12,16},{16,20},{20,24},{24,28},{28,32},{32,36}... | collective-permute-start | bytes 73736 | tf_op jit(solution)/shard_map/ppermute | solution.py:472
  29.1 3.6 %collective-permute-start.3 = (f32[48,128]{1,0:T(8,128)S(1)}, f32[48,128]{1,0:T(8,128)S(1)}, u32[]{:S(2)}, u32[]{:S(2)}) collective-permute-start(f32[48,128]{1,0:T(8,128)S(1)} %get-tuple-element.21), channel_id=1, source_target_pairs={{4,0},{8,4},{12,8},{16,12},{20,16},{24,20},{28,24},{32,28},{36,32}... | collective-permute-start | bytes 73736 | tf_op jit(solution)/shard_map/ppermute | solution.py:473
  32.8 1.5 %collective-permute-done.3.east.order1 = f32[48,128]{1,0:T(8,128)S(1)} collective-permute-done((f32[48,128]{1,0:T(8,128)S(1)}, f32[48,128]{1,0:T(8,128)S(1)}, u32[]{:S(2)}, u32[]{:S(2)}) %collective-permute-start.3) | collective-permute-done | bytes 24608 | tf_op jit(solution)/shard_map/ppermute | solution.py:473
  34.3 0.7 all-to-all-done
  35.0 1.9 %lateral_kernel.1 = (f32[1088,128]{1,0:T(8,128)}, f32[32,128]{1,0:T(8,128)S(1)}) custom-call(f32[1088,128]{1,0:T(8,128)S(1)} %bitcast.18, f32[32,128]{1,0:T(8,128)S(1)} %copy-done.6, f32[32,128]{1,0:T(8,128)S(1)} %copy-done.7, f32[32,128]{1,0:T(8,128)S(1)} %copy-done.9, f32[48,128]{1,0:T(8,128)S(1)} %collective-permute-done.2.west.order0, ...), custom_call_target="tpu_custom_call" | custom-call | flops 1000000000 | bytes 1000000 | tf_op jit(solution)/shard_map/lateral_kernel/pallas_call | solution.py:475
  36.8 12.9 %all-to-all-start.1 = ((f32[64,17,1,128]{3,2,1,0:T(1,128)}), f32[64,17,1,128]{3,2,1,0:T(1,128)S(1)}, u32[]{:S(2)}, u32[]{:S(2)}) async-start(f32[64,17,1,128]{3,2,1,0:T(1,128)} %bitcast.7), calls=%async_computation.1 | async-start | bytes 1114112 | tf_op jit(solution)/shard_map/all_to_all | solution.py:482
  49.7 0.1 copy.24
  49.8 1.7 %collective-permute-start.4 = (f32[64,128]{1,0:T(8,128)S(1)}, f32[64,128]{1,0:T(8,128)S(1)}, u32[]{:S(2)}, u32[]{:S(2)}) collective-permute-start(f32[64,128]{1,0:T(8,128)S(1)} %slice_bitcast_fusion.own), channel_id=1, source_target_pairs={{0,1},{1,2},{2,3},{3,0},{4,5},{5,6},{6,7},{7,4},{8,9},{9,10},{10,1... | collective-permute-start | bytes 98312 | tf_op jit(solution)/shard_map/ppermute | solution.py:501
  51.4 1.4 %collective-permute-start.5 = (f32[64,128]{1,0:T(8,128)S(1)}, f32[64,128]{1,0:T(8,128)S(1)}, u32[]{:S(2)}, u32[]{:S(2)}) collective-permute-start(f32[64,128]{1,0:T(8,128)S(1)} %slice_bitcast_fusion.own), channel_id=1, source_target_pairs={{0,2},{1,3},{2,0},{3,1},{4,6},{5,7},{6,4},{7,5},{8,10},{9,11},{10,... | collective-permute-start | bytes 98312 | tf_op jit(solution)/shard_map/ppermute | solution.py:501
  52.9 2.5 %collective-permute-start.6 = (f32[64,128]{1,0:T(8,128)S(1)}, f32[64,128]{1,0:T(8,128)S(1)}, u32[]{:S(2)}, u32[]{:S(2)}) collective-permute-start(f32[64,128]{1,0:T(8,128)S(1)} %slice_bitcast_fusion.own), channel_id=1, source_target_pairs={{0,3},{1,0},{2,1},{3,2},{4,7},{5,4},{6,5},{7,6},{8,11},{9,8},{10,9... | collective-permute-start | bytes 98312 | tf_op jit(solution)/shard_map/ppermute | solution.py:501
  55.4 0.1 pad_add_fusion.where
  55.5 6.4 %flood_kernel.1 = (f32[128,512]{1,0:T(8,128)S(1)}, f32[128,512]{1,0:T(8,128)}, f32[128,512]{1,0:T(8,128)}) custom-call(s32[4]{0:T(128)S(1)} %pad_add_fusion.where, f32[40,512]{1,0:T(8,128)S(1)} %collective-permute-done.above, f32[40,512]{1,0:T(8,128)S(1)} %collective-permute-done.1.below, f32[48,128]{1,0:T(8,128)S(1)} %collective-permute-done.2.west.order0, ...), custom_call_target="tpu_custom_call" | custom-call | flops 100000000 | bytes 10000000 | tf_op jit(solution)/shard_map/flood_kernel/pallas_call | solution.py:488
  61.9 0.8 %flow_kernel.1 = (f32[32,128]{1,0:T(8,128)S(1)}, f32[32,128]{1,0:T(8,128)S(1)}) custom-call(f32[32,128]{1,0:T(8,128)S(1)} %get-tuple-element.29.source, bf16[32,128,128]{2,1,0:T(8,128)(2,1)S(1)} %copy-done), custom_call_target="tpu_custom_call" | custom-call | flops 100000000 | bytes 1000000 | tf_op jit(solution)/shard_map/flow_kernel/pallas_call | solution.py:497
  62.7 3.3 %paths_kernel.1.reach = f32[128,2048]{1,0:T(8,128)S(1)} custom-call(s32[4]{0:T(128)S(1)} %pad_add_fusion.where, f32[64,128]{1,0:T(8,128)S(1)} %slice_bitcast_fusion.own, f32[64,128]{1,0:T(8,128)S(1)} %collective-permute-done.4.one, f32[64,128]{1,0:T(8,128)S(1)} %collective-permute-done.5.two, f32[64,128]{1,0:T(8,128)S(1)} %collective-permute-done.6.three), custom_call_target="tpu_custom_call" | custom-call | flops 1000000000 | bytes 1000000 | tf_op jit(solution)/shard_map/paths_kernel/pallas_call | solution.py:502
  66.0 2.0 %all-to-all-done.1 = f32[64,17,1,128]{3,2,1,0:T(1,128)S(1)} async-done(((f32[64,17,1,128]{3,2,1,0:T(1,128)}), f32[64,17,1,128]{3,2,1,0:T(1,128)S(1)}, u32[]{:S(2)}, u32[]{:S(2)}) %all-to-all-start.1) | async-done | bytes 557088 | tf_op jit(solution)/shard_map/all_to_all | solution.py:482
  68.0 0.3 gather_kernel.1
  68.2 1.6 %collective-permute-start.7 = (f32[8,128]{1,0:T(8,128)S(1)}, f32[8,128]{1,0:T(8,128)S(1)}, u32[]{:S(2)}, u32[]{:S(2)}) collective-permute-start(f32[8,128]{1,0:T(8,128)S(1)} %gather_kernel.1), channel_id=1, source_target_pairs={{0,1},{1,2},{2,3},{3,0},{4,5},{5,6},{6,7},{7,4},{8,9},{9,10},{10,1... | collective-permute-start | bytes 12296 | tf_op jit(solution)/shard_map/ppermute | solution.py:509
  69.8 1.4 %collective-permute-start.8 = (f32[8,128]{1,0:T(8,128)S(1)}, f32[8,128]{1,0:T(8,128)S(1)}, u32[]{:S(2)}, u32[]{:S(2)}) collective-permute-start(f32[8,128]{1,0:T(8,128)S(1)} %gather_kernel.1), channel_id=1, source_target_pairs={{0,2},{1,3},{2,0},{3,1},{4,6},{5,7},{6,4},{7,5},{8,10},{9,11},{10,... | collective-permute-start | bytes 12296 | tf_op jit(solution)/shard_map/ppermute | solution.py:509
  71.2 2.6 %collective-permute-start.9 = (f32[8,128]{1,0:T(8,128)S(1)}, f32[8,128]{1,0:T(8,128)S(1)}, u32[]{:S(2)}, u32[]{:S(2)}) collective-permute-start(f32[8,128]{1,0:T(8,128)S(1)} %gather_kernel.1), channel_id=1, source_target_pairs={{0,3},{1,0},{2,1},{3,2},{4,7},{5,4},{6,5},{7,6},{8,11},{9,8},{10,9... | collective-permute-start | bytes 12296 | tf_op jit(solution)/shard_map/ppermute | solution.py:509
  73.8 1.4 %final_kernel.1 = f32[128,512]{1,0:T(8,128)} custom-call(f32[128,512]{1,0:T(8,128)S(1)} %get-tuple-element.22.water, f32[1088,128]{1,0:T(8,128)S(1)} %bitcast.17, f32[8,512]{1,0:T(8,128)S(1)} %copy-done.8), custom_call_target="tpu_custom_call" | custom-call | flops 1000000000 | bytes 1000000 | tf_op jit(solution)/shard_map/final_kernel/pallas_call | solution.py:510
  75.2 0.1 dynamic-slice_bitcast_fusion
  75.3 0.7 multiply_add_fusion
  (27 shorter events, 0.1 us)
Async XLA Ops:
  0.6 26.3 %copy-start.5 = (f32[128,512]{1,0:T(8,128)S(1)}, f32[128,512]{1,0:T(8,128)}, u32[]{:S(2)}) copy-start(f32[128,512]{1,0:T(8,128)} %f4.3) | copy-start | bytes 786436
  4.5 22.4 %copy-start.1 = (f32[128,512]{1,0:T(8,128)S(1)}, f32[128,512]{1,0:T(8,128)}, u32[]{:S(2)}) copy-start(f32[128,512]{1,0:T(8,128)} %f0.3) | copy-start | bytes 786436
  4.5 22.4 %copy-start.2 = (f32[128,512]{1,0:T(8,128)S(1)}, f32[128,512]{1,0:T(8,128)}, u32[]{:S(2)}) copy-start(f32[128,512]{1,0:T(8,128)} %f1.3) | copy-start | bytes 786436
  4.5 22.4 %copy-start.3 = (f32[128,512]{1,0:T(8,128)S(1)}, f32[128,512]{1,0:T(8,128)}, u32[]{:S(2)}) copy-start(f32[128,512]{1,0:T(8,128)} %f2.3) | copy-start | bytes 786436
  4.5 22.4 %copy-start.4 = (f32[128,512]{1,0:T(8,128)S(1)}, f32[128,512]{1,0:T(8,128)}, u32[]{:S(2)}) copy-start(f32[128,512]{1,0:T(8,128)} %f3.3) | copy-start | bytes 786436
  4.5 30.4 %all-to-all-start = ((f32[64,17,1,128]{3,2,1,0:T(1,128)}), f32[64,17,1,128]{3,2,1,0:T(1,128)S(1)}, u32[]{:S(2)}, u32[]{:S(2)}) async-start(f32[64,17,1,128]{3,2,1,0:T(1,128)} %bitcast.20), calls=%async_computation | async-start | bytes 1114112 | tf_op jit(solution)/shard_map/all_to_all | solution.py:462
  16.7 5.8 %collective-permute-start = (f32[40,512]{1,0:T(8,128)}, f32[40,512]{1,0:T(8,128)S(1)}, u32[]{:S(2)}, u32[]{:S(2)}) collective-permute-start(f32[40,512]{1,0:T(8,128)} %get-tuple-element.18), channel_id=1, source_target_pairs={{0,1},{1,2},{2,3},{4,5},{5,6},{6,7},{8,9},{9,10},{10,11},{12,13},{... | collective-permute-start | bytes 245768 | tf_op jit(solution)/shard_map/ppermute | solution.py:467
  20.2 14.8 %copy-start.6 = (f32[32,128]{1,0:T(8,128)S(1)}, f32[32,128]{1,0:T(8,128)}, u32[]{:S(2)}) copy-start(f32[32,128]{1,0:T(8,128)} %section.1) | copy-start | bytes 49156
  20.2 14.8 %copy-start.7 = (f32[32,128]{1,0:T(8,128)S(1)}, f32[32,128]{1,0:T(8,128)}, u32[]{:S(2)}) copy-start(f32[32,128]{1,0:T(8,128)} %reach_source.1) | copy-start | bytes 49156
  20.2 14.8 %copy-start.9 = (f32[32,128]{1,0:T(8,128)S(1)}, f32[32,128]{1,0:T(8,128)}, u32[]{:S(2)}) copy-start(f32[32,128]{1,0:T(8,128)} %get-tuple-element.24.last_row) | copy-start | bytes 49156
  20.2 6.7 %collective-permute-start.1 = (f32[40,512]{1,0:T(8,128)}, f32[40,512]{1,0:T(8,128)S(1)}, u32[]{:S(2)}, u32[]{:S(2)}) collective-permute-start(f32[40,512]{1,0:T(8,128)} %get-tuple-element.19), channel_id=1, source_target_pairs={{1,0},{2,1},{3,2},{5,4},{6,5},{7,6},{9,8},{10,9},{11,10},{13,12},{... | collective-permute-start | bytes 245768 | tf_op jit(solution)/shard_map/ppermute | solution.py:468
  27.2 5.6 %collective-permute-start.2 = (f32[48,128]{1,0:T(8,128)S(1)}, f32[48,128]{1,0:T(8,128)S(1)}, u32[]{:S(2)}, u32[]{:S(2)}) collective-permute-start(f32[48,128]{1,0:T(8,128)S(1)} %get-tuple-element.20), channel_id=1, source_target_pairs={{0,4},{4,8},{8,12},{12,16},{16,20},{20,24},{24,28},{28,32},{32,36}... | collective-permute-start | bytes 73736 | tf_op jit(solution)/shard_map/ppermute | solution.py:472
  29.1 5.1 %collective-permute-start.3 = (f32[48,128]{1,0:T(8,128)S(1)}, f32[48,128]{1,0:T(8,128)S(1)}, u32[]{:S(2)}, u32[]{:S(2)}) collective-permute-start(f32[48,128]{1,0:T(8,128)S(1)} %get-tuple-element.21), channel_id=1, source_target_pairs={{4,0},{8,4},{12,8},{16,12},{20,16},{24,20},{28,24},{32,28},{36,32}... | collective-permute-start | bytes 73736 | tf_op jit(solution)/shard_map/ppermute | solution.py:473
  36.8 31.1 %all-to-all-start.1 = ((f32[64,17,1,128]{3,2,1,0:T(1,128)}), f32[64,17,1,128]{3,2,1,0:T(1,128)S(1)}, u32[]{:S(2)}, u32[]{:S(2)}) async-start(f32[64,17,1,128]{3,2,1,0:T(1,128)} %bitcast.7), calls=%async_computation.1 | async-start | bytes 1114112 | tf_op jit(solution)/shard_map/all_to_all | solution.py:482
  49.8 12.9 %collective-permute-start.4 = (f32[64,128]{1,0:T(8,128)S(1)}, f32[64,128]{1,0:T(8,128)S(1)}, u32[]{:S(2)}, u32[]{:S(2)}) collective-permute-start(f32[64,128]{1,0:T(8,128)S(1)} %slice_bitcast_fusion.own), channel_id=1, source_target_pairs={{0,1},{1,2},{2,3},{3,0},{4,5},{5,6},{6,7},{7,4},{8,9},{9,10},{10,1... | collective-permute-start | bytes 98312 | tf_op jit(solution)/shard_map/ppermute | solution.py:501
  51.4 11.2 %collective-permute-start.5 = (f32[64,128]{1,0:T(8,128)S(1)}, f32[64,128]{1,0:T(8,128)S(1)}, u32[]{:S(2)}, u32[]{:S(2)}) collective-permute-start(f32[64,128]{1,0:T(8,128)S(1)} %slice_bitcast_fusion.own), channel_id=1, source_target_pairs={{0,2},{1,3},{2,0},{3,1},{4,6},{5,7},{6,4},{7,5},{8,10},{9,11},{10,... | collective-permute-start | bytes 98312 | tf_op jit(solution)/shard_map/ppermute | solution.py:501
  52.9 9.8 %collective-permute-start.6 = (f32[64,128]{1,0:T(8,128)S(1)}, f32[64,128]{1,0:T(8,128)S(1)}, u32[]{:S(2)}, u32[]{:S(2)}) collective-permute-start(f32[64,128]{1,0:T(8,128)S(1)} %slice_bitcast_fusion.own), channel_id=1, source_target_pairs={{0,3},{1,0},{2,1},{3,2},{4,7},{5,4},{6,5},{7,6},{8,11},{9,8},{10,9... | collective-permute-start | bytes 98312 | tf_op jit(solution)/shard_map/ppermute | solution.py:501
  55.5 6.4 %copy-start = (bf16[32,128,128]{2,1,0:T(8,128)(2,1)S(1)}, bf16[32,128,128]{2,1,0:T(8,128)(2,1)}, u32[]{:S(2)}) copy-start(bf16[32,128,128]{2,1,0:T(8,128)(2,1)} %inverse.1) | copy-start | bytes 3145732
  68.0 5.8 %copy-start.8 = (f32[8,512]{1,0:T(8,128)S(1)}, f32[8,512]{1,0:T(8,128)}, u32[]{:S(2)}) copy-start(f32[8,512]{1,0:T(8,128)} %get-tuple-element.26.slots) | copy-start | bytes 49156
  68.2 7.0 %collective-permute-start.7 = (f32[8,128]{1,0:T(8,128)S(1)}, f32[8,128]{1,0:T(8,128)S(1)}, u32[]{:S(2)}, u32[]{:S(2)}) collective-permute-start(f32[8,128]{1,0:T(8,128)S(1)} %gather_kernel.1), channel_id=1, source_target_pairs={{0,1},{1,2},{2,3},{3,0},{4,5},{5,6},{6,7},{7,4},{8,9},{9,10},{10,1... | collective-permute-start | bytes 12296 | tf_op jit(solution)/shard_map/ppermute | solution.py:509
  69.8 5.4 %collective-permute-start.8 = (f32[8,128]{1,0:T(8,128)S(1)}, f32[8,128]{1,0:T(8,128)S(1)}, u32[]{:S(2)}, u32[]{:S(2)}) collective-permute-start(f32[8,128]{1,0:T(8,128)S(1)} %gather_kernel.1), channel_id=1, source_target_pairs={{0,2},{1,3},{2,0},{3,1},{4,6},{5,7},{6,4},{7,5},{8,10},{9,11},{10,... | collective-permute-start | bytes 12296 | tf_op jit(solution)/shard_map/ppermute | solution.py:509
  71.2 4.0 %collective-permute-start.9 = (f32[8,128]{1,0:T(8,128)S(1)}, f32[8,128]{1,0:T(8,128)S(1)}, u32[]{:S(2)}, u32[]{:S(2)}) collective-permute-start(f32[8,128]{1,0:T(8,128)S(1)} %gather_kernel.1), channel_id=1, source_target_pairs={{0,3},{1,0},{2,1},{3,2},{4,7},{5,4},{6,5},{7,6},{8,11},{9,8},{10,9... | collective-permute-start | bytes 12296 | tf_op jit(solution)/shard_map/ppermute | solution.py:509

commit v5 on v4

--- a/solution.py
+++ b/solution.py
@@ -58,7 +58,7 @@
 
 def pack_kernel(
     water_h, bed_h, rows_h, blocks_h, inverse_h, rough_h, east_h, south_h, down,
-    out, slots, last_out, top, bottom,
+    out, slots, last_out, edge_a, edge_b,
     water, bed, link_rows, link_blocks, tails, row_s, sems,
 ):
     blocks_own, reach = last_out.shape
@@ -70,11 +70,14 @@
         (inverse_h.at[:, reach - 16 : reach, :], tails),
     )
     height = water.shape[0]
+    odd = lax.axis_index("band") % 2
+    start_a = pl.multiple_of((1 - odd) * (height - HALO), HALO)
+    start_b = pl.multiple_of(odd * (height - HALO), HALO)
     for a, field in enumerate((rough_h, east_h, south_h)):
         rows = pl.ds((a + 2) * HALO, HALO)
         moves += (
-            (field.at[0:HALO, :], top.at[rows, :]),
-            (field.at[height - HALO : height, :], bottom.at[rows, :]),
+            (field.at[pl.ds(start_a, HALO), :], edge_a.at[rows, :]),
+            (field.at[pl.ds(start_b, HALO), :], edge_b.at[rows, :]),
         )
     copies = [pltpu.make_async_copy(src, dst, sems.at[i]) for i, (src, dst) in enumerate(moves)]
     for copy in copies:
@@ -104,18 +107,15 @@
     copies[2].wait()
     copies[3].wait()
     level = water[...] + bed[...]
-    top[0:HALO, :] = level[:HALO]
-    top[HALO : 2 * HALO, :] = bed[0:HALO, :]
-    bottom[0:HALO, :] = level[height - HALO :]
-    bottom[HALO : 2 * HALO, :] = bed[height - HALO : height, :]
+    for edge, start in ((edge_a, start_a), (edge_b, start_b)):
+        edge[HALO : 2 * HALO, :] = bed[pl.ds(start, HALO), :]
+        edge[0:HALO, :] = water[pl.ds(start, HALO), :] + bed[pl.ds(start, HALO), :]
     by_block = jnp.concatenate(
         [level[:, c * LANES : (c + 1) * LANES] for c in range(groups)], axis=0
     )
     by_block = paired(by_block)
-    step = 8 * CHUNK
-    for start in range(0, out.shape[0], step):
-        hot = (iota((step, links), 0) + start).astype(F32) == slot_of
-        out[start : start + step, :] = fold(mm(hot.astype(F32).astype(BF16), by_block))
+    hot = iota((out.shape[0], links), 0).astype(F32) == slot_of
+    out[...] = fold(mm(jnp.where(hot, 1.0, 0.0).astype(BF16), by_block))
     dest_hot = (iota((tiles, links), 0).astype(F32) == dest).astype(F32).astype(BF16)
     seat = iota((links, LANES), 1).astype(F32) - float(ID_LANE)
     rank_hot = jnp.where(rank == seat, local_c + 1.0, 0.0)
@@ -185,7 +185,7 @@
     downs = jnp.zeros((tiles, LANES), F32)
     gains = jnp.zeros((tiles, LANES), F32)
     for back, ref in enumerate((own, one, two, three)):
-        here = group == (band + bands - back) % bands
+        here = group == band ^ back
         x = ref[...]
         down, gain = x, x
         for turn in (1, 2, 3):
@@ -259,49 +259,49 @@
     groups = water.shape[1] // LANES
     slot_c = jnp.transpose(slots[...])[:, 0:1]
     rows = paired(returned[...])
+    hot = iota((height * groups, total), 1).astype(F32) == slot_c
+    lateral = fold(mm(jnp.where(hot, 1.0, 0.0).astype(BF16), rows))
     for c in range(groups):
-        mine = slot_c[c * height : (c + 1) * height]
-        hot = (iota((height, total), 1).astype(F32) == mine).astype(F32).astype(BF16)
-        lateral = fold(mm(hot, rows))
         cols = slice(c * LANES, (c + 1) * LANES)
-        out[:, cols] = water[:, cols] - PLAIN_SHARE * lateral
-
-
-def strips_kernel(above, below, f0, f1, f2, f3, f4, left, right):
+        out[:, cols] = water[:, cols] - PLAIN_SHARE * lateral[c * height : (c + 1) * height]
+
+
+def strips_kernel(where, got_a, got_b, f0, f1, f2, f3, f4, side_a, side_b):
     fields = (f0, f1, f2, f3, f4)
     height, width = f0.shape
     tiles = height // 8 + 2
     lane = iota((8, LANES), 1)
-    groups = left.shape[0] // 8
+    groups = side_a.shape[0] // 8
+    odd_band, odd_tile = where[1] % 2 == 1, where[0] % 2 == 1
     lefts = [jnp.zeros((8, LANES), F32) for _ in range(groups)]
     rights = [jnp.zeros((8, LANES), F32) for _ in range(groups)]
     for a, field in enumerate(fields):
         for i in range(tiles):
-            if i == 0:
-                ref, rows = above, slice(a * HALO, a * HALO + 8)
-            elif i == tiles - 1:
-                ref, rows = below, slice(a * HALO, a * HALO + 8)
-            else:
-                ref, rows = field, slice(8 * i - 8, 8 * i)
             strip = a * tiles + i
             v, off = strip // 16, (strip % 16) * 8
             here = (lane >= off) & (lane < off + 8)
-            x = ref[rows, 0:LANES]
-            y = ref[rows, width - LANES : width]
-            if ref is f0:
-                x = x + f1[rows, 0:LANES]
-                y = y + f1[rows, width - LANES : width]
+            first, last = slice(0, LANES), slice(width - LANES, width)
+            if i in (0, tiles - 1):
+                rows = slice(a * HALO, a * HALO + 8)
+                from_a = odd_band if i == 0 else jnp.logical_not(odd_band)
+                x = jnp.where(from_a, got_a[rows, first], got_b[rows, first])
+                y = jnp.where(from_a, got_a[rows, last], got_b[rows, last])
+            else:
+                rows = slice(8 * i - 8, 8 * i)
+                x, y = field[rows, first], field[rows, last]
+                if a == 0:
+                    x, y = x + f1[rows, first], y + f1[rows, last]
             x = pltpu.roll(x, off, 1) if off else x
             y = pltpu.roll(y, (off + 8) % LANES, 1) if (off + 8) % LANES else y
             lefts[v] = jnp.where(here, x, lefts[v])
             rights[v] = jnp.where(here, y, rights[v])
     for v in range(groups):
-        left[8 * v : 8 * v + 8, :] = lefts[v]
-        right[8 * v : 8 * v + 8, :] = rights[v]
+        side_a[8 * v : 8 * v + 8, :] = jnp.where(odd_tile, lefts[v], rights[v])
+        side_b[8 * v : 8 * v + 8, :] = jnp.where(odd_tile, rights[v], lefts[v])
 
 
 def flood_kernel(
-    where, above, below, west, east, f0, f1, f2, f3, f4,
+    where, got_a, got_b, col_a, col_b, f0, f1, f2, f3, f4,
     water_out, east_out, south_out,
     level_s, bed_s, rough_s, qe_s, qs_s, mbe_s, mbs_s,
 ):
@@ -314,24 +314,29 @@
     rate = GRAVITY * TIME_STEP
     slope_rate = share * rate / CELL_WIDTH
     tile_index, band_index, tile_last, band_last = where[0], where[1], where[2], where[3]
+    odd_band, odd_tile = band_index % 2 == 1, tile_index % 2 == 1
+    easts, wests = [], []
+    for v in range(col_a.shape[0] // 8):
+        x, y = col_a[8 * v : 8 * v + 8, :], col_b[8 * v : 8 * v + 8, :]
+        easts.append(jnp.where(odd_tile, y, x))
+        wests.append(jnp.where(odd_tile, x, y))
     for a, (field, dst) in enumerate(zip((f0, f1, f2, f3, f4), scratch)):
         for i in range(tiles):
-            if i == 0:
-                ref, rows = above, slice(a * HALO, a * HALO + 8)
-            elif i == tiles - 1:
-                ref, rows = below, slice(a * HALO, a * HALO + 8)
-            else:
-                ref, rows = field, slice(8 * i - 8, 8 * i)
             strip = a * tiles + i
             v, off = strip // 16, (strip % 16) * 8
-            x = east[8 * v : 8 * v + 8, :]
-            y = west[8 * v : 8 * v + 8, :]
+            x, y = easts[v], wests[v]
             x = pltpu.roll(x, LANES - off, 1) if off else x
             y = pltpu.roll(y, (LANES - 8 - off) % LANES, 1) if (LANES - 8 - off) % LANES else y
             edge = jnp.where(lane1 < 8, x, jnp.where(lane1 >= LANES - 8, y, 0.0))
-            body = ref[rows, :]
-            if ref is f0:
-                body = body + f1[rows, :]
+            if i in (0, tiles - 1):
+                rows = slice(a * HALO, a * HALO + 8)
+                from_a = odd_band if i == 0 else jnp.logical_not(odd_band)
+                body = jnp.where(from_a, got_a[rows, :], got_b[rows, :])
+            else:
+                rows = slice(8 * i - 8, 8 * i)
+                body = field[rows, :]
+                if a == 0:
+                    body = body + f1[rows, :]
             if a >= 2:
                 scale = rate / share if a == 2 else share
                 body, edge = scale * body, scale * edge
@@ -428,11 +433,11 @@
     where = jnp.stack(
         [tile_index, band_index, jnp.int32(tiles - 1), jnp.int32(bands - 1)]
     ).astype(jnp.int32)
-    ring = [[(i, (i + k) % bands) for i in range(bands)] for k in range(bands)]
+    ring = [[(i, i ^ k) for i in range(bands)] for k in range(bands)]
 
     down = block_down.reshape(1, blocks)
     edge = shaped(5 * HALO, width)
-    payload, slots, last_row, top, bottom = call(
+    payload, slots, last_row, edge_a, edge_b = call(
         pack_kernel,
         (shaped(total, LANES), shaped(8, links), shaped(blocks, reach), edge, edge),
         [HBM] * 8 + [VMEM],
@@ -464,13 +469,16 @@
     )
 
     fields = (water_depth, bed_level, roughness, flux_east, flux_south)
-    above = lax.ppermute(bottom, "band", [(i, i + 1) for i in range(bands - 1)])
-    below = lax.ppermute(top, "band", [(i + 1, i) for i in range(bands - 1)])
-    left, right = call(
-        strips_kernel, (shaped(48, LANES), shaped(48, LANES)), [VMEM] * 7, flops=10**6, size=10**6
-    )(above, below, *fields)
-    west = lax.ppermute(right, "tile", [(i, i + 1) for i in range(tiles - 1)])
-    east = lax.ppermute(left, "tile", [(i + 1, i) for i in range(tiles - 1)])
+    def pairs(count, first):
+        return [(j, i) for k in range(first, count - 1, 2) for i, j in ((k, k + 1), (k + 1, k))]
+
+    got_a = lax.ppermute(edge_a, "band", pairs(bands, 0))
+    got_b = lax.ppermute(edge_b, "band", pairs(bands, 1))
+    side_a, side_b = call(
+        strips_kernel, (shaped(48, LANES), shaped(48, LANES)), [SMEM] + [VMEM] * 7, flops=10**6, size=10**6
+    )(where, got_a, got_b, *fields)
+    col_a = lax.ppermute(side_a, "tile", pairs(tiles, 0))
+    col_b = lax.ppermute(side_b, "tile", pairs(tiles, 1))
 
     answer, source = call(
         lateral_kernel,
@@ -478,7 +486,7 @@
         [VMEM] * 4 + [ANY] * 2,
         flops=10**9,
         size=10**6,
-    )(rows_in.reshape(total, LANES), river_section, reach_source, last_row, west, east)
+    )(rows_in.reshape(total, LANES), river_section, reach_source, last_row, col_a, col_b)
     returned = lax.all_to_all(
         answer.reshape(tiles, CHUNK, 1, LANES), "tile", split_axis=0, concat_axis=0, tiled=True
     )
@@ -493,7 +501,7 @@
         flops=10**8,
         size=10**7,
         exps=10**7,
-    )(where, above, below, west, east, *fields)
+    )(where, got_a, got_b, col_a, col_b, *fields)
     base_flow, column = call(
         flow_kernel, (shaped(blocks, reach),) * 2, [VMEM] * 2, flops=10**8, size=10**6
     )(source, reach_inverse)

time: 76.8 us -> 72.5 us (0.944)
  starting transfers between devices: 46.7 us -> 34.9 us
  waiting for transfers between devices: 9.45 us -> 16.9 us
    all_to_all x1, starting transfers between devices: 12.9 us -> 5.98 us  [per_device(): lax.all_to_all(answer.reshape(tiles, CHUNK, 1, LANES), 'tile', split_axis...]
    all_to_all x1, waiting for transfers between devices: 0.7 us -> 7.17 us  [per_device(): lax.all_to_all(payload.reshape(tiles, CHUNK, 1, LANES), 'tile', split_axi...]
    ppermute x4, starting transfers between devices: 10.5 us -> 4.81 us  [the longest x1 2.4 us: per_device(): col_b = lax.ppermute(side_b, 'tile', pairs(tiles, 1))]
    ppermute x3, waiting for transfers between devices: 0.01 us -> 2.65 us  [per_device(): lax.ppermute(pushed, 'band', ring[k])]
    ppermute x4, waiting for transfers between devices: 6.73 us -> 5.34 us  [the longest x1 2.95 us: per_device(): col_b = lax.ppermute(side_b, 'tile', pairs(tiles, 1))]
  transfers between devices with their start and end apart: 12 -> 12, of which waited for: 5 -> 6; matrix products, arithmetic and copies ran while one was open for 0% -> 0% of each run, Pallas kernels for 16% -> 18%
where the time goes in v5:
time: 72.5 us; the launch traced here: 72.2 us
  starting transfers between devices  34.9 us (48%)
  Pallas kernels  18.6 us (26%)
  waiting for transfers between devices  16.9 us (23%)
  between operations  0.86 us (1%)
  other arithmetic  0.76 us (1%)
    all_to_all x1, starting transfers between devices, per_device(): lax.all_to_all(payload.reshape(tiles, CHUNK, 1, LANES), 'tile', split_axi...  12.2 us
    all_to_all x1, waiting for transfers between devices, per_device(): lax.all_to_all(payload.reshape(tiles, CHUNK, 1, LANES), 'tile', split_axi...  7.17 us
    pallas_call x1, Pallas kernels, per_device(): call(flood_kernel, (shaped(height, width),) * 3, [SMEM] + [VMEM] * 9, scr...  6.37 us
    ppermute x3, starting transfers between devices, per_device(): others = [lax.ppermute(extras, 'band', ring[k]) for k in (1, 2, 3)]  6.01 us
    all_to_all x1, starting transfers between devices, per_device(): lax.all_to_all(answer.reshape(tiles, CHUNK, 1, LANES), 'tile', split_axis...  5.98 us
    ppermute x3, starting transfers between devices, per_device(): lax.ppermute(pushed, 'band', ring[k])  5.9 us
    pallas_call x1, Pallas kernels, per_device(): call(pack_kernel, (shaped(total, LANES), shaped(8, links), shaped(blocks,...  3.85 us
    pallas_call x1, Pallas kernels, per_device(): call(paths_kernel, shaped(LANES, tiles * blocks), [SMEM] + [VMEM] * 4, fl...  3.25 us
  transfers between devices with their start and end apart: 12, of which 6 were waited for; matrix products, arithmetic and copies ran while one was open for 0% of the time, Pallas kernels for 18%

profile of v5, /device:TPU:2, one launch (start us, length us, event | category | flops | bytes accessed | tf_op | source)
XLA Modules:
  0.0 72.2 jit_solution(1564758140796762619)
XLA Ops:
  0.6 3.9 %pack_kernel.1 = (f32[1088,128]{1,0:T(8,128)}, f32[8,512]{1,0:T(8,128)}, f32[32,128]{1,0:T(8,128)}, f32[40,512]{1,0:T(8,128)}, f32[40,512]{1,0:T(8,128)}) custom-call(f32[128,512]{1,0:T(8,128)} %f0.3, f32[128,512]{1,0:T(8,128)} %f1.3, s32[1,512]{1,0:T(1,128)} %bitcast.21, s32[1,512]{1,0:T(1,128)} %bitcast.22, bf16[32,128,128]{2,1,0:T(8,128)(2,1)} %inverse.1, ...), custom_call_target="tpu_custom_call" | custom-call | flops 1000000000 | bytes 1000000 | tf_op jit(solution)/shard_map/pack_kernel/pallas_call | solution.py:440
  4.5 0.0 copy-start.2
  4.5 12.2 %all-to-all-start = ((f32[64,17,1,128]{3,2,1,0:T(1,128)}), f32[64,17,1,128]{3,2,1,0:T(1,128)S(1)}, u32[]{:S(2)}, u32[]{:S(2)}) async-start(f32[64,17,1,128]{3,2,1,0:T(1,128)} %bitcast.20), calls=%async_computation | async-start | bytes 1114112 | tf_op jit(solution)/shard_map/all_to_all | solution.py:467
  16.7 1.7 %collective-permute-start = (f32[40,512]{1,0:T(8,128)}, f32[40,512]{1,0:T(8,128)S(1)}, u32[]{:S(2)}, u32[]{:S(2)}) collective-permute-start(f32[40,512]{1,0:T(8,128)} %get-tuple-element.18), channel_id=1, source_target_pairs={{1,0},{0,1},{3,2},{2,3},{5,4},{4,5},{7,6},{6,7},{9,8},{8,9},{11,10... | collective-permute-start | bytes 245768 | tf_op jit(solution)/shard_map/ppermute | solution.py:475
  18.4 0.7 collective-permute-start.1
  19.0 0.1 pad_add_fusion.where
  19.1 2.4 %collective-permute-done.got_a = f32[40,512]{1,0:T(8,128)S(1)} collective-permute-done((f32[40,512]{1,0:T(8,128)}, f32[40,512]{1,0:T(8,128)S(1)}, u32[]{:S(2)}, u32[]{:S(2)}) %collective-permute-start) | collective-permute-done | bytes 81952 | tf_op jit(solution)/shard_map/ppermute | solution.py:475
  21.6 0.8 %strips_kernel.1 = (f32[48,128]{1,0:T(8,128)S(1)}, f32[48,128]{1,0:T(8,128)S(1)}) custom-call(s32[4]{0:T(128)S(1)} %pad_add_fusion.where, f32[40,512]{1,0:T(8,128)S(1)} %collective-permute-done.got_a, f32[40,512]{1,0:T(8,128)S(1)} %collective-permute-done.1.got_b, f32[128,512]{1,0:T(8,128)S(1)} %copy-done.1, f32[128,512]{1,0:T(8,128)S(1)} %copy-done.2, ...), custom_call_target="tpu_custom_call" | custom-call | flops 1000000 | bytes 1000000 | tf_op jit(solution)/shard_map/strips_kernel/pallas_call | solution.py:477
  22.3 0.1 collective-permute-start.2
  22.4 2.4 %collective-permute-start.3 = (f32[48,128]{1,0:T(8,128)S(1)}, f32[48,128]{1,0:T(8,128)S(1)}, u32[]{:S(2)}, u32[]{:S(2)}) collective-permute-start(f32[48,128]{1,0:T(8,128)S(1)} %get-tuple-element.21), channel_id=1, source_target_pairs={{8,4},{4,8},{16,12},{12,16},{24,20},{20,24},{32,28},{28,32},{40,36... | collective-permute-start | bytes 73736 | tf_op jit(solution)/shard_map/ppermute | solution.py:481
  24.9 3.0 %collective-permute-done.3.col_b.order1 = f32[48,128]{1,0:T(8,128)S(1)} collective-permute-done((f32[48,128]{1,0:T(8,128)S(1)}, f32[48,128]{1,0:T(8,128)S(1)}, u32[]{:S(2)}, u32[]{:S(2)}) %collective-permute-start.3) | collective-permute-done | bytes 24608 | tf_op jit(solution)/shard_map/ppermute | solution.py:481
  27.8 7.2 %all-to-all-done = f32[64,17,1,128]{3,2,1,0:T(1,128)S(1)} async-done(((f32[64,17,1,128]{3,2,1,0:T(1,128)}), f32[64,17,1,128]{3,2,1,0:T(1,128)S(1)}, u32[]{:S(2)}, u32[]{:S(2)}) %all-to-all-start) | async-done | bytes 557088 | tf_op jit(solution)/shard_map/all_to_all | solution.py:467
  35.0 1.9 %lateral_kernel.1 = (f32[1088,128]{1,0:T(8,128)}, f32[32,128]{1,0:T(8,128)S(1)}) custom-call(f32[1088,128]{1,0:T(8,128)S(1)} %bitcast.18, f32[32,128]{1,0:T(8,128)S(1)} %copy-done.6, f32[32,128]{1,0:T(8,128)S(1)} %copy-done.7, f32[32,128]{1,0:T(8,128)S(1)} %copy-done.9, f32[48,128]{1,0:T(8,128)S(1)} %collective-permute-done.2.col_a.order0, ...), custom_call_target="tpu_custom_call" | custom-call | flops 1000000000 | bytes 1000000 | tf_op jit(solution)/shard_map/lateral_kernel/pallas_call | solution.py:483
  36.8 6.0 %all-to-all-start.1 = ((f32[64,17,1,128]{3,2,1,0:T(1,128)}), f32[64,17,1,128]{3,2,1,0:T(1,128)S(1)}, u32[]{:S(2)}, u32[]{:S(2)}) async-start(f32[64,17,1,128]{3,2,1,0:T(1,128)} %bitcast.7), calls=%async_computation.1 | async-start | bytes 1114112 | tf_op jit(solution)/shard_map/all_to_all | solution.py:490
  42.8 0.1 copy.24
  42.9 3.2 %collective-permute-start.4 = (f32[64,128]{1,0:T(8,128)S(1)}, f32[64,128]{1,0:T(8,128)S(1)}, u32[]{:S(2)}, u32[]{:S(2)}) collective-permute-start(f32[64,128]{1,0:T(8,128)S(1)} %slice_bitcast_fusion.own), channel_id=1, source_target_pairs={{0,1},{1,0},{2,3},{3,2},{4,5},{5,4},{6,7},{7,6},{8,9},{9,8},{10,11... | collective-permute-start | bytes 98312 | tf_op jit(solution)/shard_map/ppermute | solution.py:509
  46.1 2.1 %collective-permute-start.5 = (f32[64,128]{1,0:T(8,128)S(1)}, f32[64,128]{1,0:T(8,128)S(1)}, u32[]{:S(2)}, u32[]{:S(2)}) collective-permute-start(f32[64,128]{1,0:T(8,128)S(1)} %slice_bitcast_fusion.own), channel_id=1, source_target_pairs={{0,2},{1,3},{2,0},{3,1},{4,6},{5,7},{6,4},{7,5},{8,10},{9,11},{10,... | collective-permute-start | bytes 98312 | tf_op jit(solution)/shard_map/ppermute | solution.py:509
  48.2 0.7 collective-permute-start.6
  48.9 6.4 %flood_kernel.1 = (f32[128,512]{1,0:T(8,128)S(1)}, f32[128,512]{1,0:T(8,128)}, f32[128,512]{1,0:T(8,128)}) custom-call(s32[4]{0:T(128)S(1)} %pad_add_fusion.where, f32[40,512]{1,0:T(8,128)S(1)} %collective-permute-done.got_a, f32[40,512]{1,0:T(8,128)S(1)} %collective-permute-done.1.got_b, f32[48,128]{1,0:T(8,128)S(1)} %collective-permute-done.2.col_a.order0, ...), custom_call_target="tpu_custom_call" | custom-call | flops 100000000 | bytes 10000000 | tf_op jit(solution)/shard_map/flood_kernel/pallas_call | solution.py:496
  55.3 0.8 %flow_kernel.1 = (f32[32,128]{1,0:T(8,128)S(1)}, f32[32,128]{1,0:T(8,128)S(1)}) custom-call(f32[32,128]{1,0:T(8,128)S(1)} %get-tuple-element.29.source, bf16[32,128,128]{2,1,0:T(8,128)(2,1)S(1)} %copy-done), custom_call_target="tpu_custom_call" | custom-call | flops 100000000 | bytes 1000000 | tf_op jit(solution)/shard_map/flow_kernel/pallas_call | solution.py:505
  56.1 0.0 collective-permute-done.4.one
  56.1 3.3 %paths_kernel.1.reach = f32[128,2048]{1,0:T(8,128)S(1)} custom-call(s32[4]{0:T(128)S(1)} %pad_add_fusion.where, f32[64,128]{1,0:T(8,128)S(1)} %slice_bitcast_fusion.own, f32[64,128]{1,0:T(8,128)S(1)} %collective-permute-done.4.one, f32[64,128]{1,0:T(8,128)S(1)} %collective-permute-done.5.two, f32[64,128]{1,0:T(8,128)S(1)} %collective-permute-done.6.three), custom_call_target="tpu_custom_call" | custom-call | flops 1000000000 | bytes 1000000 | tf_op jit(solution)/shard_map/paths_kernel/pallas_call | solution.py:510
  59.4 1.7 %all-to-all-done.1 = f32[64,17,1,128]{3,2,1,0:T(1,128)S(1)} async-done(((f32[64,17,1,128]{3,2,1,0:T(1,128)}), f32[64,17,1,128]{3,2,1,0:T(1,128)S(1)}, u32[]{:S(2)}, u32[]{:S(2)}) %all-to-all-start.1) | async-done | bytes 557088 | tf_op jit(solution)/shard_map/all_to_all | solution.py:490
  61.1 0.3 gather_kernel.1
  61.4 3.2 %collective-permute-start.7 = (f32[8,128]{1,0:T(8,128)S(1)}, f32[8,128]{1,0:T(8,128)S(1)}, u32[]{:S(2)}, u32[]{:S(2)}) collective-permute-start(f32[8,128]{1,0:T(8,128)S(1)} %gather_kernel.1), channel_id=1, source_target_pairs={{0,1},{1,0},{2,3},{3,2},{4,5},{5,4},{6,7},{7,6},{8,9},{9,8},{10,11... | collective-permute-start | bytes 12296 | tf_op jit(solution)/shard_map/ppermute | solution.py:517
  64.5 2.1 %collective-permute-start.8 = (f32[8,128]{1,0:T(8,128)S(1)}, f32[8,128]{1,0:T(8,128)S(1)}, u32[]{:S(2)}, u32[]{:S(2)}) collective-permute-start(f32[8,128]{1,0:T(8,128)S(1)} %gather_kernel.1), channel_id=1, source_target_pairs={{0,2},{1,3},{2,0},{3,1},{4,6},{5,7},{6,4},{7,5},{8,10},{9,11},{10,... | collective-permute-start | bytes 12296 | tf_op jit(solution)/shard_map/ppermute | solution.py:517
  66.6 0.7 collective-permute-start.9
  67.3 1.5 %final_kernel.1 = f32[128,512]{1,0:T(8,128)} custom-call(f32[128,512]{1,0:T(8,128)S(1)} %get-tuple-element.22.water, f32[1088,128]{1,0:T(8,128)S(1)} %bitcast.17, f32[8,512]{1,0:T(8,128)S(1)} %copy-done.8), custom_call_target="tpu_custom_call" | custom-call | flops 1000000000 | bytes 1000000 | tf_op jit(solution)/shard_map/final_kernel/pallas_call | solution.py:518
  68.8 0.9 %collective-permute-done.8 = f32[8,128]{1,0:T(8,128)S(1)} collective-permute-done((f32[8,128]{1,0:T(8,128)S(1)}, f32[8,128]{1,0:T(8,128)S(1)}, u32[]{:S(2)}, u32[]{:S(2)}) %collective-permute-start.8) | collective-permute-done | bytes 4128 | tf_op jit(solution)/shard_map/ppermute | solution.py:517
  69.6 1.8 %collective-permute-done.9 = f32[8,128]{1,0:T(8,128)S(1)} collective-permute-done((f32[8,128]{1,0:T(8,128)S(1)}, f32[8,128]{1,0:T(8,128)S(1)}, u32[]{:S(2)}, u32[]{:S(2)}) %collective-permute-start.9) | collective-permute-done | bytes 4128 | tf_op jit(solution)/shard_map/ppermute | solution.py:517
  71.4 0.1 dynamic-slice_bitcast_fusion
  71.5 0.7 multiply_add_fusion
  (27 shorter events, 0.1 us)
Async XLA Ops:
  0.6 20.9 %copy-start.5 = (f32[128,512]{1,0:T(8,128)S(1)}, f32[128,512]{1,0:T(8,128)}, u32[]{:S(2)}) copy-start(f32[128,512]{1,0:T(8,128)} %f4.3) | copy-start | bytes 786436
  4.5 17.0 %copy-start.1 = (f32[128,512]{1,0:T(8,128)S(1)}, f32[128,512]{1,0:T(8,128)}, u32[]{:S(2)}) copy-start(f32[128,512]{1,0:T(8,128)} %f0.3) | copy-start | bytes 786436
  4.5 17.0 %copy-start.2 = (f32[128,512]{1,0:T(8,128)S(1)}, f32[128,512]{1,0:T(8,128)}, u32[]{:S(2)}) copy-start(f32[128,512]{1,0:T(8,128)} %f1.3) | copy-start | bytes 786436
  4.5 17.0 %copy-start.3 = (f32[128,512]{1,0:T(8,128)S(1)}, f32[128,512]{1,0:T(8,128)}, u32[]{:S(2)}) copy-start(f32[128,512]{1,0:T(8,128)} %f2.3) | copy-start | bytes 786436
  4.5 17.0 %copy-start.4 = (f32[128,512]{1,0:T(8,128)S(1)}, f32[128,512]{1,0:T(8,128)}, u32[]{:S(2)}) copy-start(f32[128,512]{1,0:T(8,128)} %f3.3) | copy-start | bytes 786436
  4.5 30.4 %all-to-all-start = ((f32[64,17,1,128]{3,2,1,0:T(1,128)}), f32[64,17,1,128]{3,2,1,0:T(1,128)S(1)}, u32[]{:S(2)}, u32[]{:S(2)}) async-start(f32[64,17,1,128]{3,2,1,0:T(1,128)} %bitcast.20), calls=%async_computation | async-start | bytes 1114112 | tf_op jit(solution)/shard_map/all_to_all | solution.py:467
  16.7 4.8 %collective-permute-start = (f32[40,512]{1,0:T(8,128)}, f32[40,512]{1,0:T(8,128)S(1)}, u32[]{:S(2)}, u32[]{:S(2)}) collective-permute-start(f32[40,512]{1,0:T(8,128)} %get-tuple-element.18), channel_id=1, source_target_pairs={{1,0},{0,1},{3,2},{2,3},{5,4},{4,5},{7,6},{6,7},{9,8},{8,9},{11,10... | collective-permute-start | bytes 245768 | tf_op jit(solution)/shard_map/ppermute | solution.py:475
  18.4 3.1 %collective-permute-start.1 = (f32[40,512]{1,0:T(8,128)}, f32[40,512]{1,0:T(8,128)S(1)}, u32[]{:S(2)}, u32[]{:S(2)}) collective-permute-start(f32[40,512]{1,0:T(8,128)} %get-tuple-element.19), channel_id=1, source_target_pairs={{2,1},{1,2},{6,5},{5,6},{10,9},{9,10},{14,13},{13,14},{18,17},{17,... | collective-permute-start | bytes 245768 | tf_op jit(solution)/shard_map/ppermute | solution.py:476
  19.1 15.9 %copy-start.6 = (f32[32,128]{1,0:T(8,128)S(1)}, f32[32,128]{1,0:T(8,128)}, u32[]{:S(2)}) copy-start(f32[32,128]{1,0:T(8,128)} %section.1) | copy-start | bytes 49156
  19.1 15.9 %copy-start.7 = (f32[32,128]{1,0:T(8,128)S(1)}, f32[32,128]{1,0:T(8,128)}, u32[]{:S(2)}) copy-start(f32[32,128]{1,0:T(8,128)} %reach_source.1) | copy-start | bytes 49156
  19.1 15.9 %copy-start.9 = (f32[32,128]{1,0:T(8,128)S(1)}, f32[32,128]{1,0:T(8,128)}, u32[]{:S(2)}) copy-start(f32[32,128]{1,0:T(8,128)} %get-tuple-element.24.last_row) | copy-start | bytes 49156
  22.3 2.5 %collective-permute-start.2 = (f32[48,128]{1,0:T(8,128)S(1)}, f32[48,128]{1,0:T(8,128)S(1)}, u32[]{:S(2)}, u32[]{:S(2)}) collective-permute-start(f32[48,128]{1,0:T(8,128)S(1)} %get-tuple-element.20), channel_id=1, source_target_pairs={{4,0},{0,4},{12,8},{8,12},{20,16},{16,20},{28,24},{24,28},{36,32},... | collective-permute-start | bytes 73736 | tf_op jit(solution)/shard_map/ppermute | solution.py:480
  22.4 5.4 %collective-permute-start.3 = (f32[48,128]{1,0:T(8,128)S(1)}, f32[48,128]{1,0:T(8,128)S(1)}, u32[]{:S(2)}, u32[]{:S(2)}) collective-permute-start(f32[48,128]{1,0:T(8,128)S(1)} %get-tuple-element.21), channel_id=1, source_target_pairs={{8,4},{4,8},{16,12},{12,16},{24,20},{20,24},{32,28},{28,32},{40,36... | collective-permute-start | bytes 73736 | tf_op jit(solution)/shard_map/ppermute | solution.py:481
  36.8 24.3 %all-to-all-start.1 = ((f32[64,17,1,128]{3,2,1,0:T(1,128)}), f32[64,17,1,128]{3,2,1,0:T(1,128)S(1)}, u32[]{:S(2)}, u32[]{:S(2)}) async-start(f32[64,17,1,128]{3,2,1,0:T(1,128)} %bitcast.7), calls=%async_computation.1 | async-start | bytes 1114112 | tf_op jit(solution)/shard_map/all_to_all | solution.py:490
  42.9 13.2 %collective-permute-start.4 = (f32[64,128]{1,0:T(8,128)S(1)}, f32[64,128]{1,0:T(8,128)S(1)}, u32[]{:S(2)}, u32[]{:S(2)}) collective-permute-start(f32[64,128]{1,0:T(8,128)S(1)} %slice_bitcast_fusion.own), channel_id=1, source_target_pairs={{0,1},{1,0},{2,3},{3,2},{4,5},{5,4},{6,7},{7,6},{8,9},{9,8},{10,11... | collective-permute-start | bytes 98312 | tf_op jit(solution)/shard_map/ppermute | solution.py:509
  46.1 10.0 %collective-permute-start.5 = (f32[64,128]{1,0:T(8,128)S(1)}, f32[64,128]{1,0:T(8,128)S(1)}, u32[]{:S(2)}, u32[]{:S(2)}) collective-permute-start(f32[64,128]{1,0:T(8,128)S(1)} %slice_bitcast_fusion.own), channel_id=1, source_target_pairs={{0,2},{1,3},{2,0},{3,1},{4,6},{5,7},{6,4},{7,5},{8,10},{9,11},{10,... | collective-permute-start | bytes 98312 | tf_op jit(solution)/shard_map/ppermute | solution.py:509
  48.2 7.9 %collective-permute-start.6 = (f32[64,128]{1,0:T(8,128)S(1)}, f32[64,128]{1,0:T(8,128)S(1)}, u32[]{:S(2)}, u32[]{:S(2)}) collective-permute-start(f32[64,128]{1,0:T(8,128)S(1)} %slice_bitcast_fusion.own), channel_id=1, source_target_pairs={{0,3},{1,2},{2,1},{3,0},{4,7},{5,6},{6,5},{7,4},{8,11},{9,10},{10,... | collective-permute-start | bytes 98312 | tf_op jit(solution)/shard_map/ppermute | solution.py:509
  48.9 6.4 %copy-start = (bf16[32,128,128]{2,1,0:T(8,128)(2,1)S(1)}, bf16[32,128,128]{2,1,0:T(8,128)(2,1)}, u32[]{:S(2)}) copy-start(bf16[32,128,128]{2,1,0:T(8,128)(2,1)} %inverse.1) | copy-start | bytes 3145732
  61.1 6.2 %copy-start.8 = (f32[8,512]{1,0:T(8,128)S(1)}, f32[8,512]{1,0:T(8,128)}, u32[]{:S(2)}) copy-start(f32[8,512]{1,0:T(8,128)} %get-tuple-element.26.slots) | copy-start | bytes 49156
  61.4 7.4 %collective-permute-start.7 = (f32[8,128]{1,0:T(8,128)S(1)}, f32[8,128]{1,0:T(8,128)S(1)}, u32[]{:S(2)}, u32[]{:S(2)}) collective-permute-start(f32[8,128]{1,0:T(8,128)S(1)} %gather_kernel.1), channel_id=1, source_target_pairs={{0,1},{1,0},{2,3},{3,2},{4,5},{5,4},{6,7},{7,6},{8,9},{9,8},{10,11... | collective-permute-start | bytes 12296 | tf_op jit(solution)/shard_map/ppermute | solution.py:517
  64.5 5.1 %collective-permute-start.8 = (f32[8,128]{1,0:T(8,128)S(1)}, f32[8,128]{1,0:T(8,128)S(1)}, u32[]{:S(2)}, u32[]{:S(2)}) collective-permute-start(f32[8,128]{1,0:T(8,128)S(1)} %gather_kernel.1), channel_id=1, source_target_pairs={{0,2},{1,3},{2,0},{3,1},{4,6},{5,7},{6,4},{7,5},{8,10},{9,11},{10,... | collective-permute-start | bytes 12296 | tf_op jit(solution)/shard_map/ppermute | solution.py:517
  66.6 4.8 %collective-permute-start.9 = (f32[8,128]{1,0:T(8,128)S(1)}, f32[8,128]{1,0:T(8,128)S(1)}, u32[]{:S(2)}, u32[]{:S(2)}) collective-permute-start(f32[8,128]{1,0:T(8,128)S(1)} %gather_kernel.1), channel_id=1, source_target_pairs={{0,3},{1,2},{2,1},{3,0},{4,7},{5,6},{6,5},{7,4},{8,11},{9,10},{10,... | collective-permute-start | bytes 12296 | tf_op jit(solution)/shard_map/ppermute | solution.py:517

commit v6 on v5

--- a/solution.py
+++ b/solution.py
@@ -28,7 +28,6 @@
 F32 = jnp.float32
 BF16 = jnp.bfloat16
 VMEM = pl.BlockSpec(memory_space=pltpu.VMEM)
-SMEM = pl.BlockSpec(memory_space=pltpu.SMEM)
 HBM = pl.BlockSpec(memory_space=pltpu.HBM)
 ANY = pl.BlockSpec(memory_space=pl.ANY)
 
@@ -176,9 +175,9 @@
     return rows
 
 
-def paths_kernel(where, own, one, two, three, reach):
+def paths_kernel(own, one, two, three, reach):
     bands = 4
-    band, me = where[1], where[0].astype(F32) + 1.0
+    band, me = lax.axis_index("band"), lax.axis_index("tile").astype(F32) + 1.0
     tiles = own.shape[0]
     blocks = LANES // bands
     group = iota((tiles, LANES), 1) // blocks
@@ -266,13 +265,13 @@
         out[:, cols] = water[:, cols] - PLAIN_SHARE * lateral[c * height : (c + 1) * height]
 
 
-def strips_kernel(where, got_a, got_b, f0, f1, f2, f3, f4, side_a, side_b):
+def strips_kernel(got_a, got_b, f0, f1, f2, f3, f4, side_a, side_b):
     fields = (f0, f1, f2, f3, f4)
     height, width = f0.shape
     tiles = height // 8 + 2
     lane = iota((8, LANES), 1)
     groups = side_a.shape[0] // 8
-    odd_band, odd_tile = where[1] % 2 == 1, where[0] % 2 == 1
+    odd_band, odd_tile = lax.axis_index("band") % 2 == 1, lax.axis_index("tile") % 2 == 1
     lefts = [jnp.zeros((8, LANES), F32) for _ in range(groups)]
     rights = [jnp.zeros((8, LANES), F32) for _ in range(groups)]
     for a, field in enumerate(fields):
@@ -301,7 +300,7 @@
 
 
 def flood_kernel(
-    where, got_a, got_b, col_a, col_b, f0, f1, f2, f3, f4,
+    got_a, got_b, col_a, col_b, f0, f1, f2, f3, f4,
     water_out, east_out, south_out,
     level_s, bed_s, rough_s, qe_s, qs_s, mbe_s, mbs_s,
 ):
@@ -313,7 +312,8 @@
     share = TIME_STEP / CELL_WIDTH
     rate = GRAVITY * TIME_STEP
     slope_rate = share * rate / CELL_WIDTH
-    tile_index, band_index, tile_last, band_last = where[0], where[1], where[2], where[3]
+    tile_index, band_index = lax.axis_index("tile"), lax.axis_index("band")
+    tile_last, band_last = lax.axis_size("tile") - 1, lax.axis_size("band") - 1
     odd_band, odd_tile = band_index % 2 == 1, tile_index % 2 == 1
     easts, wests = [], []
     for v in range(col_a.shape[0] // 8):
@@ -430,9 +430,6 @@
     blocks, reach = reach_source.shape
     total = tiles * CHUNK
     links = link_rows.shape[-1]
-    where = jnp.stack(
-        [tile_index, band_index, jnp.int32(tiles - 1), jnp.int32(bands - 1)]
-    ).astype(jnp.int32)
     ring = [[(i, i ^ k) for i in range(bands)] for k in range(bands)]
 
     down = block_down.reshape(1, blocks)
@@ -475,8 +472,8 @@
     got_a = lax.ppermute(edge_a, "band", pairs(bands, 0))
     got_b = lax.ppermute(edge_b, "band", pairs(bands, 1))
     side_a, side_b = call(
-        strips_kernel, (shaped(48, LANES), shaped(48, LANES)), [SMEM] + [VMEM] * 7, flops=10**6, size=10**6
-    )(where, got_a, got_b, *fields)
+        strips_kernel, (shaped(48, LANES), shaped(48, LANES)), [VMEM] * 7, flops=10**6, size=10**6
+    )(got_a, got_b, *fields)
     col_a = lax.ppermute(side_a, "tile", pairs(tiles, 0))
     col_b = lax.ppermute(side_b, "tile", pairs(tiles, 1))
 
@@ -496,20 +493,20 @@
     water_now, final_east, final_south = call(
         flood_kernel,
         (shaped(height, width),) * 3,
-        [SMEM] + [VMEM] * 9,
+        [VMEM] * 9,
         scratch=[pltpu.VMEM((tall, wide), F32)] * 7,
         flops=10**8,
         size=10**7,
         exps=10**7,
-    )(where, got_a, got_b, col_a, col_b, *fields)
+    )(got_a, got_b, col_a, col_b, *fields)
     base_flow, column = call(
         flow_kernel, (shaped(blocks, reach),) * 2, [VMEM] * 2, flops=10**8, size=10**6
     )(source, reach_inverse)
     extras = rows_in.reshape(tiles, CHUNK, LANES)[:, SLOTS, :]
     others = [lax.ppermute(extras, "band", ring[k]) for k in (1, 2, 3)]
     reached = call(
-        paths_kernel, shaped(LANES, tiles * blocks), [SMEM] + [VMEM] * 4, flops=10**9, size=10**6
-    )(where, extras, *others)
+        paths_kernel, shaped(LANES, tiles * blocks), [VMEM] * 4, flops=10**9, size=10**6
+    )(extras, *others)
 
     pushed = call(gather_kernel, shaped(8, LANES), [VMEM] * 2, flops=10**6, size=10**6)(
         returned.reshape(total, LANES), reached

time: 72.5 us -> 72.1 us (level)
  waiting for transfers between devices: 16.9 us -> 18.8 us
  Pallas kernels: 18.6 us -> 17 us
    pallas_call x3, Pallas kernels: 10.4 us -> 8.81 us  [the longest x1 5.85 us: per_device(): call(flood_kernel, (shaped(height, width),) * 3, [VMEM] * 9, scratch=[plt...]
    all_to_all x1, waiting for transfers between devices: 1.7 us -> 3.17 us  [per_device(): lax.all_to_all(answer.reshape(tiles, CHUNK, 1, LANES), 'tile', split_axis...]
  transfers between devices with their start and end apart: 12 -> 12, of which waited for: 6 -> 6; matrix products, arithmetic and copies ran while one was open for 0% -> 0% of each run, Pallas kernels for 18% -> 15%
where the time goes in v6:
time: 72.1 us; the launch traced here: 71.8 us
  starting transfers between devices  34.2 us (47%)
  waiting for transfers between devices  18.8 us (26%)
  Pallas kernels  17 us (24%)
  between operations  0.86 us (1%)
    all_to_all x1, starting transfers between devices, per_device(): lax.all_to_all(payload.reshape(tiles, CHUNK, 1, LANES), 'tile', split_axi...  12.2 us
    all_to_all x1, waiting for transfers between devices, per_device(): lax.all_to_all(payload.reshape(tiles, CHUNK, 1, LANES), 'tile', split_axi...  7.61 us
    all_to_all x1, starting transfers between devices, per_device(): lax.all_to_all(answer.reshape(tiles, CHUNK, 1, LANES), 'tile', split_axis...  5.98 us
    pallas_call x1, Pallas kernels, per_device(): call(flood_kernel, (shaped(height, width),) * 3, [VMEM] * 9, scratch=[plt...  5.85 us
    ppermute x3, starting transfers between devices, per_device(): others = [lax.ppermute(extras, 'band', ring[k]) for k in (1, 2, 3)]  5.61 us
    ppermute x3, starting transfers between devices, per_device(): lax.ppermute(pushed, 'band', ring[k])  5.5 us
    pallas_call x1, Pallas kernels, per_device(): call(pack_kernel, (shaped(total, LANES), shaped(8, links), shaped(blocks,...  3.85 us
    all_to_all x1, waiting for transfers between devices, per_device(): lax.all_to_all(answer.reshape(tiles, CHUNK, 1, LANES), 'tile', split_axis...  3.17 us
  transfers between devices with their start and end apart: 12, of which 6 were waited for; matrix products, arithmetic and copies ran while one was open for 0% of the time, Pallas kernels for 15%

profile of v6, /device:TPU:2, one launch (start us, length us, event | category | flops | bytes accessed | tf_op | source)
XLA Modules:
  0.0 71.8 jit_solution(6022969865307261478)
XLA Ops:
  0.6 3.9 %pack_kernel.1 = (f32[1088,128]{1,0:T(8,128)}, f32[8,512]{1,0:T(8,128)}, f32[32,128]{1,0:T(8,128)}, f32[40,512]{1,0:T(8,128)}, f32[40,512]{1,0:T(8,128)}) custom-call(f32[128,512]{1,0:T(8,128)} %f0.3, f32[128,512]{1,0:T(8,128)} %f1.3, s32[1,512]{1,0:T(1,128)} %bitcast.19, s32[1,512]{1,0:T(1,128)} %bitcast.20, bf16[32,128,128]{2,1,0:T(8,128)(2,1)} %inverse.1, ...), custom_call_target="tpu_custom_call" | custom-call | flops 1000000000 | bytes 1000000 | tf_op jit(solution)/shard_map/pack_kernel/pallas_call | solution.py:437
  4.5 0.0 copy-start.1
  4.5 0.0 copy-start.2
  4.5 0.0 copy-start.3
  4.5 12.2 %all-to-all-start = ((f32[64,17,1,128]{3,2,1,0:T(1,128)}), f32[64,17,1,128]{3,2,1,0:T(1,128)S(1)}, u32[]{:S(2)}, u32[]{:S(2)}) async-start(f32[64,17,1,128]{3,2,1,0:T(1,128)} %bitcast.18), calls=%async_computation | async-start | bytes 1114112 | tf_op jit(solution)/shard_map/all_to_all | solution.py:464
  16.7 1.7 %collective-permute-start = (f32[40,512]{1,0:T(8,128)}, f32[40,512]{1,0:T(8,128)S(1)}, u32[]{:S(2)}, u32[]{:S(2)}) collective-permute-start(f32[40,512]{1,0:T(8,128)} %get-tuple-element.18), channel_id=1, source_target_pairs={{1,0},{0,1},{3,2},{2,3},{5,4},{4,5},{7,6},{6,7},{9,8},{8,9},{11,10... | collective-permute-start | bytes 245768 | tf_op jit(solution)/shard_map/ppermute | solution.py:472
  18.4 0.8 %collective-permute-start.1 = (f32[40,512]{1,0:T(8,128)}, f32[40,512]{1,0:T(8,128)S(1)}, u32[]{:S(2)}, u32[]{:S(2)}) collective-permute-start(f32[40,512]{1,0:T(8,128)} %get-tuple-element.19), channel_id=1, source_target_pairs={{2,1},{1,2},{6,5},{5,6},{10,9},{9,10},{14,13},{13,14},{18,17},{17,... | collective-permute-start | bytes 245768 | tf_op jit(solution)/shard_map/ppermute | solution.py:473
  19.2 2.3 %collective-permute-done.got_a = f32[40,512]{1,0:T(8,128)S(1)} collective-permute-done((f32[40,512]{1,0:T(8,128)}, f32[40,512]{1,0:T(8,128)S(1)}, u32[]{:S(2)}, u32[]{:S(2)}) %collective-permute-start) | collective-permute-done | bytes 81952 | tf_op jit(solution)/shard_map/ppermute | solution.py:472
  21.6 0.2 strips_kernel.1
  21.8 0.1 collective-permute-start.2
  21.9 2.4 %collective-permute-start.3 = (f32[48,128]{1,0:T(8,128)S(1)}, f32[48,128]{1,0:T(8,128)S(1)}, u32[]{:S(2)}, u32[]{:S(2)}) collective-permute-start(f32[48,128]{1,0:T(8,128)S(1)} %get-tuple-element.21), channel_id=1, source_target_pairs={{8,4},{4,8},{16,12},{12,16},{24,20},{20,24},{32,28},{28,32},{40,36... | collective-permute-start | bytes 73736 | tf_op jit(solution)/shard_map/ppermute | solution.py:478
  24.3 3.0 %collective-permute-done.3.col_b.order1 = f32[48,128]{1,0:T(8,128)S(1)} collective-permute-done((f32[48,128]{1,0:T(8,128)S(1)}, f32[48,128]{1,0:T(8,128)S(1)}, u32[]{:S(2)}, u32[]{:S(2)}) %collective-permute-start.3) | collective-permute-done | bytes 24608 | tf_op jit(solution)/shard_map/ppermute | solution.py:478
  27.4 7.6 %all-to-all-done = f32[64,17,1,128]{3,2,1,0:T(1,128)S(1)} async-done(((f32[64,17,1,128]{3,2,1,0:T(1,128)}), f32[64,17,1,128]{3,2,1,0:T(1,128)S(1)}, u32[]{:S(2)}, u32[]{:S(2)}) %all-to-all-start) | async-done | bytes 557088 | tf_op jit(solution)/shard_map/all_to_all | solution.py:464
  35.0 1.8 %lateral_kernel.1 = (f32[1088,128]{1,0:T(8,128)}, f32[32,128]{1,0:T(8,128)S(1)}) custom-call(f32[1088,128]{1,0:T(8,128)S(1)} %bitcast.16, f32[32,128]{1,0:T(8,128)S(1)} %copy-done.6, f32[32,128]{1,0:T(8,128)S(1)} %copy-done.7, f32[32,128]{1,0:T(8,128)S(1)} %copy-done.9, f32[48,128]{1,0:T(8,128)S(1)} %collective-permute-done.2.col_a.order0, ...), custom_call_target="tpu_custom_call" | custom-call | flops 1000000000 | bytes 1000000 | tf_op jit(solution)/shard_map/lateral_kernel/pallas_call | solution.py:480
  36.8 6.0 %all-to-all-start.1 = ((f32[64,17,1,128]{3,2,1,0:T(1,128)}), f32[64,17,1,128]{3,2,1,0:T(1,128)S(1)}, u32[]{:S(2)}, u32[]{:S(2)}) async-start(f32[64,17,1,128]{3,2,1,0:T(1,128)} %bitcast.5), calls=%async_computation.1 | async-start | bytes 1114112 | tf_op jit(solution)/shard_map/all_to_all | solution.py:487
  42.8 0.1 copy.24
  42.9 2.8 %collective-permute-start.4 = (f32[64,128]{1,0:T(8,128)S(1)}, f32[64,128]{1,0:T(8,128)S(1)}, u32[]{:S(2)}, u32[]{:S(2)}) collective-permute-start(f32[64,128]{1,0:T(8,128)S(1)} %slice_bitcast_fusion.own), channel_id=1, source_target_pairs={{0,1},{1,0},{2,3},{3,2},{4,5},{5,4},{6,7},{7,6},{8,9},{9,8},{10,11... | collective-permute-start | bytes 98312 | tf_op jit(solution)/shard_map/ppermute | solution.py:506
  45.7 2.1 %collective-permute-start.5 = (f32[64,128]{1,0:T(8,128)S(1)}, f32[64,128]{1,0:T(8,128)S(1)}, u32[]{:S(2)}, u32[]{:S(2)}) collective-permute-start(f32[64,128]{1,0:T(8,128)S(1)} %slice_bitcast_fusion.own), channel_id=1, source_target_pairs={{0,2},{1,3},{2,0},{3,1},{4,6},{5,7},{6,4},{7,5},{8,10},{9,11},{10,... | collective-permute-start | bytes 98312 | tf_op jit(solution)/shard_map/ppermute | solution.py:506
  47.8 0.7 collective-permute-start.6
  48.5 5.8 %flood_kernel.1 = (f32[128,512]{1,0:T(8,128)S(1)}, f32[128,512]{1,0:T(8,128)}, f32[128,512]{1,0:T(8,128)}) custom-call(f32[40,512]{1,0:T(8,128)S(1)} %collective-permute-done.got_a, f32[40,512]{1,0:T(8,128)S(1)} %collective-permute-done.1.got_b, f32[48,128]{1,0:T(8,128)S(1)} %collective-permute-done.2.col_a.order0, ...), custom_call_target="tpu_custom_call" | custom-call | flops 100000000 | bytes 10000000 | tf_op jit(solution)/shard_map/flood_kernel/pallas_call | solution.py:493
  54.4 0.8 %flow_kernel.1 = (f32[32,128]{1,0:T(8,128)S(1)}, f32[32,128]{1,0:T(8,128)S(1)}) custom-call(f32[32,128]{1,0:T(8,128)S(1)} %get-tuple-element.29.source, bf16[32,128,128]{2,1,0:T(8,128)(2,1)S(1)} %copy-done), custom_call_target="tpu_custom_call" | custom-call | flops 100000000 | bytes 1000000 | tf_op jit(solution)/shard_map/flow_kernel/pallas_call | solution.py:502
  55.2 2.7 %paths_kernel.1.reach = f32[128,2048]{1,0:T(8,128)S(1)} custom-call(f32[64,128]{1,0:T(8,128)S(1)} %slice_bitcast_fusion.own, f32[64,128]{1,0:T(8,128)S(1)} %collective-permute-done.4.one, f32[64,128]{1,0:T(8,128)S(1)} %collective-permute-done.5.two, f32[64,128]{1,0:T(8,128)S(1)} %collective-permute-done.6.three), custom_call_target="tpu_custom_call" | custom-call | flops 1000000000 | bytes 1000000 | tf_op jit(solution)/shard_map/paths_kernel/pallas_call | solution.py:507
  57.9 3.2 %all-to-all-done.1 = f32[64,17,1,128]{3,2,1,0:T(1,128)S(1)} async-done(((f32[64,17,1,128]{3,2,1,0:T(1,128)}), f32[64,17,1,128]{3,2,1,0:T(1,128)S(1)}, u32[]{:S(2)}, u32[]{:S(2)}) %all-to-all-start.1) | async-done | bytes 557088 | tf_op jit(solution)/shard_map/all_to_all | solution.py:487
  61.1 0.3 gather_kernel.1
  61.4 2.8 %collective-permute-start.7 = (f32[8,128]{1,0:T(8,128)S(1)}, f32[8,128]{1,0:T(8,128)S(1)}, u32[]{:S(2)}, u32[]{:S(2)}) collective-permute-start(f32[8,128]{1,0:T(8,128)S(1)} %gather_kernel.1), channel_id=1, source_target_pairs={{0,1},{1,0},{2,3},{3,2},{4,5},{5,4},{6,7},{7,6},{8,9},{9,8},{10,11... | collective-permute-start | bytes 12296 | tf_op jit(solution)/shard_map/ppermute | solution.py:514
  64.1 2.1 %collective-permute-start.8 = (f32[8,128]{1,0:T(8,128)S(1)}, f32[8,128]{1,0:T(8,128)S(1)}, u32[]{:S(2)}, u32[]{:S(2)}) collective-permute-start(f32[8,128]{1,0:T(8,128)S(1)} %gather_kernel.1), channel_id=1, source_target_pairs={{0,2},{1,3},{2,0},{3,1},{4,6},{5,7},{6,4},{7,5},{8,10},{9,11},{10,... | collective-permute-start | bytes 12296 | tf_op jit(solution)/shard_map/ppermute | solution.py:514
  66.2 0.7 collective-permute-start.9
  66.9 1.5 %final_kernel.1 = f32[128,512]{1,0:T(8,128)} custom-call(f32[128,512]{1,0:T(8,128)S(1)} %get-tuple-element.22.water, f32[1088,128]{1,0:T(8,128)S(1)} %bitcast.15, f32[8,512]{1,0:T(8,128)S(1)} %copy-done.8), custom_call_target="tpu_custom_call" | custom-call | flops 1000000000 | bytes 1000000 | tf_op jit(solution)/shard_map/final_kernel/pallas_call | solution.py:515
  68.4 0.9 %collective-permute-done.8 = f32[8,128]{1,0:T(8,128)S(1)} collective-permute-done((f32[8,128]{1,0:T(8,128)S(1)}, f32[8,128]{1,0:T(8,128)S(1)}, u32[]{:S(2)}, u32[]{:S(2)}) %collective-permute-start.8) | collective-permute-done | bytes 4128 | tf_op jit(solution)/shard_map/ppermute | solution.py:514
  69.2 1.8 %collective-permute-done.9 = f32[8,128]{1,0:T(8,128)S(1)} collective-permute-done((f32[8,128]{1,0:T(8,128)S(1)}, f32[8,128]{1,0:T(8,128)S(1)}, u32[]{:S(2)}, u32[]{:S(2)}) %collective-permute-start.9) | collective-permute-done | bytes 4128 | tf_op jit(solution)/shard_map/ppermute | solution.py:514
  71.0 0.1 dynamic-slice_bitcast_fusion
  71.1 0.7 multiply_add_fusion
  (26 shorter events, 0.1 us)
Async XLA Ops:
  0.6 20.9 %copy-start.5 = (f32[128,512]{1,0:T(8,128)S(1)}, f32[128,512]{1,0:T(8,128)}, u32[]{:S(2)}) copy-start(f32[128,512]{1,0:T(8,128)} %f4.3) | copy-start | bytes 786436
  4.5 17.0 %copy-start.1 = (f32[128,512]{1,0:T(8,128)S(1)}, f32[128,512]{1,0:T(8,128)}, u32[]{:S(2)}) copy-start(f32[128,512]{1,0:T(8,128)} %f0.3) | copy-start | bytes 786436
  4.5 17.0 %copy-start.2 = (f32[128,512]{1,0:T(8,128)S(1)}, f32[128,512]{1,0:T(8,128)}, u32[]{:S(2)}) copy-start(f32[128,512]{1,0:T(8,128)} %f1.3) | copy-start | bytes 786436
  4.5 17.0 %copy-start.3 = (f32[128,512]{1,0:T(8,128)S(1)}, f32[128,512]{1,0:T(8,128)}, u32[]{:S(2)}) copy-start(f32[128,512]{1,0:T(8,128)} %f2.3) | copy-start | bytes 786436
  4.5 17.0 %copy-start.4 = (f32[128,512]{1,0:T(8,128)S(1)}, f32[128,512]{1,0:T(8,128)}, u32[]{:S(2)}) copy-start(f32[128,512]{1,0:T(8,128)} %f3.3) | copy-start | bytes 786436
  4.5 30.4 %all-to-all-start = ((f32[64,17,1,128]{3,2,1,0:T(1,128)}), f32[64,17,1,128]{3,2,1,0:T(1,128)S(1)}, u32[]{:S(2)}, u32[]{:S(2)}) async-start(f32[64,17,1,128]{3,2,1,0:T(1,128)} %bitcast.18), calls=%async_computation | async-start | bytes 1114112 | tf_op jit(solution)/shard_map/all_to_all | solution.py:464
  16.7 4.8 %collective-permute-start = (f32[40,512]{1,0:T(8,128)}, f32[40,512]{1,0:T(8,128)S(1)}, u32[]{:S(2)}, u32[]{:S(2)}) collective-permute-start(f32[40,512]{1,0:T(8,128)} %get-tuple-element.18), channel_id=1, source_target_pairs={{1,0},{0,1},{3,2},{2,3},{5,4},{4,5},{7,6},{6,7},{9,8},{8,9},{11,10... | collective-permute-start | bytes 245768 | tf_op jit(solution)/shard_map/ppermute | solution.py:472
  18.4 16.6 %copy-start.6 = (f32[32,128]{1,0:T(8,128)S(1)}, f32[32,128]{1,0:T(8,128)}, u32[]{:S(2)}) copy-start(f32[32,128]{1,0:T(8,128)} %section.1) | copy-start | bytes 49156
  18.4 16.6 %copy-start.7 = (f32[32,128]{1,0:T(8,128)S(1)}, f32[32,128]{1,0:T(8,128)}, u32[]{:S(2)}) copy-start(f32[32,128]{1,0:T(8,128)} %reach_source.1) | copy-start | bytes 49156
  18.4 16.6 %copy-start.9 = (f32[32,128]{1,0:T(8,128)S(1)}, f32[32,128]{1,0:T(8,128)}, u32[]{:S(2)}) copy-start(f32[32,128]{1,0:T(8,128)} %get-tuple-element.24.last_row) | copy-start | bytes 49156
  18.4 3.1 %collective-permute-start.1 = (f32[40,512]{1,0:T(8,128)}, f32[40,512]{1,0:T(8,128)S(1)}, u32[]{:S(2)}, u32[]{:S(2)}) collective-permute-start(f32[40,512]{1,0:T(8,128)} %get-tuple-element.19), channel_id=1, source_target_pairs={{2,1},{1,2},{6,5},{5,6},{10,9},{9,10},{14,13},{13,14},{18,17},{17,... | collective-permute-start | bytes 245768 | tf_op jit(solution)/shard_map/ppermute | solution.py:473
  21.8 2.5 %collective-permute-start.2 = (f32[48,128]{1,0:T(8,128)S(1)}, f32[48,128]{1,0:T(8,128)S(1)}, u32[]{:S(2)}, u32[]{:S(2)}) collective-permute-start(f32[48,128]{1,0:T(8,128)S(1)} %get-tuple-element.20), channel_id=1, source_target_pairs={{4,0},{0,4},{12,8},{8,12},{20,16},{16,20},{28,24},{24,28},{36,32},... | collective-permute-start | bytes 73736 | tf_op jit(solution)/shard_map/ppermute | solution.py:477
  21.9 5.5 %collective-permute-start.3 = (f32[48,128]{1,0:T(8,128)S(1)}, f32[48,128]{1,0:T(8,128)S(1)}, u32[]{:S(2)}, u32[]{:S(2)}) collective-permute-start(f32[48,128]{1,0:T(8,128)S(1)} %get-tuple-element.21), channel_id=1, source_target_pairs={{8,4},{4,8},{16,12},{12,16},{24,20},{20,24},{32,28},{28,32},{40,36... | collective-permute-start | bytes 73736 | tf_op jit(solution)/shard_map/ppermute | solution.py:478
  36.8 24.3 %all-to-all-start.1 = ((f32[64,17,1,128]{3,2,1,0:T(1,128)}), f32[64,17,1,128]{3,2,1,0:T(1,128)S(1)}, u32[]{:S(2)}, u32[]{:S(2)}) async-start(f32[64,17,1,128]{3,2,1,0:T(1,128)} %bitcast.5), calls=%async_computation.1 | async-start | bytes 1114112 | tf_op jit(solution)/shard_map/all_to_all | solution.py:487
  42.9 12.2 %collective-permute-start.4 = (f32[64,128]{1,0:T(8,128)S(1)}, f32[64,128]{1,0:T(8,128)S(1)}, u32[]{:S(2)}, u32[]{:S(2)}) collective-permute-start(f32[64,128]{1,0:T(8,128)S(1)} %slice_bitcast_fusion.own), channel_id=1, source_target_pairs={{0,1},{1,0},{2,3},{3,2},{4,5},{5,4},{6,7},{7,6},{8,9},{9,8},{10,11... | collective-permute-start | bytes 98312 | tf_op jit(solution)/shard_map/ppermute | solution.py:506
  45.7 9.4 %collective-permute-start.5 = (f32[64,128]{1,0:T(8,128)S(1)}, f32[64,128]{1,0:T(8,128)S(1)}, u32[]{:S(2)}, u32[]{:S(2)}) collective-permute-start(f32[64,128]{1,0:T(8,128)S(1)} %slice_bitcast_fusion.own), channel_id=1, source_target_pairs={{0,2},{1,3},{2,0},{3,1},{4,6},{5,7},{6,4},{7,5},{8,10},{9,11},{10,... | collective-permute-start | bytes 98312 | tf_op jit(solution)/shard_map/ppermute | solution.py:506
  47.8 7.4 %collective-permute-start.6 = (f32[64,128]{1,0:T(8,128)S(1)}, f32[64,128]{1,0:T(8,128)S(1)}, u32[]{:S(2)}, u32[]{:S(2)}) collective-permute-start(f32[64,128]{1,0:T(8,128)S(1)} %slice_bitcast_fusion.own), channel_id=1, source_target_pairs={{0,3},{1,2},{2,1},{3,0},{4,7},{5,6},{6,5},{7,4},{8,11},{9,10},{10,... | collective-permute-start | bytes 98312 | tf_op jit(solution)/shard_map/ppermute | solution.py:506
  48.5 5.9 %copy-start = (bf16[32,128,128]{2,1,0:T(8,128)(2,1)S(1)}, bf16[32,128,128]{2,1,0:T(8,128)(2,1)}, u32[]{:S(2)}) copy-start(bf16[32,128,128]{2,1,0:T(8,128)(2,1)} %inverse.1) | copy-start | bytes 3145732
  61.1 5.8 %copy-start.8 = (f32[8,512]{1,0:T(8,128)S(1)}, f32[8,512]{1,0:T(8,128)}, u32[]{:S(2)}) copy-start(f32[8,512]{1,0:T(8,128)} %get-tuple-element.26.slots) | copy-start | bytes 49156
  61.4 7.0 %collective-permute-start.7 = (f32[8,128]{1,0:T(8,128)S(1)}, f32[8,128]{1,0:T(8,128)S(1)}, u32[]{:S(2)}, u32[]{:S(2)}) collective-permute-start(f32[8,128]{1,0:T(8,128)S(1)} %gather_kernel.1), channel_id=1, source_target_pairs={{0,1},{1,0},{2,3},{3,2},{4,5},{5,4},{6,7},{7,6},{8,9},{9,8},{10,11... | collective-permute-start | bytes 12296 | tf_op jit(solution)/shard_map/ppermute | solution.py:514
  64.1 5.1 %collective-permute-start.8 = (f32[8,128]{1,0:T(8,128)S(1)}, f32[8,128]{1,0:T(8,128)S(1)}, u32[]{:S(2)}, u32[]{:S(2)}) collective-permute-start(f32[8,128]{1,0:T(8,128)S(1)} %gather_kernel.1), channel_id=1, source_target_pairs={{0,2},{1,3},{2,0},{3,1},{4,6},{5,7},{6,4},{7,5},{8,10},{9,11},{10,... | collective-permute-start | bytes 12296 | tf_op jit(solution)/shard_map/ppermute | solution.py:514
  66.2 4.8 %collective-permute-start.9 = (f32[8,128]{1,0:T(8,128)S(1)}, f32[8,128]{1,0:T(8,128)S(1)}, u32[]{:S(2)}, u32[]{:S(2)}) collective-permute-start(f32[8,128]{1,0:T(8,128)S(1)} %gather_kernel.1), channel_id=1, source_target_pairs={{0,3},{1,2},{2,1},{3,0},{4,7},{5,6},{6,5},{7,4},{8,11},{9,10},{10,... | collective-permute-start | bytes 12296 | tf_op jit(solution)/shard_map/ppermute | solution.py:514

commit v7 on v6

--- a/solution.py
+++ b/solution.py
@@ -56,9 +56,9 @@
 
 
 def pack_kernel(
-    water_h, bed_h, rows_h, blocks_h, inverse_h, rough_h, east_h, south_h, down,
+    water_h, bed_h, rows_h, blocks_h, inverse_h, rough_h, east_h, south_h, down_h,
     out, slots, last_out, edge_a, edge_b,
-    water, bed, link_rows, link_blocks, tails, row_s, sems,
+    water, bed, link_rows, link_blocks, tails, row_s, down, sems,
 ):
     blocks_own, reach = last_out.shape
     moves = (
@@ -67,6 +67,7 @@
         (water_h, water),
         (bed_h, bed),
         (inverse_h.at[:, reach - 16 : reach, :], tails),
+        (down_h, down),
     )
     height = water.shape[0]
     odd = lax.axis_index("band") % 2
@@ -119,7 +120,8 @@
     seat = iota((links, LANES), 1).astype(F32) - float(ID_LANE)
     rank_hot = jnp.where(rank == seat, local_c + 1.0, 0.0)
     ids = mm(dest_hot, rank_hot.astype(BF16))
-    copies[4].wait()
+    for copy in copies[4:]:
+        copy.wait()
     last = tails[:, 15, :].astype(F32)
     last_out[...] = last
     first = (iota((8, reach), 1) == 0).astype(F32).astype(BF16)
@@ -131,8 +133,6 @@
     row_s[...] = jnp.zeros(row_s.shape, F32)
     row_s[0:1, 0:blocks_own] = down[...].astype(F32)
     out[pl.ds(SLOTS, tiles, CHUNK), :] = ids + (row_s[0:1, :] + gain[0:1, :])
-    for copy in copies[5:]:
-        copy.wait()
 
 
 def lateral_kernel(rows_in, section, reach_source, last_row, order0, order1, out, source):
@@ -250,6 +250,17 @@
         column_now = jnp.where(row == g, x[2 * blocks :], column_now)
     base[...] = base_now
     column[...] = column_now
+
+
+def discharge_kernel(base, column, own, one, two, three, out):
+    blocks = base.shape[0]
+    band = lax.axis_index("band")
+    total = own[...] + one[...] + two[...] + three[...]
+    turned = jnp.transpose(total)[:, 0:1]
+    inflow = turned[0:blocks]
+    for b in range(1, LANES // blocks):
+        inflow = jnp.where(band == b, turned[b * blocks : (b + 1) * blocks], inflow)
+    out[...] = base[...] + column[...] * inflow
 
 
 def final_kernel(water, returned, slots, out):
@@ -405,7 +416,7 @@
     return jax.ShapeDtypeStruct(shape, F32)
 
 
-def call(kernel, out_shape, specs, scratch=(), flops=0, size=0, exps=0, limit=40 * 1024 * 1024):
+def call(kernel, out_shape, specs, scratch=(), flops=0, size=0, exps=0, limit=16 * 1024 * 1024):
     return pl.pallas_call(
         kernel,
         out_shape=out_shape,
@@ -437,7 +448,7 @@
     payload, slots, last_row, edge_a, edge_b = call(
         pack_kernel,
         (shaped(total, LANES), shaped(8, links), shaped(blocks, reach), edge, edge),
-        [HBM] * 8 + [VMEM],
+        [HBM] * 9,
         scratch=[
             pltpu.VMEM((height, width), F32),
             pltpu.VMEM((height, width), F32),
@@ -445,7 +456,8 @@
             pltpu.VMEM((1, links), jnp.int32),
             pltpu.VMEM((blocks, 16, reach), BF16),
             pltpu.VMEM((8, LANES), F32),
-            pltpu.SemaphoreType.DMA((11,)),
+            pltpu.VMEM((1, blocks), jnp.int32),
+            pltpu.SemaphoreType.DMA((12,)),
         ],
         limit=None,
         flops=10**9,
@@ -515,8 +527,9 @@
     final_depth = call(
         final_kernel, shaped(height, width), [VMEM] * 3, flops=10**9, size=10**6
     )(water_now, returned.reshape(total, LANES), slots)
-    inflow = lax.dynamic_slice_in_dim(sum(parts)[0], band_index * blocks, blocks)
-    discharge = base_flow + column * inflow[:, None]
+    discharge = call(
+        discharge_kernel, shaped(blocks, reach), [VMEM] * 6, flops=10**4, size=10**4
+    )(base_flow, column, *parts)
     return (final_depth, final_east, final_south, discharge)
 
 

time: 72.1 us -> 71.5 us (level)
    pallas_call x0 -> x1, Pallas kernels: none -> 0.78 us  [per_device(): call(discharge_kernel, shaped(blocks, reach), [VMEM] * 6, flops=10 ** 4,...]
  transfers between devices with their start and end apart: 12 -> 12, of which waited for: 6 -> 6; matrix products, arithmetic and copies ran while one was open for 0% -> 0% of each run, Pallas kernels for 15% -> 16%
where the time goes in v7:
time: 71.5 us; the launch traced here: 71.1 us
  starting transfers between devices  34.2 us (48%)
  waiting for transfers between devices  18.8 us (26%)
  Pallas kernels  17.2 us (24%)
  between operations  0.86 us (1%)
    all_to_all x1, starting transfers between devices, per_device(): lax.all_to_all(payload.reshape(tiles, CHUNK, 1, LANES), 'tile', split_axi...  12.2 us
    all_to_all x1, waiting for transfers between devices, per_device(): lax.all_to_all(payload.reshape(tiles, CHUNK, 1, LANES), 'tile', split_axi...  7.61 us
    all_to_all x1, starting transfers between devices, per_device(): lax.all_to_all(answer.reshape(tiles, CHUNK, 1, LANES), 'tile', split_axis...  5.98 us
    pallas_call x1, Pallas kernels, per_device(): call(flood_kernel, (shaped(height, width),) * 3, [VMEM] * 9, scratch=[plt...  5.85 us
    ppermute x3, starting transfers between devices, per_device(): others = [lax.ppermute(extras, 'band', ring[k]) for k in (1, 2, 3)]  5.61 us
    ppermute x3, starting transfers between devices, per_device(): lax.ppermute(pushed, 'band', ring[k])  5.5 us
    pallas_call x1, Pallas kernels, per_device(): call(pack_kernel, (shaped(total, LANES), shaped(8, links), shaped(blocks,...  3.17 us
    all_to_all x1, waiting for transfers between devices, per_device(): lax.all_to_all(answer.reshape(tiles, CHUNK, 1, LANES), 'tile', split_axis...  3.12 us
  transfers between devices with their start and end apart: 12, of which 6 were waited for; matrix products, arithmetic and copies ran while one was open for 0% of the time, Pallas kernels for 16%

profile of v7, /device:TPU:2, one launch (start us, length us, event | category | flops | bytes accessed | tf_op | source)
XLA Modules:
  0.0 71.1 jit_solution(14000307777810542810)
XLA Ops:
  0.6 3.2 %pack_kernel.1 = (f32[1088,128]{1,0:T(8,128)}, f32[8,512]{1,0:T(8,128)}, f32[32,128]{1,0:T(8,128)}, f32[40,512]{1,0:T(8,128)}, f32[40,512]{1,0:T(8,128)}) custom-call(f32[128,512]{1,0:T(8,128)} %f0.3, f32[128,512]{1,0:T(8,128)} %f1.3, s32[1,512]{1,0:T(1,128)} %bitcast.17, s32[1,512]{1,0:T(1,128)} %bitcast.18, bf16[32,128,128]{2,1,0:T(8,128)(2,1)} %inverse.1, ...), custom_call_target="tpu_custom_call" | custom-call | flops 1000000000 | bytes 1000000 | tf_op jit(solution)/shard_map/pack_kernel/pallas_call | solution.py:448
  3.8 0.0 copy-start.1
  3.8 0.0 copy-start.2
  3.8 0.0 copy-start.3
  3.9 12.2 %all-to-all-start = ((f32[64,17,1,128]{3,2,1,0:T(1,128)}), f32[64,17,1,128]{3,2,1,0:T(1,128)S(1)}, u32[]{:S(2)}, u32[]{:S(2)}) async-start(f32[64,17,1,128]{3,2,1,0:T(1,128)} %bitcast.16), calls=%async_computation | async-start | bytes 1114112 | tf_op jit(solution)/shard_map/all_to_all | solution.py:476
  16.0 1.7 %collective-permute-start = (f32[40,512]{1,0:T(8,128)}, f32[40,512]{1,0:T(8,128)S(1)}, u32[]{:S(2)}, u32[]{:S(2)}) collective-permute-start(f32[40,512]{1,0:T(8,128)} %get-tuple-element.18), channel_id=1, source_target_pairs={{1,0},{0,1},{3,2},{2,3},{5,4},{4,5},{7,6},{6,7},{9,8},{8,9},{11,10... | collective-permute-start | bytes 245768 | tf_op jit(solution)/shard_map/ppermute | solution.py:484
  17.7 0.8 %collective-permute-start.1 = (f32[40,512]{1,0:T(8,128)}, f32[40,512]{1,0:T(8,128)S(1)}, u32[]{:S(2)}, u32[]{:S(2)}) collective-permute-start(f32[40,512]{1,0:T(8,128)} %get-tuple-element.19), channel_id=1, source_target_pairs={{2,1},{1,2},{6,5},{5,6},{10,9},{9,10},{14,13},{13,14},{18,17},{17,... | collective-permute-start | bytes 245768 | tf_op jit(solution)/shard_map/ppermute | solution.py:485
  18.5 2.3 %collective-permute-done.got_a = f32[40,512]{1,0:T(8,128)S(1)} collective-permute-done((f32[40,512]{1,0:T(8,128)}, f32[40,512]{1,0:T(8,128)S(1)}, u32[]{:S(2)}, u32[]{:S(2)}) %collective-permute-start) | collective-permute-done | bytes 81952 | tf_op jit(solution)/shard_map/ppermute | solution.py:484
  20.9 0.2 strips_kernel.1
  21.1 0.1 collective-permute-start.2
  21.2 2.4 %collective-permute-start.3 = (f32[48,128]{1,0:T(8,128)S(1)}, f32[48,128]{1,0:T(8,128)S(1)}, u32[]{:S(2)}, u32[]{:S(2)}) collective-permute-start(f32[48,128]{1,0:T(8,128)S(1)} %get-tuple-element.21), channel_id=1, source_target_pairs={{8,4},{4,8},{16,12},{12,16},{24,20},{20,24},{32,28},{28,32},{40,36... | collective-permute-start | bytes 73736 | tf_op jit(solution)/shard_map/ppermute | solution.py:490
  23.6 3.0 %collective-permute-done.3.col_b.order1 = f32[48,128]{1,0:T(8,128)S(1)} collective-permute-done((f32[48,128]{1,0:T(8,128)S(1)}, f32[48,128]{1,0:T(8,128)S(1)}, u32[]{:S(2)}, u32[]{:S(2)}) %collective-permute-start.3) | collective-permute-done | bytes 24608 | tf_op jit(solution)/shard_map/ppermute | solution.py:490
  26.7 7.6 %all-to-all-done = f32[64,17,1,128]{3,2,1,0:T(1,128)S(1)} async-done(((f32[64,17,1,128]{3,2,1,0:T(1,128)}), f32[64,17,1,128]{3,2,1,0:T(1,128)S(1)}, u32[]{:S(2)}, u32[]{:S(2)}) %all-to-all-start) | async-done | bytes 557088 | tf_op jit(solution)/shard_map/all_to_all | solution.py:476
  34.3 1.9 %lateral_kernel.1 = (f32[1088,128]{1,0:T(8,128)}, f32[32,128]{1,0:T(8,128)S(1)}) custom-call(f32[1088,128]{1,0:T(8,128)S(1)} %bitcast.14, f32[32,128]{1,0:T(8,128)S(1)} %copy-done.6, f32[32,128]{1,0:T(8,128)S(1)} %copy-done.7, f32[32,128]{1,0:T(8,128)S(1)} %copy-done.9, f32[48,128]{1,0:T(8,128)S(1)} %collective-permute-done.2.col_a.order0, ...), custom_call_target="tpu_custom_call" | custom-call | flops 1000000000 | bytes 1000000 | tf_op jit(solution)/shard_map/lateral_kernel/pallas_call | solution.py:492
  36.2 6.0 %all-to-all-start.1 = ((f32[64,17,1,128]{3,2,1,0:T(1,128)}), f32[64,17,1,128]{3,2,1,0:T(1,128)S(1)}, u32[]{:S(2)}, u32[]{:S(2)}) async-start(f32[64,17,1,128]{3,2,1,0:T(1,128)} %bitcast.5), calls=%async_computation.1 | async-start | bytes 1114112 | tf_op jit(solution)/shard_map/all_to_all | solution.py:499
  42.1 0.1 copy.24
  42.2 2.8 %collective-permute-start.4 = (f32[64,128]{1,0:T(8,128)S(1)}, f32[64,128]{1,0:T(8,128)S(1)}, u32[]{:S(2)}, u32[]{:S(2)}) collective-permute-start(f32[64,128]{1,0:T(8,128)S(1)} %slice_bitcast_fusion.own), channel_id=1, source_target_pairs={{0,1},{1,0},{2,3},{3,2},{4,5},{5,4},{6,7},{7,6},{8,9},{9,8},{10,11... | collective-permute-start | bytes 98312 | tf_op jit(solution)/shard_map/ppermute | solution.py:518
  45.1 2.1 %collective-permute-start.5 = (f32[64,128]{1,0:T(8,128)S(1)}, f32[64,128]{1,0:T(8,128)S(1)}, u32[]{:S(2)}, u32[]{:S(2)}) collective-permute-start(f32[64,128]{1,0:T(8,128)S(1)} %slice_bitcast_fusion.own), channel_id=1, source_target_pairs={{0,2},{1,3},{2,0},{3,1},{4,6},{5,7},{6,4},{7,5},{8,10},{9,11},{10,... | collective-permute-start | bytes 98312 | tf_op jit(solution)/shard_map/ppermute | solution.py:518
  47.2 0.7 collective-permute-start.6
  47.8 5.8 %flood_kernel.1 = (f32[128,512]{1,0:T(8,128)S(1)}, f32[128,512]{1,0:T(8,128)}, f32[128,512]{1,0:T(8,128)}) custom-call(f32[40,512]{1,0:T(8,128)S(1)} %collective-permute-done.got_a, f32[40,512]{1,0:T(8,128)S(1)} %collective-permute-done.1.got_b, f32[48,128]{1,0:T(8,128)S(1)} %collective-permute-done.2.col_a.order0, ...), custom_call_target="tpu_custom_call" | custom-call | flops 100000000 | bytes 10000000 | tf_op jit(solution)/shard_map/flood_kernel/pallas_call | solution.py:505
  53.7 0.8 %flow_kernel.1 = (f32[32,128]{1,0:T(8,128)S(1)}, f32[32,128]{1,0:T(8,128)S(1)}) custom-call(f32[32,128]{1,0:T(8,128)S(1)} %get-tuple-element.29.source, bf16[32,128,128]{2,1,0:T(8,128)(2,1)S(1)} %copy-done), custom_call_target="tpu_custom_call" | custom-call | flops 100000000 | bytes 1000000 | tf_op jit(solution)/shard_map/flow_kernel/pallas_call | solution.py:514
  54.5 0.0 collective-permute-done.5.two
  54.5 2.8 %paths_kernel.1.reach = f32[128,2048]{1,0:T(8,128)S(1)} custom-call(f32[64,128]{1,0:T(8,128)S(1)} %slice_bitcast_fusion.own, f32[64,128]{1,0:T(8,128)S(1)} %collective-permute-done.4.one, f32[64,128]{1,0:T(8,128)S(1)} %collective-permute-done.5.two, f32[64,128]{1,0:T(8,128)S(1)} %collective-permute-done.6.three), custom_call_target="tpu_custom_call" | custom-call | flops 1000000000 | bytes 1000000 | tf_op jit(solution)/shard_map/paths_kernel/pallas_call | solution.py:519
  57.3 3.1 %all-to-all-done.1 = f32[64,17,1,128]{3,2,1,0:T(1,128)S(1)} async-done(((f32[64,17,1,128]{3,2,1,0:T(1,128)}), f32[64,17,1,128]{3,2,1,0:T(1,128)S(1)}, u32[]{:S(2)}, u32[]{:S(2)}) %all-to-all-start.1) | async-done | bytes 557088 | tf_op jit(solution)/shard_map/all_to_all | solution.py:499
  60.4 0.3 gather_kernel.1.own
  60.7 2.8 %collective-permute-start.7 = (f32[8,128]{1,0:T(8,128)S(1)}, f32[8,128]{1,0:T(8,128)S(1)}, u32[]{:S(2)}, u32[]{:S(2)}) collective-permute-start(f32[8,128]{1,0:T(8,128)S(1)} %gather_kernel.1.own), channel_id=1, source_target_pairs={{0,1},{1,0},{2,3},{3,2},{4,5},{5,4},{6,7},{7,6},{8,9},{9,8},{10,11... | collective-permute-start | bytes 12296 | tf_op jit(solution)/shard_map/ppermute | solution.py:526
  63.4 2.1 %collective-permute-start.8 = (f32[8,128]{1,0:T(8,128)S(1)}, f32[8,128]{1,0:T(8,128)S(1)}, u32[]{:S(2)}, u32[]{:S(2)}) collective-permute-start(f32[8,128]{1,0:T(8,128)S(1)} %gather_kernel.1.own), channel_id=1, source_target_pairs={{0,2},{1,3},{2,0},{3,1},{4,6},{5,7},{6,4},{7,5},{8,10},{9,11},{10,... | collective-permute-start | bytes 12296 | tf_op jit(solution)/shard_map/ppermute | solution.py:526
  65.5 0.7 collective-permute-start.9
  66.2 1.5 %final_kernel.1 = f32[128,512]{1,0:T(8,128)} custom-call(f32[128,512]{1,0:T(8,128)S(1)} %get-tuple-element.22.water, f32[1088,128]{1,0:T(8,128)S(1)} %bitcast.13, f32[8,512]{1,0:T(8,128)S(1)} %copy-done.8), custom_call_target="tpu_custom_call" | custom-call | flops 1000000000 | bytes 1000000 | tf_op jit(solution)/shard_map/final_kernel/pallas_call | solution.py:527
  67.7 0.9 %collective-permute-done.8.two = f32[8,128]{1,0:T(8,128)S(1)} collective-permute-done((f32[8,128]{1,0:T(8,128)S(1)}, f32[8,128]{1,0:T(8,128)S(1)}, u32[]{:S(2)}, u32[]{:S(2)}) %collective-permute-start.8) | collective-permute-done | bytes 4128 | tf_op jit(solution)/shard_map/ppermute | solution.py:526
  68.5 1.8 %collective-permute-done.9.three = f32[8,128]{1,0:T(8,128)S(1)} collective-permute-done((f32[8,128]{1,0:T(8,128)S(1)}, f32[8,128]{1,0:T(8,128)S(1)}, u32[]{:S(2)}, u32[]{:S(2)}) %collective-permute-start.9) | collective-permute-done | bytes 4128 | tf_op jit(solution)/shard_map/ppermute | solution.py:526
  70.3 0.8 %discharge_kernel.1 = f32[32,128]{1,0:T(8,128)} custom-call(f32[32,128]{1,0:T(8,128)S(1)} %get-tuple-element.30.base, f32[32,128]{1,0:T(8,128)S(1)} %get-tuple-element.31.column, f32[8,128]{1,0:T(8,128)S(1)} %gather_kernel.1.own, f32[8,128]{1,0:T(8,128)S(1)} %collective-permute-done.7.one, f32[8,128]{1,0:T(8,128)S(1)} %collective-permute-done.8.two, ...), custom_call_target="tpu_custom_call" | custom-call | flops 10000 | bytes 10000 | tf_op jit(solution)/shard_map/discharge_kernel/pallas_call | solution.py:530
  (23 shorter events, 0.1 us)
Async XLA Ops:
  0.6 20.2 %copy-start.5 = (f32[128,512]{1,0:T(8,128)S(1)}, f32[128,512]{1,0:T(8,128)}, u32[]{:S(2)}) copy-start(f32[128,512]{1,0:T(8,128)} %f4.3) | copy-start | bytes 786436
  3.8 17.0 %copy-start.1 = (f32[128,512]{1,0:T(8,128)S(1)}, f32[128,512]{1,0:T(8,128)}, u32[]{:S(2)}) copy-start(f32[128,512]{1,0:T(8,128)} %f0.3) | copy-start | bytes 786436
  3.8 17.0 %copy-start.2 = (f32[128,512]{1,0:T(8,128)S(1)}, f32[128,512]{1,0:T(8,128)}, u32[]{:S(2)}) copy-start(f32[128,512]{1,0:T(8,128)} %f1.3) | copy-start | bytes 786436
  3.8 17.0 %copy-start.3 = (f32[128,512]{1,0:T(8,128)S(1)}, f32[128,512]{1,0:T(8,128)}, u32[]{:S(2)}) copy-start(f32[128,512]{1,0:T(8,128)} %f2.3) | copy-start | bytes 786436
  3.9 17.0 %copy-start.4 = (f32[128,512]{1,0:T(8,128)S(1)}, f32[128,512]{1,0:T(8,128)}, u32[]{:S(2)}) copy-start(f32[128,512]{1,0:T(8,128)} %f3.3) | copy-start | bytes 786436
  3.9 30.4 %all-to-all-start = ((f32[64,17,1,128]{3,2,1,0:T(1,128)}), f32[64,17,1,128]{3,2,1,0:T(1,128)S(1)}, u32[]{:S(2)}, u32[]{:S(2)}) async-start(f32[64,17,1,128]{3,2,1,0:T(1,128)} %bitcast.16), calls=%async_computation | async-start | bytes 1114112 | tf_op jit(solution)/shard_map/all_to_all | solution.py:476
  16.0 4.8 %collective-permute-start = (f32[40,512]{1,0:T(8,128)}, f32[40,512]{1,0:T(8,128)S(1)}, u32[]{:S(2)}, u32[]{:S(2)}) collective-permute-start(f32[40,512]{1,0:T(8,128)} %get-tuple-element.18), channel_id=1, source_target_pairs={{1,0},{0,1},{3,2},{2,3},{5,4},{4,5},{7,6},{6,7},{9,8},{8,9},{11,10... | collective-permute-start | bytes 245768 | tf_op jit(solution)/shard_map/ppermute | solution.py:484
  17.7 16.6 %copy-start.6 = (f32[32,128]{1,0:T(8,128)S(1)}, f32[32,128]{1,0:T(8,128)}, u32[]{:S(2)}) copy-start(f32[32,128]{1,0:T(8,128)} %section.1) | copy-start | bytes 49156
  17.7 16.6 %copy-start.7 = (f32[32,128]{1,0:T(8,128)S(1)}, f32[32,128]{1,0:T(8,128)}, u32[]{:S(2)}) copy-start(f32[32,128]{1,0:T(8,128)} %reach_source.1) | copy-start | bytes 49156
  17.7 16.6 %copy-start.9 = (f32[32,128]{1,0:T(8,128)S(1)}, f32[32,128]{1,0:T(8,128)}, u32[]{:S(2)}) copy-start(f32[32,128]{1,0:T(8,128)} %get-tuple-element.24.last_row) | copy-start | bytes 49156
  17.7 3.1 %collective-permute-start.1 = (f32[40,512]{1,0:T(8,128)}, f32[40,512]{1,0:T(8,128)S(1)}, u32[]{:S(2)}, u32[]{:S(2)}) collective-permute-start(f32[40,512]{1,0:T(8,128)} %get-tuple-element.19), channel_id=1, source_target_pairs={{2,1},{1,2},{6,5},{5,6},{10,9},{9,10},{14,13},{13,14},{18,17},{17,... | collective-permute-start | bytes 245768 | tf_op jit(solution)/shard_map/ppermute | solution.py:485
  21.1 2.5 %collective-permute-start.2 = (f32[48,128]{1,0:T(8,128)S(1)}, f32[48,128]{1,0:T(8,128)S(1)}, u32[]{:S(2)}, u32[]{:S(2)}) collective-permute-start(f32[48,128]{1,0:T(8,128)S(1)} %get-tuple-element.20), channel_id=1, source_target_pairs={{4,0},{0,4},{12,8},{8,12},{20,16},{16,20},{28,24},{24,28},{36,32},... | collective-permute-start | bytes 73736 | tf_op jit(solution)/shard_map/ppermute | solution.py:489
  21.2 5.5 %collective-permute-start.3 = (f32[48,128]{1,0:T(8,128)S(1)}, f32[48,128]{1,0:T(8,128)S(1)}, u32[]{:S(2)}, u32[]{:S(2)}) collective-permute-start(f32[48,128]{1,0:T(8,128)S(1)} %get-tuple-element.21), channel_id=1, source_target_pairs={{8,4},{4,8},{16,12},{12,16},{24,20},{20,24},{32,28},{28,32},{40,36... | collective-permute-start | bytes 73736 | tf_op jit(solution)/shard_map/ppermute | solution.py:490
  36.2 24.2 %all-to-all-start.1 = ((f32[64,17,1,128]{3,2,1,0:T(1,128)}), f32[64,17,1,128]{3,2,1,0:T(1,128)S(1)}, u32[]{:S(2)}, u32[]{:S(2)}) async-start(f32[64,17,1,128]{3,2,1,0:T(1,128)} %bitcast.5), calls=%async_computation.1 | async-start | bytes 1114112 | tf_op jit(solution)/shard_map/all_to_all | solution.py:499
  42.2 11.5 %copy-start = (bf16[32,128,128]{2,1,0:T(8,128)(2,1)S(1)}, bf16[32,128,128]{2,1,0:T(8,128)(2,1)}, u32[]{:S(2)}) copy-start(bf16[32,128,128]{2,1,0:T(8,128)(2,1)} %inverse.1) | copy-start | bytes 3145732
  42.2 12.2 %collective-permute-start.4 = (f32[64,128]{1,0:T(8,128)S(1)}, f32[64,128]{1,0:T(8,128)S(1)}, u32[]{:S(2)}, u32[]{:S(2)}) collective-permute-start(f32[64,128]{1,0:T(8,128)S(1)} %slice_bitcast_fusion.own), channel_id=1, source_target_pairs={{0,1},{1,0},{2,3},{3,2},{4,5},{5,4},{6,7},{7,6},{8,9},{9,8},{10,11... | collective-permute-start | bytes 98312 | tf_op jit(solution)/shard_map/ppermute | solution.py:518
  45.1 9.4 %collective-permute-start.5 = (f32[64,128]{1,0:T(8,128)S(1)}, f32[64,128]{1,0:T(8,128)S(1)}, u32[]{:S(2)}, u32[]{:S(2)}) collective-permute-start(f32[64,128]{1,0:T(8,128)S(1)} %slice_bitcast_fusion.own), channel_id=1, source_target_pairs={{0,2},{1,3},{2,0},{3,1},{4,6},{5,7},{6,4},{7,5},{8,10},{9,11},{10,... | collective-permute-start | bytes 98312 | tf_op jit(solution)/shard_map/ppermute | solution.py:518
  47.2 7.4 %collective-permute-start.6 = (f32[64,128]{1,0:T(8,128)S(1)}, f32[64,128]{1,0:T(8,128)S(1)}, u32[]{:S(2)}, u32[]{:S(2)}) collective-permute-start(f32[64,128]{1,0:T(8,128)S(1)} %slice_bitcast_fusion.own), channel_id=1, source_target_pairs={{0,3},{1,2},{2,1},{3,0},{4,7},{5,6},{6,5},{7,4},{8,11},{9,10},{10,... | collective-permute-start | bytes 98312 | tf_op jit(solution)/shard_map/ppermute | solution.py:518
  60.4 5.8 %copy-start.8 = (f32[8,512]{1,0:T(8,128)S(1)}, f32[8,512]{1,0:T(8,128)}, u32[]{:S(2)}) copy-start(f32[8,512]{1,0:T(8,128)} %get-tuple-element.26.slots) | copy-start | bytes 49156
  60.7 7.0 %collective-permute-start.7 = (f32[8,128]{1,0:T(8,128)S(1)}, f32[8,128]{1,0:T(8,128)S(1)}, u32[]{:S(2)}, u32[]{:S(2)}) collective-permute-start(f32[8,128]{1,0:T(8,128)S(1)} %gather_kernel.1.own), channel_id=1, source_target_pairs={{0,1},{1,0},{2,3},{3,2},{4,5},{5,4},{6,7},{7,6},{8,9},{9,8},{10,11... | collective-permute-start | bytes 12296 | tf_op jit(solution)/shard_map/ppermute | solution.py:526
  63.4 5.1 %collective-permute-start.8 = (f32[8,128]{1,0:T(8,128)S(1)}, f32[8,128]{1,0:T(8,128)S(1)}, u32[]{:S(2)}, u32[]{:S(2)}) collective-permute-start(f32[8,128]{1,0:T(8,128)S(1)} %gather_kernel.1.own), channel_id=1, source_target_pairs={{0,2},{1,3},{2,0},{3,1},{4,6},{5,7},{6,4},{7,5},{8,10},{9,11},{10,... | collective-permute-start | bytes 12296 | tf_op jit(solution)/shard_map/ppermute | solution.py:526
  65.5 4.8 %collective-permute-start.9 = (f32[8,128]{1,0:T(8,128)S(1)}, f32[8,128]{1,0:T(8,128)S(1)}, u32[]{:S(2)}, u32[]{:S(2)}) collective-permute-start(f32[8,128]{1,0:T(8,128)S(1)} %gather_kernel.1.own), channel_id=1, source_target_pairs={{0,3},{1,2},{2,1},{3,0},{4,7},{5,6},{6,5},{7,4},{8,11},{9,10},{10,... | collective-permute-start | bytes 12296 | tf_op jit(solution)/shard_map/ppermute | solution.py:526

commit v8 on v7

--- a/solution.py
+++ b/solution.py
@@ -57,8 +57,9 @@
 
 def pack_kernel(
     water_h, bed_h, rows_h, blocks_h, inverse_h, rough_h, east_h, south_h, down_h,
-    out, slots, last_out, edge_a, edge_b,
-    water, bed, link_rows, link_blocks, tails, row_s, down, sems,
+    out_h, slots_h, last_h, edge_a_h, edge_b_h,
+    water, bed, link_rows, link_blocks, tails, row_s, down,
+    out, slots, last_out, edge_a, edge_b, sems, out_sems,
 ):
     blocks_own, reach = last_out.shape
     moves = (
@@ -82,6 +83,12 @@
     copies = [pltpu.make_async_copy(src, dst, sems.at[i]) for i, (src, dst) in enumerate(moves)]
     for copy in copies:
         copy.start()
+    sent = []
+
+    def send(src, dst):
+        sent.append(pltpu.make_async_copy(src, dst, out_sems.at[len(sent)]))
+        sent[-1].start()
+
     copies[0].wait()
     copies[1].wait()
     rows = link_rows[...]
@@ -104,6 +111,7 @@
     lane = iota((links, links), 1).astype(F32)
     slot_of = jnp.sum(jnp.where(place_c == lane, position_c, 0.0), axis=0, keepdims=True)
     slots[...] = jnp.broadcast_to(slot_of, slots.shape)
+    send(slots, slots_h)
     copies[2].wait()
     copies[3].wait()
     level = water[...] + bed[...]
@@ -114,8 +122,6 @@
         [level[:, c * LANES : (c + 1) * LANES] for c in range(groups)], axis=0
     )
     by_block = paired(by_block)
-    hot = iota((out.shape[0], links), 0).astype(F32) == slot_of
-    out[...] = fold(mm(jnp.where(hot, 1.0, 0.0).astype(BF16), by_block))
     dest_hot = (iota((tiles, links), 0).astype(F32) == dest).astype(F32).astype(BF16)
     seat = iota((links, LANES), 1).astype(F32) - float(ID_LANE)
     rank_hot = jnp.where(rank == seat, local_c + 1.0, 0.0)
@@ -124,6 +130,9 @@
         copy.wait()
     last = tails[:, 15, :].astype(F32)
     last_out[...] = last
+    send(last_out, last_h)
+    send(edge_a, edge_a_h)
+    send(edge_b, edge_b_h)
     first = (iota((8, reach), 1) == 0).astype(F32).astype(BF16)
     seated = jnp.concatenate(
         [jnp.zeros((GAIN_LANE, reach), F32), last, jnp.zeros((LANES - GAIN_LANE - blocks_own, reach), F32)],
@@ -132,7 +141,17 @@
     gain = mm(first, seated.astype(BF16), ((1,), (1,)))
     row_s[...] = jnp.zeros(row_s.shape, F32)
     row_s[0:1, 0:blocks_own] = down[...].astype(F32)
-    out[pl.ds(SLOTS, tiles, CHUNK), :] = ids + (row_s[0:1, :] + gain[0:1, :])
+    extras = ids + (row_s[0:1, :] + gain[0:1, :])
+    parts = 4
+    size, chunks = out.shape[0] // parts, tiles // parts
+    for part in range(parts):
+        rows = slice(part * size, (part + 1) * size)
+        hot = (iota((size, links), 0) + part * size).astype(F32) == slot_of
+        out[rows, :] = fold(mm(jnp.where(hot, 1.0, 0.0).astype(BF16), by_block))
+        out[pl.ds(part * size + SLOTS, chunks, CHUNK), :] = extras[part * chunks : (part + 1) * chunks]
+        send(out.at[rows, :], out_h.at[rows, :])
+    for copy in sent:
+        copy.wait()
 
 
 def lateral_kernel(rows_in, section, reach_source, last_row, order0, order1, out, source):
@@ -151,11 +170,13 @@
     seat = jnp.where(lane == within, mm(spread, ids), 0.0)
     block = mm(seat.astype(BF16), jnp.ones((LANES, LANES), BF16)) - 1.0
     hot = (block == lane).astype(F32).astype(BF16)
+    rows = rows_in[...]
+    counted = jnp.concatenate([paired(rows), jnp.ones((total, LANES), BF16)], axis=1)
+    found = mm(hot, counted, ((0,), (0,)))[:blocks]
+    sums = fold(found[:, : 2 * LANES]) - found[:, 2 * LANES :] * section[...]
+    src = reach_source[...] + (RIVER_SHARE * LATERAL_RATE) * sums
     section_in = fold(mm(hot[:, :blocks], paired(section[...])))
-    lateral = jnp.where(block >= 0.0, LATERAL_RATE * (rows_in[...] - section_in), 0.0)
-    out[...] = lateral
-    sums = fold(mm(hot, paired(lateral), ((0,), (0,))))[:blocks]
-    src = reach_source[...] + RIVER_SHARE * sums
+    out[...] = jnp.where(block >= 0.0, LATERAL_RATE * (rows - section_in), 0.0)
     source[...] = src
     ends = jnp.concatenate([src * last_row[...], jnp.zeros((LANES - blocks, LANES), F32)], axis=0)
     ends_hi, ends_lo = halves(ends)
@@ -263,14 +284,16 @@
     out[...] = base[...] + column[...] * inflow
 
 
-def final_kernel(water, returned, slots, out):
-    total = returned.shape[0]
+def hot_kernel(slots, out):
+    slot_c = jnp.transpose(slots[...])[:, 0:1]
+    hot = iota(out.shape, 1).astype(F32) == slot_c
+    out[...] = jnp.where(hot, 1.0, 0.0).astype(BF16)
+
+
+def final_kernel(water, returned, hot, out):
     height = water.shape[0]
     groups = water.shape[1] // LANES
-    slot_c = jnp.transpose(slots[...])[:, 0:1]
-    rows = paired(returned[...])
-    hot = iota((height * groups, total), 1).astype(F32) == slot_c
-    lateral = fold(mm(jnp.where(hot, 1.0, 0.0).astype(BF16), rows))
+    lateral = fold(mm(hot[...], paired(returned[...])))
     for c in range(groups):
         cols = slice(c * LANES, (c + 1) * LANES)
         out[:, cols] = water[:, cols] - PLAIN_SHARE * lateral[c * height : (c + 1) * height]
@@ -416,12 +439,12 @@
     return jax.ShapeDtypeStruct(shape, F32)
 
 
-def call(kernel, out_shape, specs, scratch=(), flops=0, size=0, exps=0, limit=16 * 1024 * 1024):
+def call(kernel, out_shape, specs, scratch=(), flops=0, size=0, exps=0, limit=16 * 1024 * 1024, outside=False):
     return pl.pallas_call(
         kernel,
         out_shape=out_shape,
         in_specs=specs,
-        out_specs=jax.tree.map(lambda _: VMEM, out_shape),
+        out_specs=jax.tree.map(lambda _: HBM if outside else VMEM, out_shape),
         scratch_shapes=list(scratch),
         compiler_params=pltpu.CompilerParams(vmem_limit_bytes=limit),
         cost_estimate=pl.CostEstimate(flops=flops, bytes_accessed=size, transcendentals=exps),
@@ -457,9 +480,16 @@
             pltpu.VMEM((blocks, 16, reach), BF16),
             pltpu.VMEM((8, LANES), F32),
             pltpu.VMEM((1, blocks), jnp.int32),
+            pltpu.VMEM((total, LANES), F32),
+            pltpu.VMEM((8, links), F32),
+            pltpu.VMEM((blocks, reach), F32),
+            pltpu.VMEM((5 * HALO, width), F32),
+            pltpu.VMEM((5 * HALO, width), F32),
             pltpu.SemaphoreType.DMA((12,)),
+            pltpu.SemaphoreType.DMA((8,)),
         ],
         limit=None,
+        outside=True,
         flops=10**9,
         size=10**6,
     )(
@@ -524,9 +554,12 @@
         returned.reshape(total, LANES), reached
     )
     parts = [pushed] + [lax.ppermute(pushed, "band", ring[k]) for k in (1, 2, 3)]
+    hot = call(
+        hot_kernel, jax.ShapeDtypeStruct((links, total), BF16), [VMEM], flops=10**8, size=10**6
+    )(slots)
     final_depth = call(
         final_kernel, shaped(height, width), [VMEM] * 3, flops=10**9, size=10**6
-    )(water_now, returned.reshape(total, LANES), slots)
+    )(water_now, returned.reshape(total, LANES), hot)
     discharge = call(
         discharge_kernel, shaped(blocks, reach), [VMEM] * 6, flops=10**4, size=10**4
     )(base_flow, column, *parts)

time: 71.5 us -> 69.9 us (0.978)
  starting transfers between devices: 34.2 us -> 32.6 us
    ppermute x3, starting transfers between devices: 5.5 us -> 4.69 us  [per_device(): lax.ppermute(pushed, 'band', ring[k])]
    ppermute x3, starting transfers between devices: 5.61 us -> 4.8 us  [per_device(): others = [lax.ppermute(extras, 'band', ring[k]) for k in (1, 2, 3)]]
where the time goes in v8:
time: 69.9 us; the launch traced here: 69.5 us
  starting transfers between devices  32.6 us (47%)
  waiting for transfers between devices  19.1 us (27%)
  Pallas kernels  16.9 us (24%)
  between operations  0.89 us (1%)
    all_to_all x1, starting transfers between devices, per_device(): lax.all_to_all(payload.reshape(tiles, CHUNK, 1, LANES), 'tile', split_axi...  12.2 us
    all_to_all x1, waiting for transfers between devices, per_device(): lax.all_to_all(payload.reshape(tiles, CHUNK, 1, LANES), 'tile', split_axi...  7.61 us
    all_to_all x1, starting transfers between devices, per_device(): lax.all_to_all(answer.reshape(tiles, CHUNK, 1, LANES), 'tile', split_axis...  6.12 us
    pallas_call x1, Pallas kernels, per_device(): call(flood_kernel, (shaped(height, width),) * 3, [VMEM] * 9, scratch=[plt...  5.86 us
    ppermute x3, starting transfers between devices, per_device(): others = [lax.ppermute(extras, 'band', ring[k]) for k in (1, 2, 3)]  4.8 us
    ppermute x3, starting transfers between devices, per_device(): lax.ppermute(pushed, 'band', ring[k])  4.69 us
    all_to_all x1, waiting for transfers between devices, per_device(): lax.all_to_all(answer.reshape(tiles, CHUNK, 1, LANES), 'tile', split_axis...  3.55 us
    ppermute x1, waiting for transfers between devices, per_device(): col_b = lax.ppermute(side_b, 'tile', pairs(tiles, 1))  3.05 us
  transfers between devices with their start and end apart: 12, of which 6 were waited for; matrix products, arithmetic and copies ran while one was open for 0% of the time, Pallas kernels for 16%

profile of v8, /device:TPU:2, one launch (start us, length us, event | category | flops | bytes accessed | tf_op | source)
XLA Modules:
  0.0 69.5 jit_solution(6216872039032820352)
XLA Ops:
  0.6 3.0 %pack_kernel.1 = (f32[1088,128]{1,0:T(8,128)}, f32[8,512]{1,0:T(8,128)}, f32[32,128]{1,0:T(8,128)}, f32[40,512]{1,0:T(8,128)}, f32[40,512]{1,0:T(8,128)}) custom-call(f32[128,512]{1,0:T(8,128)} %f0.3, f32[128,512]{1,0:T(8,128)} %f1.3, s32[1,512]{1,0:T(1,128)} %bitcast.17, s32[1,512]{1,0:T(1,128)} %bitcast.18, bf16[32,128,128]{2,1,0:T(8,128)(2,1)} %inverse.1, ...), custom_call_target="tpu_custom_call" | custom-call | flops 1000000000 | bytes 1000000 | tf_op jit(solution)/shard_map/pack_kernel/pallas_call | solution.py:471
  3.6 0.0 copy-start.2
  3.6 0.0 copy-start.3
  3.7 0.0 copy-start.8
  3.7 0.0 copy-start.9
  3.7 12.2 %all-to-all-start = ((f32[64,17,1,128]{3,2,1,0:T(1,128)}), f32[64,17,1,128]{3,2,1,0:T(1,128)S(1)}, u32[]{:S(2)}, u32[]{:S(2)}) async-start(f32[64,17,1,128]{3,2,1,0:T(1,128)} %bitcast.16), calls=%async_computation | async-start | bytes 1114112 | tf_op jit(solution)/shard_map/all_to_all | solution.py:506
  15.9 1.7 %collective-permute-start = (f32[40,512]{1,0:T(8,128)}, f32[40,512]{1,0:T(8,128)S(1)}, u32[]{:S(2)}, u32[]{:S(2)}) collective-permute-start(f32[40,512]{1,0:T(8,128)} %get-tuple-element.18), channel_id=1, source_target_pairs={{1,0},{0,1},{3,2},{2,3},{5,4},{4,5},{7,6},{6,7},{9,8},{8,9},{11,10... | collective-permute-start | bytes 245768 | tf_op jit(solution)/shard_map/ppermute | solution.py:514
  17.5 0.7 collective-permute-start.1
  18.2 2.5 %collective-permute-done.got_a = f32[40,512]{1,0:T(8,128)S(1)} collective-permute-done((f32[40,512]{1,0:T(8,128)}, f32[40,512]{1,0:T(8,128)S(1)}, u32[]{:S(2)}, u32[]{:S(2)}) %collective-permute-start) | collective-permute-done | bytes 81952 | tf_op jit(solution)/shard_map/ppermute | solution.py:514
  20.7 0.2 strips_kernel.1
  21.0 0.1 collective-permute-start.2
  21.1 2.4 %collective-permute-start.3 = (f32[48,128]{1,0:T(8,128)S(1)}, f32[48,128]{1,0:T(8,128)S(1)}, u32[]{:S(2)}, u32[]{:S(2)}) collective-permute-start(f32[48,128]{1,0:T(8,128)S(1)} %get-tuple-element.21), channel_id=1, source_target_pairs={{8,4},{4,8},{16,12},{12,16},{24,20},{20,24},{32,28},{28,32},{40,36... | collective-permute-start | bytes 73736 | tf_op jit(solution)/shard_map/ppermute | solution.py:520
  23.5 3.0 %collective-permute-done.3.col_b.order1 = f32[48,128]{1,0:T(8,128)S(1)} collective-permute-done((f32[48,128]{1,0:T(8,128)S(1)}, f32[48,128]{1,0:T(8,128)S(1)}, u32[]{:S(2)}, u32[]{:S(2)}) %collective-permute-start.3) | collective-permute-done | bytes 24608 | tf_op jit(solution)/shard_map/ppermute | solution.py:520
  26.5 7.6 %all-to-all-done = f32[64,17,1,128]{3,2,1,0:T(1,128)S(1)} async-done(((f32[64,17,1,128]{3,2,1,0:T(1,128)}), f32[64,17,1,128]{3,2,1,0:T(1,128)S(1)}, u32[]{:S(2)}, u32[]{:S(2)}) %all-to-all-start) | async-done | bytes 557088 | tf_op jit(solution)/shard_map/all_to_all | solution.py:506
  34.1 1.6 %lateral_kernel.1 = (f32[1088,128]{1,0:T(8,128)}, f32[32,128]{1,0:T(8,128)S(1)}) custom-call(f32[1088,128]{1,0:T(8,128)S(1)} %bitcast.14, f32[32,128]{1,0:T(8,128)S(1)} %copy-done.7, f32[32,128]{1,0:T(8,128)S(1)} %copy-done.8, f32[32,128]{1,0:T(8,128)S(1)} %copy-done.9, f32[48,128]{1,0:T(8,128)S(1)} %collective-permute-done.2.col_a.order0, ...), custom_call_target="tpu_custom_call" | custom-call | flops 1000000000 | bytes 1000000 | tf_op jit(solution)/shard_map/lateral_kernel/pallas_call | solution.py:522
  35.8 6.1 %all-to-all-start.1 = ((f32[64,17,1,128]{3,2,1,0:T(1,128)}), f32[64,17,1,128]{3,2,1,0:T(1,128)S(1)}, u32[]{:S(2)}, u32[]{:S(2)}) async-start(f32[64,17,1,128]{3,2,1,0:T(1,128)} %bitcast.5), calls=%async_computation.1 | async-start | bytes 1114112 | tf_op jit(solution)/shard_map/all_to_all | solution.py:529
  41.9 0.1 copy.24
  42.0 3.1 %collective-permute-start.6 = (f32[64,128]{1,0:T(8,128)S(1)}, f32[64,128]{1,0:T(8,128)S(1)}, u32[]{:S(2)}, u32[]{:S(2)}) collective-permute-start(f32[64,128]{1,0:T(8,128)S(1)} %slice_bitcast_fusion.own), channel_id=1, source_target_pairs={{0,3},{1,2},{2,1},{3,0},{4,7},{5,6},{6,5},{7,4},{8,11},{9,10},{10,... | collective-permute-start | bytes 98312 | tf_op jit(solution)/shard_map/ppermute | solution.py:548
  45.1 1.7 %collective-permute-start.5 = (f32[64,128]{1,0:T(8,128)S(1)}, f32[64,128]{1,0:T(8,128)S(1)}, u32[]{:S(2)}, u32[]{:S(2)}) collective-permute-start(f32[64,128]{1,0:T(8,128)S(1)} %slice_bitcast_fusion.own), channel_id=1, source_target_pairs={{0,2},{1,3},{2,0},{3,1},{4,6},{5,7},{6,4},{7,5},{8,10},{9,11},{10,... | collective-permute-start | bytes 98312 | tf_op jit(solution)/shard_map/ppermute | solution.py:548
  46.8 0.4 hot_kernel.1.hot
  47.2 5.9 %flood_kernel.1 = (f32[128,512]{1,0:T(8,128)S(1)}, f32[128,512]{1,0:T(8,128)}, f32[128,512]{1,0:T(8,128)}) custom-call(f32[40,512]{1,0:T(8,128)S(1)} %collective-permute-done.got_a, f32[40,512]{1,0:T(8,128)S(1)} %collective-permute-done.1.got_b, f32[48,128]{1,0:T(8,128)S(1)} %collective-permute-done.2.col_a.order0, ...), custom_call_target="tpu_custom_call" | custom-call | flops 100000000 | bytes 10000000 | tf_op jit(solution)/shard_map/flood_kernel/pallas_call | solution.py:535
  53.0 0.8 %flow_kernel.1 = (f32[32,128]{1,0:T(8,128)S(1)}, f32[32,128]{1,0:T(8,128)S(1)}) custom-call(f32[32,128]{1,0:T(8,128)S(1)} %get-tuple-element.29.source, bf16[32,128,128]{2,1,0:T(8,128)(2,1)S(1)} %copy-done), custom_call_target="tpu_custom_call" | custom-call | flops 100000000 | bytes 1000000 | tf_op jit(solution)/shard_map/flow_kernel/pallas_call | solution.py:544
  53.8 0.0 collective-permute-done.6.three
  53.9 2.8 %paths_kernel.1.reach = f32[128,2048]{1,0:T(8,128)S(1)} custom-call(f32[64,128]{1,0:T(8,128)S(1)} %slice_bitcast_fusion.own, f32[64,128]{1,0:T(8,128)S(1)} %collective-permute-done.4.one, f32[64,128]{1,0:T(8,128)S(1)} %collective-permute-done.5.two, f32[64,128]{1,0:T(8,128)S(1)} %collective-permute-done.6.three), custom_call_target="tpu_custom_call" | custom-call | flops 1000000000 | bytes 1000000 | tf_op jit(solution)/shard_map/paths_kernel/pallas_call | solution.py:549
  56.6 3.6 %all-to-all-done.1 = f32[64,17,1,128]{3,2,1,0:T(1,128)S(1)} async-done(((f32[64,17,1,128]{3,2,1,0:T(1,128)}), f32[64,17,1,128]{3,2,1,0:T(1,128)S(1)}, u32[]{:S(2)}, u32[]{:S(2)}) %all-to-all-start.1) | async-done | bytes 557088 | tf_op jit(solution)/shard_map/all_to_all | solution.py:529
  60.2 0.3 gather_kernel.1.own
  60.4 3.0 %collective-permute-start.9 = (f32[8,128]{1,0:T(8,128)S(1)}, f32[8,128]{1,0:T(8,128)S(1)}, u32[]{:S(2)}, u32[]{:S(2)}) collective-permute-start(f32[8,128]{1,0:T(8,128)S(1)} %gather_kernel.1.own), channel_id=1, source_target_pairs={{0,3},{1,2},{2,1},{3,0},{4,7},{5,6},{6,5},{7,4},{8,11},{9,10},{10,... | collective-permute-start | bytes 12296 | tf_op jit(solution)/shard_map/ppermute | solution.py:556
  63.5 1.7 %collective-permute-start.8 = (f32[8,128]{1,0:T(8,128)S(1)}, f32[8,128]{1,0:T(8,128)S(1)}, u32[]{:S(2)}, u32[]{:S(2)}) collective-permute-start(f32[8,128]{1,0:T(8,128)S(1)} %gather_kernel.1.own), channel_id=1, source_target_pairs={{0,2},{1,3},{2,0},{3,1},{4,6},{5,7},{6,4},{7,5},{8,10},{9,11},{10,... | collective-permute-start | bytes 12296 | tf_op jit(solution)/shard_map/ppermute | solution.py:556
  65.1 1.2 %final_kernel.1 = f32[128,512]{1,0:T(8,128)} custom-call(f32[128,512]{1,0:T(8,128)S(1)} %get-tuple-element.22.water, f32[1088,128]{1,0:T(8,128)S(1)} %bitcast.13, bf16[512,1088]{1,0:T(8,128)(2,1)S(1)} %hot_kernel.1.hot), custom_call_target="tpu_custom_call" | custom-call | flops 1000000000 | bytes 1000000 | tf_op jit(solution)/shard_map/final_kernel/pallas_call | solution.py:560
  66.4 2.2 %collective-permute-done.8.two = f32[8,128]{1,0:T(8,128)S(1)} collective-permute-done((f32[8,128]{1,0:T(8,128)S(1)}, f32[8,128]{1,0:T(8,128)S(1)}, u32[]{:S(2)}, u32[]{:S(2)}) %collective-permute-start.8) | collective-permute-done | bytes 4128 | tf_op jit(solution)/shard_map/ppermute | solution.py:556
  68.6 0.2 collective-permute-done.7.one
  68.7 0.8 %discharge_kernel.1 = f32[32,128]{1,0:T(8,128)} custom-call(f32[32,128]{1,0:T(8,128)S(1)} %get-tuple-element.30.base, f32[32,128]{1,0:T(8,128)S(1)} %get-tuple-element.31.column, f32[8,128]{1,0:T(8,128)S(1)} %gather_kernel.1.own, f32[8,128]{1,0:T(8,128)S(1)} %collective-permute-done.7.one, f32[8,128]{1,0:T(8,128)S(1)} %collective-permute-done.8.two, ...), custom_call_target="tpu_custom_call" | custom-call | flops 10000 | bytes 10000 | tf_op jit(solution)/shard_map/discharge_kernel/pallas_call | solution.py:563
  (24 shorter events, 0.1 us)
Async XLA Ops:
  0.6 20.0 %copy-start.5 = (f32[128,512]{1,0:T(8,128)S(1)}, f32[128,512]{1,0:T(8,128)}, u32[]{:S(2)}) copy-start(f32[128,512]{1,0:T(8,128)} %f4.3) | copy-start | bytes 786436
  3.6 17.1 %copy-start.1 = (f32[128,512]{1,0:T(8,128)S(1)}, f32[128,512]{1,0:T(8,128)}, u32[]{:S(2)}) copy-start(f32[128,512]{1,0:T(8,128)} %f0.3) | copy-start | bytes 786436
  3.6 17.0 %copy-start.2 = (f32[128,512]{1,0:T(8,128)S(1)}, f32[128,512]{1,0:T(8,128)}, u32[]{:S(2)}) copy-start(f32[128,512]{1,0:T(8,128)} %f1.3) | copy-start | bytes 786436
  3.6 17.0 %copy-start.3 = (f32[128,512]{1,0:T(8,128)S(1)}, f32[128,512]{1,0:T(8,128)}, u32[]{:S(2)}) copy-start(f32[128,512]{1,0:T(8,128)} %f2.3) | copy-start | bytes 786436
  3.7 17.0 %copy-start.4 = (f32[128,512]{1,0:T(8,128)S(1)}, f32[128,512]{1,0:T(8,128)}, u32[]{:S(2)}) copy-start(f32[128,512]{1,0:T(8,128)} %f3.3) | copy-start | bytes 786436
  3.7 30.5 %copy-start.7 = (f32[32,128]{1,0:T(8,128)S(1)}, f32[32,128]{1,0:T(8,128)}, u32[]{:S(2)}) copy-start(f32[32,128]{1,0:T(8,128)} %section.1) | copy-start | bytes 49156
  3.7 30.5 %copy-start.8 = (f32[32,128]{1,0:T(8,128)S(1)}, f32[32,128]{1,0:T(8,128)}, u32[]{:S(2)}) copy-start(f32[32,128]{1,0:T(8,128)} %reach_source.1) | copy-start | bytes 49156
  3.7 30.4 %copy-start.9 = (f32[32,128]{1,0:T(8,128)S(1)}, f32[32,128]{1,0:T(8,128)}, u32[]{:S(2)}) copy-start(f32[32,128]{1,0:T(8,128)} %get-tuple-element.24.last_row) | copy-start | bytes 49156
  3.7 30.4 %all-to-all-start = ((f32[64,17,1,128]{3,2,1,0:T(1,128)}), f32[64,17,1,128]{3,2,1,0:T(1,128)S(1)}, u32[]{:S(2)}, u32[]{:S(2)}) async-start(f32[64,17,1,128]{3,2,1,0:T(1,128)} %bitcast.16), calls=%async_computation | async-start | bytes 1114112 | tf_op jit(solution)/shard_map/all_to_all | solution.py:506
  15.9 4.8 %collective-permute-start = (f32[40,512]{1,0:T(8,128)}, f32[40,512]{1,0:T(8,128)S(1)}, u32[]{:S(2)}, u32[]{:S(2)}) collective-permute-start(f32[40,512]{1,0:T(8,128)} %get-tuple-element.18), channel_id=1, source_target_pairs={{1,0},{0,1},{3,2},{2,3},{5,4},{4,5},{7,6},{6,7},{9,8},{8,9},{11,10... | collective-permute-start | bytes 245768 | tf_op jit(solution)/shard_map/ppermute | solution.py:514
  17.5 3.1 %collective-permute-start.1 = (f32[40,512]{1,0:T(8,128)}, f32[40,512]{1,0:T(8,128)S(1)}, u32[]{:S(2)}, u32[]{:S(2)}) collective-permute-start(f32[40,512]{1,0:T(8,128)} %get-tuple-element.19), channel_id=1, source_target_pairs={{2,1},{1,2},{6,5},{5,6},{10,9},{9,10},{14,13},{13,14},{18,17},{17,... | collective-permute-start | bytes 245768 | tf_op jit(solution)/shard_map/ppermute | solution.py:515
  21.0 2.5 %collective-permute-start.2 = (f32[48,128]{1,0:T(8,128)S(1)}, f32[48,128]{1,0:T(8,128)S(1)}, u32[]{:S(2)}, u32[]{:S(2)}) collective-permute-start(f32[48,128]{1,0:T(8,128)S(1)} %get-tuple-element.20), channel_id=1, source_target_pairs={{4,0},{0,4},{12,8},{8,12},{20,16},{16,20},{28,24},{24,28},{36,32},... | collective-permute-start | bytes 73736 | tf_op jit(solution)/shard_map/ppermute | solution.py:519
  21.1 5.5 %collective-permute-start.3 = (f32[48,128]{1,0:T(8,128)S(1)}, f32[48,128]{1,0:T(8,128)S(1)}, u32[]{:S(2)}, u32[]{:S(2)}) collective-permute-start(f32[48,128]{1,0:T(8,128)S(1)} %get-tuple-element.21), channel_id=1, source_target_pairs={{8,4},{4,8},{16,12},{12,16},{24,20},{20,24},{32,28},{28,32},{40,36... | collective-permute-start | bytes 73736 | tf_op jit(solution)/shard_map/ppermute | solution.py:520
  35.8 11.0 %copy-start.6 = (f32[8,512]{1,0:T(8,128)S(1)}, f32[8,512]{1,0:T(8,128)}, u32[]{:S(2)}) copy-start(f32[8,512]{1,0:T(8,128)} %get-tuple-element.26.slots) | copy-start | bytes 49156
  35.8 24.4 %all-to-all-start.1 = ((f32[64,17,1,128]{3,2,1,0:T(1,128)}), f32[64,17,1,128]{3,2,1,0:T(1,128)S(1)}, u32[]{:S(2)}, u32[]{:S(2)}) async-start(f32[64,17,1,128]{3,2,1,0:T(1,128)} %bitcast.5), calls=%async_computation.1 | async-start | bytes 1114112 | tf_op jit(solution)/shard_map/all_to_all | solution.py:529
  42.0 11.8 %collective-permute-start.6 = (f32[64,128]{1,0:T(8,128)S(1)}, f32[64,128]{1,0:T(8,128)S(1)}, u32[]{:S(2)}, u32[]{:S(2)}) collective-permute-start(f32[64,128]{1,0:T(8,128)S(1)} %slice_bitcast_fusion.own), channel_id=1, source_target_pairs={{0,3},{1,2},{2,1},{3,0},{4,7},{5,6},{6,5},{7,4},{8,11},{9,10},{10,... | collective-permute-start | bytes 98312 | tf_op jit(solution)/shard_map/ppermute | solution.py:548
  45.1 8.8 %collective-permute-start.5 = (f32[64,128]{1,0:T(8,128)S(1)}, f32[64,128]{1,0:T(8,128)S(1)}, u32[]{:S(2)}, u32[]{:S(2)}) collective-permute-start(f32[64,128]{1,0:T(8,128)S(1)} %slice_bitcast_fusion.own), channel_id=1, source_target_pairs={{0,2},{1,3},{2,0},{3,1},{4,6},{5,7},{6,4},{7,5},{8,10},{9,11},{10,... | collective-permute-start | bytes 98312 | tf_op jit(solution)/shard_map/ppermute | solution.py:548
  46.8 7.1 %collective-permute-start.4 = (f32[64,128]{1,0:T(8,128)S(1)}, f32[64,128]{1,0:T(8,128)S(1)}, u32[]{:S(2)}, u32[]{:S(2)}) collective-permute-start(f32[64,128]{1,0:T(8,128)S(1)} %slice_bitcast_fusion.own), channel_id=1, source_target_pairs={{0,1},{1,0},{2,3},{3,2},{4,5},{5,4},{6,7},{7,6},{8,9},{9,8},{10,11... | collective-permute-start | bytes 98312 | tf_op jit(solution)/shard_map/ppermute | solution.py:548
  47.2 5.9 %copy-start = (bf16[32,128,128]{2,1,0:T(8,128)(2,1)S(1)}, bf16[32,128,128]{2,1,0:T(8,128)(2,1)}, u32[]{:S(2)}) copy-start(bf16[32,128,128]{2,1,0:T(8,128)(2,1)} %inverse.1) | copy-start | bytes 3145732
  60.4 5.9 %collective-permute-start.9 = (f32[8,128]{1,0:T(8,128)S(1)}, f32[8,128]{1,0:T(8,128)S(1)}, u32[]{:S(2)}, u32[]{:S(2)}) collective-permute-start(f32[8,128]{1,0:T(8,128)S(1)} %gather_kernel.1.own), channel_id=1, source_target_pairs={{0,3},{1,2},{2,1},{3,0},{4,7},{5,6},{6,5},{7,4},{8,11},{9,10},{10,... | collective-permute-start | bytes 12296 | tf_op jit(solution)/shard_map/ppermute | solution.py:556
  63.5 5.1 %collective-permute-start.8 = (f32[8,128]{1,0:T(8,128)S(1)}, f32[8,128]{1,0:T(8,128)S(1)}, u32[]{:S(2)}, u32[]{:S(2)}) collective-permute-start(f32[8,128]{1,0:T(8,128)S(1)} %gather_kernel.1.own), channel_id=1, source_target_pairs={{0,2},{1,3},{2,0},{3,1},{4,6},{5,7},{6,4},{7,5},{8,10},{9,11},{10,... | collective-permute-start | bytes 12296 | tf_op jit(solution)/shard_map/ppermute | solution.py:556
  65.1 3.6 %collective-permute-start.7 = (f32[8,128]{1,0:T(8,128)S(1)}, f32[8,128]{1,0:T(8,128)S(1)}, u32[]{:S(2)}, u32[]{:S(2)}) collective-permute-start(f32[8,128]{1,0:T(8,128)S(1)} %gather_kernel.1.own), channel_id=1, source_target_pairs={{0,1},{1,0},{2,3},{3,2},{4,5},{5,4},{6,7},{7,6},{8,9},{9,8},{10,11... | collective-permute-start | bytes 12296 | tf_op jit(solution)/shard_map/ppermute | solution.py:556

commit v9 on v8

--- a/solution.py
+++ b/solution.py
@@ -299,7 +299,7 @@
         out[:, cols] = water[:, cols] - PLAIN_SHARE * lateral[c * height : (c + 1) * height]
 
 
-def strips_kernel(got_a, got_b, f0, f1, f2, f3, f4, side_a, side_b):
+def strips_kernel(got_a, got_b, f0, f1, f2, f3, f4, order, side_a, side_b):
     fields = (f0, f1, f2, f3, f4)
     height, width = f0.shape
     tiles = height // 8 + 2
@@ -513,9 +513,12 @@
 
     got_a = lax.ppermute(edge_a, "band", pairs(bands, 0))
     got_b = lax.ppermute(edge_b, "band", pairs(bands, 1))
+    hot = call(
+        hot_kernel, jax.ShapeDtypeStruct((links, total), BF16), [VMEM], flops=10**8, size=10**6
+    )(slots)
     side_a, side_b = call(
-        strips_kernel, (shaped(48, LANES), shaped(48, LANES)), [VMEM] * 7, flops=10**6, size=10**6
-    )(got_a, got_b, *fields)
+        strips_kernel, (shaped(48, LANES), shaped(48, LANES)), [VMEM] * 7 + [ANY], flops=10**6, size=10**6
+    )(got_a, got_b, *fields, hot)
     col_a = lax.ppermute(side_a, "tile", pairs(tiles, 0))
     col_b = lax.ppermute(side_b, "tile", pairs(tiles, 1))
 
@@ -545,7 +548,7 @@
         flow_kernel, (shaped(blocks, reach),) * 2, [VMEM] * 2, flops=10**8, size=10**6
     )(source, reach_inverse)
     extras = rows_in.reshape(tiles, CHUNK, LANES)[:, SLOTS, :]
-    others = [lax.ppermute(extras, "band", ring[k]) for k in (1, 2, 3)]
+    others = [lax.ppermute(extras, "band", ring[k]) for k in (3, 2, 1)][::-1]
     reached = call(
         paths_kernel, shaped(LANES, tiles * blocks), [VMEM] * 4, flops=10**9, size=10**6
     )(extras, *others)
@@ -553,10 +556,7 @@
     pushed = call(gather_kernel, shaped(8, LANES), [VMEM] * 2, flops=10**6, size=10**6)(
         returned.reshape(total, LANES), reached
     )
-    parts = [pushed] + [lax.ppermute(pushed, "band", ring[k]) for k in (1, 2, 3)]
-    hot = call(
-        hot_kernel, jax.ShapeDtypeStruct((links, total), BF16), [VMEM], flops=10**8, size=10**6
-    )(slots)
+    parts = [pushed] + [lax.ppermute(pushed, "band", ring[k]) for k in (3, 2, 1)]
     final_depth = call(
         final_kernel, shaped(height, width), [VMEM] * 3, flops=10**9, size=10**6
     )(water_now, returned.reshape(total, LANES), hot)

time: 69.9 us -> 69.7 us (level)
  waiting for transfers between devices: 19.1 us -> 17.6 us
  local copies, waits for them, and re-layouts: 0.12 us -> 0.85 us
    ppermute x1, waiting for transfers between devices: 2.47 us -> 1.35 us  [per_device(): got_a = lax.ppermute(edge_a, 'band', pairs(bands, 0))]
    unnamed x20 -> x30, local copies, waits for them, and re-layouts: 0.06 us -> 0.8 us
where the time goes in v9:
time: 69.7 us; the launch traced here: 69.3 us
  starting transfers between devices  33.1 us (47%)
  waiting for transfers between devices  17.6 us (25%)
  Pallas kernels  16.7 us (24%)
  between operations  0.93 us (1%)
  local copies, waits for them, and re-layouts  0.85 us (1%)
    all_to_all x1, starting transfers between devices, per_device(): lax.all_to_all(payload.reshape(tiles, CHUNK, 1, LANES), 'tile', split_axi...  12.2 us
    all_to_all x1, waiting for transfers between devices, per_device(): lax.all_to_all(payload.reshape(tiles, CHUNK, 1, LANES), 'tile', split_axi...  7.61 us
    all_to_all x1, starting transfers between devices, per_device(): lax.all_to_all(answer.reshape(tiles, CHUNK, 1, LANES), 'tile', split_axis...  5.98 us
    pallas_call x1, Pallas kernels, per_device(): call(flood_kernel, (shaped(height, width),) * 3, [VMEM] * 9, scratch=[plt...  5.85 us
    ppermute x3, starting transfers between devices, per_device(): others = [lax.ppermute(extras, 'band', ring[k]) for k in (3, 2, 1)][::-1]  5.48 us
    ppermute x3, starting transfers between devices, per_device(): lax.ppermute(pushed, 'band', ring[k])  4.7 us
    all_to_all x1, waiting for transfers between devices, per_device(): lax.all_to_all(answer.reshape(tiles, CHUNK, 1, LANES), 'tile', split_axis...  3.23 us
    ppermute x1, waiting for transfers between devices, per_device(): col_b = lax.ppermute(side_b, 'tile', pairs(tiles, 1))  3.05 us
  transfers between devices with their start and end apart: 12, of which 6 were waited for; matrix products, arithmetic and copies ran while one was open for 0% of the time, Pallas kernels for 16%

profile of v9, /device:TPU:2, one launch (start us, length us, event | category | flops | bytes accessed | tf_op | source)
XLA Modules:
  0.0 69.3 jit_solution(4219704305443363519)
XLA Ops:
  0.6 2.9 %pack_kernel.1 = (f32[1088,128]{1,0:T(8,128)}, f32[8,512]{1,0:T(8,128)}, f32[32,128]{1,0:T(8,128)}, f32[40,512]{1,0:T(8,128)}, f32[40,512]{1,0:T(8,128)}) custom-call(f32[128,512]{1,0:T(8,128)} %f0.3, f32[128,512]{1,0:T(8,128)} %f1.3, s32[1,512]{1,0:T(1,128)} %bitcast.17, s32[1,512]{1,0:T(1,128)} %bitcast.18, bf16[32,128,128]{2,1,0:T(8,128)(2,1)} %inverse.1, ...), custom_call_target="tpu_custom_call" | custom-call | flops 1000000000 | bytes 1000000 | tf_op jit(solution)/shard_map/pack_kernel/pallas_call | solution.py:471
  3.6 0.0 copy-start.3
  3.6 0.0 copy-start.4
  3.6 12.2 %all-to-all-start = ((f32[64,17,1,128]{3,2,1,0:T(1,128)}), f32[64,17,1,128]{3,2,1,0:T(1,128)S(1)}, u32[]{:S(2)}, u32[]{:S(2)}) async-start(f32[64,17,1,128]{3,2,1,0:T(1,128)} %bitcast.16), calls=%async_computation | async-start | bytes 1114112 | tf_op jit(solution)/shard_map/all_to_all | solution.py:506
  15.8 1.7 %collective-permute-start = (f32[40,512]{1,0:T(8,128)}, f32[40,512]{1,0:T(8,128)S(1)}, u32[]{:S(2)}, u32[]{:S(2)}) collective-permute-start(f32[40,512]{1,0:T(8,128)} %get-tuple-element.18), channel_id=1, source_target_pairs={{1,0},{0,1},{3,2},{2,3},{5,4},{4,5},{7,6},{6,7},{9,8},{8,9},{11,10... | collective-permute-start | bytes 245768 | tf_op jit(solution)/shard_map/ppermute | solution.py:514
  17.5 0.7 collective-permute-start.1
  18.1 0.7 %copy-done.7 = f32[8,512]{1,0:T(8,128)S(1)} copy-done((f32[8,512]{1,0:T(8,128)S(1)}, f32[8,512]{1,0:T(8,128)}, u32[]{:S(2)}) %copy-start.7) | copy-done | bytes 16408
  18.8 0.4 hot_kernel.1.order.hot
  19.3 1.3 %collective-permute-done.got_a = f32[40,512]{1,0:T(8,128)S(1)} collective-permute-done((f32[40,512]{1,0:T(8,128)}, f32[40,512]{1,0:T(8,128)S(1)}, u32[]{:S(2)}, u32[]{:S(2)}) %collective-permute-start) | collective-permute-done | bytes 81952 | tf_op jit(solution)/shard_map/ppermute | solution.py:514
  20.6 0.2 strips_kernel.1
  20.9 0.1 collective-permute-start.2
  21.0 2.4 %collective-permute-start.3 = (f32[48,128]{1,0:T(8,128)S(1)}, f32[48,128]{1,0:T(8,128)S(1)}, u32[]{:S(2)}, u32[]{:S(2)}) collective-permute-start(f32[48,128]{1,0:T(8,128)S(1)} %get-tuple-element.22), channel_id=1, source_target_pairs={{8,4},{4,8},{16,12},{12,16},{24,20},{20,24},{32,28},{28,32},{40,36... | collective-permute-start | bytes 73736 | tf_op jit(solution)/shard_map/ppermute | solution.py:523
  23.4 3.0 %collective-permute-done.3.col_b.order1 = f32[48,128]{1,0:T(8,128)S(1)} collective-permute-done((f32[48,128]{1,0:T(8,128)S(1)}, f32[48,128]{1,0:T(8,128)S(1)}, u32[]{:S(2)}, u32[]{:S(2)}) %collective-permute-start.3) | collective-permute-done | bytes 24608 | tf_op jit(solution)/shard_map/ppermute | solution.py:523
  26.5 7.6 %all-to-all-done = f32[64,17,1,128]{3,2,1,0:T(1,128)S(1)} async-done(((f32[64,17,1,128]{3,2,1,0:T(1,128)}), f32[64,17,1,128]{3,2,1,0:T(1,128)S(1)}, u32[]{:S(2)}, u32[]{:S(2)}) %all-to-all-start) | async-done | bytes 557088 | tf_op jit(solution)/shard_map/all_to_all | solution.py:506
  34.1 1.6 %lateral_kernel.1 = (f32[1088,128]{1,0:T(8,128)}, f32[32,128]{1,0:T(8,128)S(1)}) custom-call(f32[1088,128]{1,0:T(8,128)S(1)} %bitcast.14, f32[32,128]{1,0:T(8,128)S(1)} %copy-done.10, f32[32,128]{1,0:T(8,128)S(1)} %copy-done.11, f32[32,128]{1,0:T(8,128)S(1)} %copy-done.14, f32[48,128]{1,0:T(8,128)S(1)} %collective-permute-done.2.col_a.order0, ...), custom_call_target="tpu_custom_call" | custom-call | flops 1000000000 | bytes 1000000 | tf_op jit(solution)/shard_map/lateral_kernel/pallas_call | solution.py:525
  35.7 6.0 %all-to-all-start.1 = ((f32[64,17,1,128]{3,2,1,0:T(1,128)}), f32[64,17,1,128]{3,2,1,0:T(1,128)S(1)}, u32[]{:S(2)}, u32[]{:S(2)}) async-start(f32[64,17,1,128]{3,2,1,0:T(1,128)} %bitcast.5), calls=%async_computation.1 | async-start | bytes 1114112 | tf_op jit(solution)/shard_map/all_to_all | solution.py:532
  41.7 0.1 copy.24
  41.8 2.7 %collective-permute-start.4 = (f32[64,128]{1,0:T(8,128)S(1)}, f32[64,128]{1,0:T(8,128)S(1)}, u32[]{:S(2)}, u32[]{:S(2)}) collective-permute-start(f32[64,128]{1,0:T(8,128)S(1)} %slice_bitcast_fusion.own), channel_id=1, source_target_pairs={{0,1},{1,0},{2,3},{3,2},{4,5},{5,4},{6,7},{7,6},{8,9},{9,8},{10,11... | collective-permute-start | bytes 98312 | tf_op jit(solution)/shard_map/ppermute | solution.py:551
  44.5 2.1 %collective-permute-start.5 = (f32[64,128]{1,0:T(8,128)S(1)}, f32[64,128]{1,0:T(8,128)S(1)}, u32[]{:S(2)}, u32[]{:S(2)}) collective-permute-start(f32[64,128]{1,0:T(8,128)S(1)} %slice_bitcast_fusion.own), channel_id=1, source_target_pairs={{0,2},{1,3},{2,0},{3,1},{4,6},{5,7},{6,4},{7,5},{8,10},{9,11},{10,... | collective-permute-start | bytes 98312 | tf_op jit(solution)/shard_map/ppermute | solution.py:551
  46.6 0.7 collective-permute-start.6
  47.2 5.8 %flood_kernel.1 = (f32[128,512]{1,0:T(8,128)S(1)}, f32[128,512]{1,0:T(8,128)}, f32[128,512]{1,0:T(8,128)}) custom-call(f32[40,512]{1,0:T(8,128)S(1)} %collective-permute-done.got_a, f32[40,512]{1,0:T(8,128)S(1)} %collective-permute-done.1.got_b, f32[48,128]{1,0:T(8,128)S(1)} %collective-permute-done.2.col_a.order0, f32[48,128]{1,0:T(8,128)S(1)} %copy-done.9, ...), custom_call_target="tpu_custom_call" | custom-call | flops 100000000 | bytes 10000000 | tf_op jit(solution)/shard_map/flood_kernel/pallas_call | solution.py:538
  53.1 0.8 %flow_kernel.1 = (f32[32,128]{1,0:T(8,128)S(1)}, f32[32,128]{1,0:T(8,128)S(1)}) custom-call(f32[32,128]{1,0:T(8,128)S(1)} %get-tuple-element.29.source, bf16[32,128,128]{2,1,0:T(8,128)(2,1)S(1)} %copy-done), custom_call_target="tpu_custom_call" | custom-call | flops 100000000 | bytes 1000000 | tf_op jit(solution)/shard_map/flow_kernel/pallas_call | solution.py:547
  53.9 0.0 collective-permute-done.4.one
  53.9 2.7 %paths_kernel.1.reach = f32[128,2048]{1,0:T(8,128)S(1)} custom-call(f32[64,128]{1,0:T(8,128)S(1)} %slice_bitcast_fusion.own, f32[64,128]{1,0:T(8,128)S(1)} %collective-permute-done.4.one, f32[64,128]{1,0:T(8,128)S(1)} %collective-permute-done.5.two, f32[64,128]{1,0:T(8,128)S(1)} %collective-permute-done.6.three), custom_call_target="tpu_custom_call" | custom-call | flops 1000000000 | bytes 1000000 | tf_op jit(solution)/shard_map/paths_kernel/pallas_call | solution.py:552
  56.7 3.2 %all-to-all-done.1 = f32[64,17,1,128]{3,2,1,0:T(1,128)S(1)} async-done(((f32[64,17,1,128]{3,2,1,0:T(1,128)}), f32[64,17,1,128]{3,2,1,0:T(1,128)S(1)}, u32[]{:S(2)}, u32[]{:S(2)}) %all-to-all-start.1) | async-done | bytes 557088 | tf_op jit(solution)/shard_map/all_to_all | solution.py:532
  59.9 0.3 gather_kernel.1.own
  60.2 3.0 %collective-permute-start.7 = (f32[8,128]{1,0:T(8,128)S(1)}, f32[8,128]{1,0:T(8,128)S(1)}, u32[]{:S(2)}, u32[]{:S(2)}) collective-permute-start(f32[8,128]{1,0:T(8,128)S(1)} %gather_kernel.1.own), channel_id=1, source_target_pairs={{0,3},{1,2},{2,1},{3,0},{4,7},{5,6},{6,5},{7,4},{8,11},{9,10},{10,... | collective-permute-start | bytes 12296 | tf_op jit(solution)/shard_map/ppermute | solution.py:559
  63.2 1.7 %collective-permute-start.8 = (f32[8,128]{1,0:T(8,128)S(1)}, f32[8,128]{1,0:T(8,128)S(1)}, u32[]{:S(2)}, u32[]{:S(2)}) collective-permute-start(f32[8,128]{1,0:T(8,128)S(1)} %gather_kernel.1.own), channel_id=1, source_target_pairs={{0,2},{1,3},{2,0},{3,1},{4,6},{5,7},{6,4},{7,5},{8,10},{9,11},{10,... | collective-permute-start | bytes 12296 | tf_op jit(solution)/shard_map/ppermute | solution.py:559
  64.9 1.2 %final_kernel.1 = f32[128,512]{1,0:T(8,128)} custom-call(f32[128,512]{1,0:T(8,128)S(1)} %copy-done.13, f32[1088,128]{1,0:T(8,128)S(1)} %bitcast.13, bf16[512,1088]{1,0:T(8,128)(2,1)S(1)} %hot_kernel.1.order.hot), custom_call_target="tpu_custom_call" | custom-call | flops 1000000000 | bytes 1000000 | tf_op jit(solution)/shard_map/final_kernel/pallas_call | solution.py:560
  66.1 2.2 %collective-permute-done.8.two = f32[8,128]{1,0:T(8,128)S(1)} collective-permute-done((f32[8,128]{1,0:T(8,128)S(1)}, f32[8,128]{1,0:T(8,128)S(1)}, u32[]{:S(2)}, u32[]{:S(2)}) %collective-permute-start.8) | collective-permute-done | bytes 4128 | tf_op jit(solution)/shard_map/ppermute | solution.py:559
  68.3 0.2 collective-permute-done.9.three
  68.5 0.8 %discharge_kernel.1 = f32[32,128]{1,0:T(8,128)} custom-call(f32[32,128]{1,0:T(8,128)S(1)} %get-tuple-element.30.base, f32[32,128]{1,0:T(8,128)S(1)} %get-tuple-element.31.column, f32[8,128]{1,0:T(8,128)S(1)} %gather_kernel.1.own, f32[8,128]{1,0:T(8,128)S(1)} %collective-permute-done.7.one, f32[8,128]{1,0:T(8,128)S(1)} %collective-permute-done.8.two, ...), custom_call_target="tpu_custom_call" | custom-call | flops 10000 | bytes 10000 | tf_op jit(solution)/shard_map/discharge_kernel/pallas_call | solution.py:563
  (34 shorter events, 0.1 us)
Async XLA Ops:
  3.6 17.0 %copy-start.1 = (f32[128,512]{1,0:T(8,128)S(1)}, f32[128,512]{1,0:T(8,128)}, u32[]{:S(2)}) copy-start(f32[128,512]{1,0:T(8,128)} %f0.3) | copy-start | bytes 786436
  3.6 17.0 %copy-start.2 = (f32[128,512]{1,0:T(8,128)S(1)}, f32[128,512]{1,0:T(8,128)}, u32[]{:S(2)}) copy-start(f32[128,512]{1,0:T(8,128)} %f1.3) | copy-start | bytes 786436
  3.6 17.0 %copy-start.3 = (f32[128,512]{1,0:T(8,128)S(1)}, f32[128,512]{1,0:T(8,128)}, u32[]{:S(2)}) copy-start(f32[128,512]{1,0:T(8,128)} %f2.3) | copy-start | bytes 786436
  3.6 17.0 %copy-start.4 = (f32[128,512]{1,0:T(8,128)S(1)}, f32[128,512]{1,0:T(8,128)}, u32[]{:S(2)}) copy-start(f32[128,512]{1,0:T(8,128)} %f3.3) | copy-start | bytes 786436
  3.6 17.0 %copy-start.5 = (f32[128,512]{1,0:T(8,128)S(1)}, f32[128,512]{1,0:T(8,128)}, u32[]{:S(2)}) copy-start(f32[128,512]{1,0:T(8,128)} %f4.3) | copy-start | bytes 786436
  3.6 30.4 %all-to-all-start = ((f32[64,17,1,128]{3,2,1,0:T(1,128)}), f32[64,17,1,128]{3,2,1,0:T(1,128)S(1)}, u32[]{:S(2)}, u32[]{:S(2)}) async-start(f32[64,17,1,128]{3,2,1,0:T(1,128)} %bitcast.16), calls=%async_computation | async-start | bytes 1114112 | tf_op jit(solution)/shard_map/all_to_all | solution.py:506
  15.8 4.8 %collective-permute-start = (f32[40,512]{1,0:T(8,128)}, f32[40,512]{1,0:T(8,128)S(1)}, u32[]{:S(2)}, u32[]{:S(2)}) collective-permute-start(f32[40,512]{1,0:T(8,128)} %get-tuple-element.18), channel_id=1, source_target_pairs={{1,0},{0,1},{3,2},{2,3},{5,4},{4,5},{7,6},{6,7},{9,8},{8,9},{11,10... | collective-permute-start | bytes 245768 | tf_op jit(solution)/shard_map/ppermute | solution.py:514
  17.5 3.1 %collective-permute-start.1 = (f32[40,512]{1,0:T(8,128)}, f32[40,512]{1,0:T(8,128)S(1)}, u32[]{:S(2)}, u32[]{:S(2)}) collective-permute-start(f32[40,512]{1,0:T(8,128)} %get-tuple-element.19), channel_id=1, source_target_pairs={{2,1},{1,2},{6,5},{5,6},{10,9},{9,10},{14,13},{13,14},{18,17},{17,... | collective-permute-start | bytes 245768 | tf_op jit(solution)/shard_map/ppermute | solution.py:515
  18.1 0.7 %copy-start.7 = (f32[8,512]{1,0:T(8,128)S(1)}, f32[8,512]{1,0:T(8,128)}, u32[]{:S(2)}) copy-start(f32[8,512]{1,0:T(8,128)} %get-tuple-element.20.slots) | copy-start | bytes 49156
  19.2 14.8 %copy-start.10 = (f32[32,128]{1,0:T(8,128)S(1)}, f32[32,128]{1,0:T(8,128)}, u32[]{:S(2)}) copy-start(f32[32,128]{1,0:T(8,128)} %section.1) | copy-start | bytes 49156
  19.2 14.8 %copy-start.11 = (f32[32,128]{1,0:T(8,128)S(1)}, f32[32,128]{1,0:T(8,128)}, u32[]{:S(2)}) copy-start(f32[32,128]{1,0:T(8,128)} %reach_source.1) | copy-start | bytes 49156
  19.2 14.8 %copy-start.14 = (f32[32,128]{1,0:T(8,128)S(1)}, f32[32,128]{1,0:T(8,128)}, u32[]{:S(2)}) copy-start(f32[32,128]{1,0:T(8,128)} %get-tuple-element.25.last_row) | copy-start | bytes 49156
  20.9 2.5 %collective-permute-start.2 = (f32[48,128]{1,0:T(8,128)S(1)}, f32[48,128]{1,0:T(8,128)S(1)}, u32[]{:S(2)}, u32[]{:S(2)}) collective-permute-start(f32[48,128]{1,0:T(8,128)S(1)} %get-tuple-element.21), channel_id=1, source_target_pairs={{4,0},{0,4},{12,8},{8,12},{20,16},{16,20},{28,24},{24,28},{36,32},... | collective-permute-start | bytes 73736 | tf_op jit(solution)/shard_map/ppermute | solution.py:522
  21.0 5.5 %collective-permute-start.3 = (f32[48,128]{1,0:T(8,128)S(1)}, f32[48,128]{1,0:T(8,128)S(1)}, u32[]{:S(2)}, u32[]{:S(2)}) collective-permute-start(f32[48,128]{1,0:T(8,128)S(1)} %get-tuple-element.22), channel_id=1, source_target_pairs={{8,4},{4,8},{16,12},{12,16},{24,20},{20,24},{32,28},{28,32},{40,36... | collective-permute-start | bytes 73736 | tf_op jit(solution)/shard_map/ppermute | solution.py:523
  26.5 9.2 %copy-start.8 = (f32[48,128]{1,0:T(8,128)}, f32[48,128]{1,0:T(8,128)S(1)}, u32[]{:S(2)}) copy-start(f32[48,128]{1,0:T(8,128)S(1)} %collective-permute-done.3.col_b.order1) | copy-start | bytes 73732
  35.7 24.3 %all-to-all-start.1 = ((f32[64,17,1,128]{3,2,1,0:T(1,128)}), f32[64,17,1,128]{3,2,1,0:T(1,128)S(1)}, u32[]{:S(2)}, u32[]{:S(2)}) async-start(f32[64,17,1,128]{3,2,1,0:T(1,128)} %bitcast.5), calls=%async_computation.1 | async-start | bytes 1114112 | tf_op jit(solution)/shard_map/all_to_all | solution.py:532
  41.7 5.6 %copy-start.6 = (f32[128,512]{1,0:T(8,128)S(1)}, f32[128,512]{1,0:T(8,128)}, u32[]{:S(2)}) copy-start(f32[128,512]{1,0:T(8,128)} %f4.3) | copy-start | bytes 786436
  41.7 5.6 %copy-start.9 = (f32[48,128]{1,0:T(8,128)S(1)}, f32[48,128]{1,0:T(8,128)}, u32[]{:S(2)}) copy-start(f32[48,128]{1,0:T(8,128)} %copy-done.8) | copy-start | bytes 73732
  41.8 11.3 %copy-start = (bf16[32,128,128]{2,1,0:T(8,128)(2,1)S(1)}, bf16[32,128,128]{2,1,0:T(8,128)(2,1)}, u32[]{:S(2)}) copy-start(bf16[32,128,128]{2,1,0:T(8,128)(2,1)} %inverse.1) | copy-start | bytes 3145732
  41.8 12.1 %collective-permute-start.4 = (f32[64,128]{1,0:T(8,128)S(1)}, f32[64,128]{1,0:T(8,128)S(1)}, u32[]{:S(2)}, u32[]{:S(2)}) collective-permute-start(f32[64,128]{1,0:T(8,128)S(1)} %slice_bitcast_fusion.own), channel_id=1, source_target_pairs={{0,1},{1,0},{2,3},{3,2},{4,5},{5,4},{6,7},{7,6},{8,9},{9,8},{10,11... | collective-permute-start | bytes 98312 | tf_op jit(solution)/shard_map/ppermute | solution.py:551
  44.5 9.4 %collective-permute-start.5 = (f32[64,128]{1,0:T(8,128)S(1)}, f32[64,128]{1,0:T(8,128)S(1)}, u32[]{:S(2)}, u32[]{:S(2)}) collective-permute-start(f32[64,128]{1,0:T(8,128)S(1)} %slice_bitcast_fusion.own), channel_id=1, source_target_pairs={{0,2},{1,3},{2,0},{3,1},{4,6},{5,7},{6,4},{7,5},{8,10},{9,11},{10,... | collective-permute-start | bytes 98312 | tf_op jit(solution)/shard_map/ppermute | solution.py:551
  46.6 7.4 %collective-permute-start.6 = (f32[64,128]{1,0:T(8,128)S(1)}, f32[64,128]{1,0:T(8,128)S(1)}, u32[]{:S(2)}, u32[]{:S(2)}) collective-permute-start(f32[64,128]{1,0:T(8,128)S(1)} %slice_bitcast_fusion.own), channel_id=1, source_target_pairs={{0,3},{1,2},{2,1},{3,0},{4,7},{5,6},{6,5},{7,4},{8,11},{9,10},{10,... | collective-permute-start | bytes 98312 | tf_op jit(solution)/shard_map/ppermute | solution.py:551
  53.1 0.8 %copy-start.12 = (f32[128,512]{1,0:T(8,128)}, f32[128,512]{1,0:T(8,128)S(1)}, u32[]{:S(2)}) copy-start(f32[128,512]{1,0:T(8,128)S(1)} %get-tuple-element.23.water) | copy-start | bytes 786436
  56.7 8.2 %copy-start.13 = (f32[128,512]{1,0:T(8,128)S(1)}, f32[128,512]{1,0:T(8,128)}, u32[]{:S(2)}) copy-start(f32[128,512]{1,0:T(8,128)} %copy-done.12) | copy-start | bytes 786436
  60.2 5.9 %collective-permute-start.7 = (f32[8,128]{1,0:T(8,128)S(1)}, f32[8,128]{1,0:T(8,128)S(1)}, u32[]{:S(2)}, u32[]{:S(2)}) collective-permute-start(f32[8,128]{1,0:T(8,128)S(1)} %gather_kernel.1.own), channel_id=1, source_target_pairs={{0,3},{1,2},{2,1},{3,0},{4,7},{5,6},{6,5},{7,4},{8,11},{9,10},{10,... | collective-permute-start | bytes 12296 | tf_op jit(solution)/shard_map/ppermute | solution.py:559
  63.2 5.1 %collective-permute-start.8 = (f32[8,128]{1,0:T(8,128)S(1)}, f32[8,128]{1,0:T(8,128)S(1)}, u32[]{:S(2)}, u32[]{:S(2)}) collective-permute-start(f32[8,128]{1,0:T(8,128)S(1)} %gather_kernel.1.own), channel_id=1, source_target_pairs={{0,2},{1,3},{2,0},{3,1},{4,6},{5,7},{6,4},{7,5},{8,10},{9,11},{10,... | collective-permute-start | bytes 12296 | tf_op jit(solution)/shard_map/ppermute | solution.py:559
  64.9 3.6 %collective-permute-start.9 = (f32[8,128]{1,0:T(8,128)S(1)}, f32[8,128]{1,0:T(8,128)S(1)}, u32[]{:S(2)}, u32[]{:S(2)}) collective-permute-start(f32[8,128]{1,0:T(8,128)S(1)} %gather_kernel.1.own), channel_id=1, source_target_pairs={{0,1},{1,0},{2,3},{3,2},{4,5},{5,4},{6,7},{7,6},{8,9},{9,8},{10,11... | collective-permute-start | bytes 12296 | tf_op jit(solution)/shard_map/ppermute | solution.py:559

commit v10 on v9

--- a/solution.py
+++ b/solution.py
@@ -1,5 +1,3 @@
-import functools
-
 import jax
 import jax.numpy as jnp
 from jax import lax
@@ -128,7 +126,7 @@
     ids = mm(dest_hot, rank_hot.astype(BF16))
     for copy in copies[4:]:
         copy.wait()
-    last = tails[:, 15, :].astype(F32)
+    last = tails[...].astype(F32)[:, 15, :]
     last_out[...] = last
     send(last_out, last_h)
     send(edge_a, edge_a_h)

time: 69.7 us -> 69.7 us (level)
  no operation moved by 1% of the time
where the time goes in v10:
time: 69.7 us; the launch traced here: 69.3 us
  starting transfers between devices  33.1 us (47%)
  waiting for transfers between devices  17.6 us (25%)
  Pallas kernels  16.8 us (24%)
  between operations  0.93 us (1%)
  local copies, waits for them, and re-layouts  0.85 us (1%)
    all_to_all x1, starting transfers between devices, per_device(): lax.all_to_all(payload.reshape(tiles, CHUNK, 1, LANES), 'tile', split_axi...  12.2 us
    all_to_all x1, waiting for transfers between devices, per_device(): lax.all_to_all(payload.reshape(tiles, CHUNK, 1, LANES), 'tile', split_axi...  7.61 us
    all_to_all x1, starting transfers between devices, per_device(): lax.all_to_all(answer.reshape(tiles, CHUNK, 1, LANES), 'tile', split_axis...  5.98 us
    pallas_call x1, Pallas kernels, per_device(): call(flood_kernel, (shaped(height, width),) * 3, [VMEM] * 9, scratch=[plt...  5.85 us
    ppermute x3, starting transfers between devices, per_device(): others = [lax.ppermute(extras, 'band', ring[k]) for k in (3, 2, 1)][::-1]  5.48 us
    ppermute x3, starting transfers between devices, per_device(): lax.ppermute(pushed, 'band', ring[k])  4.7 us
    all_to_all x1, waiting for transfers between devices, per_device(): lax.all_to_all(answer.reshape(tiles, CHUNK, 1, LANES), 'tile', split_axis...  3.2 us
    ppermute x1, waiting for transfers between devices, per_device(): col_b = lax.ppermute(side_b, 'tile', pairs(tiles, 1))  3.05 us
  transfers between devices with their start and end apart: 12, of which 6 were waited for; matrix products, arithmetic and copies ran while one was open for 0% of the time, Pallas kernels for 16%

profile of v10, /device:TPU:2, one launch (start us, length us, event | category | flops | bytes accessed | tf_op | source)
XLA Modules:
  0.0 69.3 jit_solution(5583132237160977632)
XLA Ops:
  0.6 2.9 %pack_kernel.1 = (f32[1088,128]{1,0:T(8,128)}, f32[8,512]{1,0:T(8,128)}, f32[32,128]{1,0:T(8,128)}, f32[40,512]{1,0:T(8,128)}, f32[40,512]{1,0:T(8,128)}) custom-call(f32[128,512]{1,0:T(8,128)} %f0.3, f32[128,512]{1,0:T(8,128)} %f1.3, s32[1,512]{1,0:T(1,128)} %bitcast.17, s32[1,512]{1,0:T(1,128)} %bitcast.18, bf16[32,128,128]{2,1,0:T(8,128)(2,1)} %inverse.1, ...), custom_call_target="tpu_custom_call" | custom-call | flops 1000000000 | bytes 1000000 | tf_op jit(solution)/shard_map/pack_kernel/pallas_call | solution.py:469
  3.6 0.0 copy-start.1
  3.6 0.0 copy-start.2
  3.6 12.2 %all-to-all-start = ((f32[64,17,1,128]{3,2,1,0:T(1,128)}), f32[64,17,1,128]{3,2,1,0:T(1,128)S(1)}, u32[]{:S(2)}, u32[]{:S(2)}) async-start(f32[64,17,1,128]{3,2,1,0:T(1,128)} %bitcast.16), calls=%async_computation | async-start | bytes 1114112 | tf_op jit(solution)/shard_map/all_to_all | solution.py:504
  15.8 1.7 %collective-permute-start = (f32[40,512]{1,0:T(8,128)}, f32[40,512]{1,0:T(8,128)S(1)}, u32[]{:S(2)}, u32[]{:S(2)}) collective-permute-start(f32[40,512]{1,0:T(8,128)} %get-tuple-element.18), channel_id=1, source_target_pairs={{1,0},{0,1},{3,2},{2,3},{5,4},{4,5},{7,6},{6,7},{9,8},{8,9},{11,10... | collective-permute-start | bytes 245768 | tf_op jit(solution)/shard_map/ppermute | solution.py:512
  17.5 0.7 collective-permute-start.1
  18.1 0.7 %copy-done.7 = f32[8,512]{1,0:T(8,128)S(1)} copy-done((f32[8,512]{1,0:T(8,128)S(1)}, f32[8,512]{1,0:T(8,128)}, u32[]{:S(2)}) %copy-start.7) | copy-done | bytes 16408
  18.8 0.4 hot_kernel.1.order.hot
  19.2 1.3 %collective-permute-done.got_a = f32[40,512]{1,0:T(8,128)S(1)} collective-permute-done((f32[40,512]{1,0:T(8,128)}, f32[40,512]{1,0:T(8,128)S(1)}, u32[]{:S(2)}, u32[]{:S(2)}) %collective-permute-start) | collective-permute-done | bytes 81952 | tf_op jit(solution)/shard_map/ppermute | solution.py:512
  20.6 0.2 strips_kernel.1
  20.9 0.1 collective-permute-start.2
  21.0 2.4 %collective-permute-start.3 = (f32[48,128]{1,0:T(8,128)S(1)}, f32[48,128]{1,0:T(8,128)S(1)}, u32[]{:S(2)}, u32[]{:S(2)}) collective-permute-start(f32[48,128]{1,0:T(8,128)S(1)} %get-tuple-element.22), channel_id=1, source_target_pairs={{8,4},{4,8},{16,12},{12,16},{24,20},{20,24},{32,28},{28,32},{40,36... | collective-permute-start | bytes 73736 | tf_op jit(solution)/shard_map/ppermute | solution.py:521
  23.4 3.0 %collective-permute-done.3.col_b.order1 = f32[48,128]{1,0:T(8,128)S(1)} collective-permute-done((f32[48,128]{1,0:T(8,128)S(1)}, f32[48,128]{1,0:T(8,128)S(1)}, u32[]{:S(2)}, u32[]{:S(2)}) %collective-permute-start.3) | collective-permute-done | bytes 24608 | tf_op jit(solution)/shard_map/ppermute | solution.py:521
  26.5 7.6 %all-to-all-done = f32[64,17,1,128]{3,2,1,0:T(1,128)S(1)} async-done(((f32[64,17,1,128]{3,2,1,0:T(1,128)}), f32[64,17,1,128]{3,2,1,0:T(1,128)S(1)}, u32[]{:S(2)}, u32[]{:S(2)}) %all-to-all-start) | async-done | bytes 557088 | tf_op jit(solution)/shard_map/all_to_all | solution.py:504
  34.1 1.6 %lateral_kernel.1 = (f32[1088,128]{1,0:T(8,128)}, f32[32,128]{1,0:T(8,128)S(1)}) custom-call(f32[1088,128]{1,0:T(8,128)S(1)} %bitcast.14, f32[32,128]{1,0:T(8,128)S(1)} %copy-done.10, f32[32,128]{1,0:T(8,128)S(1)} %copy-done.11, f32[32,128]{1,0:T(8,128)S(1)} %copy-done.14, f32[48,128]{1,0:T(8,128)S(1)} %collective-permute-done.2.col_a.order0, ...), custom_call_target="tpu_custom_call" | custom-call | flops 1000000000 | bytes 1000000 | tf_op jit(solution)/shard_map/lateral_kernel/pallas_call | solution.py:523
  35.7 6.0 %all-to-all-start.1 = ((f32[64,17,1,128]{3,2,1,0:T(1,128)}), f32[64,17,1,128]{3,2,1,0:T(1,128)S(1)}, u32[]{:S(2)}, u32[]{:S(2)}) async-start(f32[64,17,1,128]{3,2,1,0:T(1,128)} %bitcast.5), calls=%async_computation.1 | async-start | bytes 1114112 | tf_op jit(solution)/shard_map/all_to_all | solution.py:530
  41.7 0.1 copy.24
  41.8 2.7 %collective-permute-start.4 = (f32[64,128]{1,0:T(8,128)S(1)}, f32[64,128]{1,0:T(8,128)S(1)}, u32[]{:S(2)}, u32[]{:S(2)}) collective-permute-start(f32[64,128]{1,0:T(8,128)S(1)} %slice_bitcast_fusion.own), channel_id=1, source_target_pairs={{0,1},{1,0},{2,3},{3,2},{4,5},{5,4},{6,7},{7,6},{8,9},{9,8},{10,11... | collective-permute-start | bytes 98312 | tf_op jit(solution)/shard_map/ppermute | solution.py:549
  44.5 2.1 %collective-permute-start.5 = (f32[64,128]{1,0:T(8,128)S(1)}, f32[64,128]{1,0:T(8,128)S(1)}, u32[]{:S(2)}, u32[]{:S(2)}) collective-permute-start(f32[64,128]{1,0:T(8,128)S(1)} %slice_bitcast_fusion.own), channel_id=1, source_target_pairs={{0,2},{1,3},{2,0},{3,1},{4,6},{5,7},{6,4},{7,5},{8,10},{9,11},{10,... | collective-permute-start | bytes 98312 | tf_op jit(solution)/shard_map/ppermute | solution.py:549
  46.6 0.7 collective-permute-start.6
  47.2 5.8 %flood_kernel.1 = (f32[128,512]{1,0:T(8,128)S(1)}, f32[128,512]{1,0:T(8,128)}, f32[128,512]{1,0:T(8,128)}) custom-call(f32[40,512]{1,0:T(8,128)S(1)} %collective-permute-done.got_a, f32[40,512]{1,0:T(8,128)S(1)} %collective-permute-done.1.got_b, f32[48,128]{1,0:T(8,128)S(1)} %collective-permute-done.2.col_a.order0, f32[48,128]{1,0:T(8,128)S(1)} %copy-done.9, ...), custom_call_target="tpu_custom_call" | custom-call | flops 100000000 | bytes 10000000 | tf_op jit(solution)/shard_map/flood_kernel/pallas_call | solution.py:536
  53.1 0.8 %flow_kernel.1 = (f32[32,128]{1,0:T(8,128)S(1)}, f32[32,128]{1,0:T(8,128)S(1)}) custom-call(f32[32,128]{1,0:T(8,128)S(1)} %get-tuple-element.29.source, bf16[32,128,128]{2,1,0:T(8,128)(2,1)S(1)} %copy-done), custom_call_target="tpu_custom_call" | custom-call | flops 100000000 | bytes 1000000 | tf_op jit(solution)/shard_map/flow_kernel/pallas_call | solution.py:545
  53.9 0.0 collective-permute-done.5.two
  53.9 2.8 %paths_kernel.1.reach = f32[128,2048]{1,0:T(8,128)S(1)} custom-call(f32[64,128]{1,0:T(8,128)S(1)} %slice_bitcast_fusion.own, f32[64,128]{1,0:T(8,128)S(1)} %collective-permute-done.4.one, f32[64,128]{1,0:T(8,128)S(1)} %collective-permute-done.5.two, f32[64,128]{1,0:T(8,128)S(1)} %collective-permute-done.6.three), custom_call_target="tpu_custom_call" | custom-call | flops 1000000000 | bytes 1000000 | tf_op jit(solution)/shard_map/paths_kernel/pallas_call | solution.py:550
  56.7 3.2 %all-to-all-done.1 = f32[64,17,1,128]{3,2,1,0:T(1,128)S(1)} async-done(((f32[64,17,1,128]{3,2,1,0:T(1,128)}), f32[64,17,1,128]{3,2,1,0:T(1,128)S(1)}, u32[]{:S(2)}, u32[]{:S(2)}) %all-to-all-start.1) | async-done | bytes 557088 | tf_op jit(solution)/shard_map/all_to_all | solution.py:530
  59.9 0.3 gather_kernel.1.own
  60.2 3.0 %collective-permute-start.7 = (f32[8,128]{1,0:T(8,128)S(1)}, f32[8,128]{1,0:T(8,128)S(1)}, u32[]{:S(2)}, u32[]{:S(2)}) collective-permute-start(f32[8,128]{1,0:T(8,128)S(1)} %gather_kernel.1.own), channel_id=1, source_target_pairs={{0,3},{1,2},{2,1},{3,0},{4,7},{5,6},{6,5},{7,4},{8,11},{9,10},{10,... | collective-permute-start | bytes 12296 | tf_op jit(solution)/shard_map/ppermute | solution.py:557
  63.2 1.7 %collective-permute-start.8 = (f32[8,128]{1,0:T(8,128)S(1)}, f32[8,128]{1,0:T(8,128)S(1)}, u32[]{:S(2)}, u32[]{:S(2)}) collective-permute-start(f32[8,128]{1,0:T(8,128)S(1)} %gather_kernel.1.own), channel_id=1, source_target_pairs={{0,2},{1,3},{2,0},{3,1},{4,6},{5,7},{6,4},{7,5},{8,10},{9,11},{10,... | collective-permute-start | bytes 12296 | tf_op jit(solution)/shard_map/ppermute | solution.py:557
  64.9 1.2 %final_kernel.1 = f32[128,512]{1,0:T(8,128)} custom-call(f32[128,512]{1,0:T(8,128)S(1)} %copy-done.13, f32[1088,128]{1,0:T(8,128)S(1)} %bitcast.13, bf16[512,1088]{1,0:T(8,128)(2,1)S(1)} %hot_kernel.1.order.hot), custom_call_target="tpu_custom_call" | custom-call | flops 1000000000 | bytes 1000000 | tf_op jit(solution)/shard_map/final_kernel/pallas_call | solution.py:558
  66.1 2.2 %collective-permute-done.8.two = f32[8,128]{1,0:T(8,128)S(1)} collective-permute-done((f32[8,128]{1,0:T(8,128)S(1)}, f32[8,128]{1,0:T(8,128)S(1)}, u32[]{:S(2)}, u32[]{:S(2)}) %collective-permute-start.8) | collective-permute-done | bytes 4128 | tf_op jit(solution)/shard_map/ppermute | solution.py:557
  68.3 0.2 collective-permute-done.9.three
  68.5 0.8 %discharge_kernel.1 = f32[32,128]{1,0:T(8,128)} custom-call(f32[32,128]{1,0:T(8,128)S(1)} %get-tuple-element.30.base, f32[32,128]{1,0:T(8,128)S(1)} %get-tuple-element.31.column, f32[8,128]{1,0:T(8,128)S(1)} %gather_kernel.1.own, f32[8,128]{1,0:T(8,128)S(1)} %collective-permute-done.7.one, f32[8,128]{1,0:T(8,128)S(1)} %collective-permute-done.8.two, ...), custom_call_target="tpu_custom_call" | custom-call | flops 10000 | bytes 10000 | tf_op jit(solution)/shard_map/discharge_kernel/pallas_call | solution.py:561
  (34 shorter events, 0.1 us)
Async XLA Ops:
  3.6 17.0 %copy-start.1 = (f32[128,512]{1,0:T(8,128)S(1)}, f32[128,512]{1,0:T(8,128)}, u32[]{:S(2)}) copy-start(f32[128,512]{1,0:T(8,128)} %f0.3) | copy-start | bytes 786436
  3.6 17.0 %copy-start.2 = (f32[128,512]{1,0:T(8,128)S(1)}, f32[128,512]{1,0:T(8,128)}, u32[]{:S(2)}) copy-start(f32[128,512]{1,0:T(8,128)} %f1.3) | copy-start | bytes 786436
  3.6 17.0 %copy-start.3 = (f32[128,512]{1,0:T(8,128)S(1)}, f32[128,512]{1,0:T(8,128)}, u32[]{:S(2)}) copy-start(f32[128,512]{1,0:T(8,128)} %f2.3) | copy-start | bytes 786436
  3.6 17.0 %copy-start.4 = (f32[128,512]{1,0:T(8,128)S(1)}, f32[128,512]{1,0:T(8,128)}, u32[]{:S(2)}) copy-start(f32[128,512]{1,0:T(8,128)} %f3.3) | copy-start | bytes 786436
  3.6 17.0 %copy-start.5 = (f32[128,512]{1,0:T(8,128)S(1)}, f32[128,512]{1,0:T(8,128)}, u32[]{:S(2)}) copy-start(f32[128,512]{1,0:T(8,128)} %f4.3) | copy-start | bytes 786436
  3.6 30.4 %all-to-all-start = ((f32[64,17,1,128]{3,2,1,0:T(1,128)}), f32[64,17,1,128]{3,2,1,0:T(1,128)S(1)}, u32[]{:S(2)}, u32[]{:S(2)}) async-start(f32[64,17,1,128]{3,2,1,0:T(1,128)} %bitcast.16), calls=%async_computation | async-start | bytes 1114112 | tf_op jit(solution)/shard_map/all_to_all | solution.py:504
  15.8 4.8 %collective-permute-start = (f32[40,512]{1,0:T(8,128)}, f32[40,512]{1,0:T(8,128)S(1)}, u32[]{:S(2)}, u32[]{:S(2)}) collective-permute-start(f32[40,512]{1,0:T(8,128)} %get-tuple-element.18), channel_id=1, source_target_pairs={{1,0},{0,1},{3,2},{2,3},{5,4},{4,5},{7,6},{6,7},{9,8},{8,9},{11,10... | collective-permute-start | bytes 245768 | tf_op jit(solution)/shard_map/ppermute | solution.py:512
  17.5 3.1 %collective-permute-start.1 = (f32[40,512]{1,0:T(8,128)}, f32[40,512]{1,0:T(8,128)S(1)}, u32[]{:S(2)}, u32[]{:S(2)}) collective-permute-start(f32[40,512]{1,0:T(8,128)} %get-tuple-element.19), channel_id=1, source_target_pairs={{2,1},{1,2},{6,5},{5,6},{10,9},{9,10},{14,13},{13,14},{18,17},{17,... | collective-permute-start | bytes 245768 | tf_op jit(solution)/shard_map/ppermute | solution.py:513
  18.1 0.7 %copy-start.7 = (f32[8,512]{1,0:T(8,128)S(1)}, f32[8,512]{1,0:T(8,128)}, u32[]{:S(2)}) copy-start(f32[8,512]{1,0:T(8,128)} %get-tuple-element.20.slots) | copy-start | bytes 49156
  19.2 14.8 %copy-start.10 = (f32[32,128]{1,0:T(8,128)S(1)}, f32[32,128]{1,0:T(8,128)}, u32[]{:S(2)}) copy-start(f32[32,128]{1,0:T(8,128)} %section.1) | copy-start | bytes 49156
  19.2 14.8 %copy-start.11 = (f32[32,128]{1,0:T(8,128)S(1)}, f32[32,128]{1,0:T(8,128)}, u32[]{:S(2)}) copy-start(f32[32,128]{1,0:T(8,128)} %reach_source.1) | copy-start | bytes 49156
  19.2 14.8 %copy-start.14 = (f32[32,128]{1,0:T(8,128)S(1)}, f32[32,128]{1,0:T(8,128)}, u32[]{:S(2)}) copy-start(f32[32,128]{1,0:T(8,128)} %get-tuple-element.25.last_row) | copy-start | bytes 49156
  20.9 2.5 %collective-permute-start.2 = (f32[48,128]{1,0:T(8,128)S(1)}, f32[48,128]{1,0:T(8,128)S(1)}, u32[]{:S(2)}, u32[]{:S(2)}) collective-permute-start(f32[48,128]{1,0:T(8,128)S(1)} %get-tuple-element.21), channel_id=1, source_target_pairs={{4,0},{0,4},{12,8},{8,12},{20,16},{16,20},{28,24},{24,28},{36,32},... | collective-permute-start | bytes 73736 | tf_op jit(solution)/shard_map/ppermute | solution.py:520
  21.0 5.5 %collective-permute-start.3 = (f32[48,128]{1,0:T(8,128)S(1)}, f32[48,128]{1,0:T(8,128)S(1)}, u32[]{:S(2)}, u32[]{:S(2)}) collective-permute-start(f32[48,128]{1,0:T(8,128)S(1)} %get-tuple-element.22), channel_id=1, source_target_pairs={{8,4},{4,8},{16,12},{12,16},{24,20},{20,24},{32,28},{28,32},{40,36... | collective-permute-start | bytes 73736 | tf_op jit(solution)/shard_map/ppermute | solution.py:521
  26.5 9.2 %copy-start.8 = (f32[48,128]{1,0:T(8,128)}, f32[48,128]{1,0:T(8,128)S(1)}, u32[]{:S(2)}) copy-start(f32[48,128]{1,0:T(8,128)S(1)} %collective-permute-done.3.col_b.order1) | copy-start | bytes 73732
  35.7 24.3 %all-to-all-start.1 = ((f32[64,17,1,128]{3,2,1,0:T(1,128)}), f32[64,17,1,128]{3,2,1,0:T(1,128)S(1)}, u32[]{:S(2)}, u32[]{:S(2)}) async-start(f32[64,17,1,128]{3,2,1,0:T(1,128)} %bitcast.5), calls=%async_computation.1 | async-start | bytes 1114112 | tf_op jit(solution)/shard_map/all_to_all | solution.py:530
  41.7 5.6 %copy-start.6 = (f32[128,512]{1,0:T(8,128)S(1)}, f32[128,512]{1,0:T(8,128)}, u32[]{:S(2)}) copy-start(f32[128,512]{1,0:T(8,128)} %f4.3) | copy-start | bytes 786436
  41.7 5.6 %copy-start.9 = (f32[48,128]{1,0:T(8,128)S(1)}, f32[48,128]{1,0:T(8,128)}, u32[]{:S(2)}) copy-start(f32[48,128]{1,0:T(8,128)} %copy-done.8) | copy-start | bytes 73732
  41.8 11.3 %copy-start = (bf16[32,128,128]{2,1,0:T(8,128)(2,1)S(1)}, bf16[32,128,128]{2,1,0:T(8,128)(2,1)}, u32[]{:S(2)}) copy-start(bf16[32,128,128]{2,1,0:T(8,128)(2,1)} %inverse.1) | copy-start | bytes 3145732
  41.8 12.1 %collective-permute-start.4 = (f32[64,128]{1,0:T(8,128)S(1)}, f32[64,128]{1,0:T(8,128)S(1)}, u32[]{:S(2)}, u32[]{:S(2)}) collective-permute-start(f32[64,128]{1,0:T(8,128)S(1)} %slice_bitcast_fusion.own), channel_id=1, source_target_pairs={{0,1},{1,0},{2,3},{3,2},{4,5},{5,4},{6,7},{7,6},{8,9},{9,8},{10,11... | collective-permute-start | bytes 98312 | tf_op jit(solution)/shard_map/ppermute | solution.py:549
  44.5 9.4 %collective-permute-start.5 = (f32[64,128]{1,0:T(8,128)S(1)}, f32[64,128]{1,0:T(8,128)S(1)}, u32[]{:S(2)}, u32[]{:S(2)}) collective-permute-start(f32[64,128]{1,0:T(8,128)S(1)} %slice_bitcast_fusion.own), channel_id=1, source_target_pairs={{0,2},{1,3},{2,0},{3,1},{4,6},{5,7},{6,4},{7,5},{8,10},{9,11},{10,... | collective-permute-start | bytes 98312 | tf_op jit(solution)/shard_map/ppermute | solution.py:549
  46.6 7.4 %collective-permute-start.6 = (f32[64,128]{1,0:T(8,128)S(1)}, f32[64,128]{1,0:T(8,128)S(1)}, u32[]{:S(2)}, u32[]{:S(2)}) collective-permute-start(f32[64,128]{1,0:T(8,128)S(1)} %slice_bitcast_fusion.own), channel_id=1, source_target_pairs={{0,3},{1,2},{2,1},{3,0},{4,7},{5,6},{6,5},{7,4},{8,11},{9,10},{10,... | collective-permute-start | bytes 98312 | tf_op jit(solution)/shard_map/ppermute | solution.py:549
  53.1 0.8 %copy-start.12 = (f32[128,512]{1,0:T(8,128)}, f32[128,512]{1,0:T(8,128)S(1)}, u32[]{:S(2)}) copy-start(f32[128,512]{1,0:T(8,128)S(1)} %get-tuple-element.23.water) | copy-start | bytes 786436
  56.7 8.2 %copy-start.13 = (f32[128,512]{1,0:T(8,128)S(1)}, f32[128,512]{1,0:T(8,128)}, u32[]{:S(2)}) copy-start(f32[128,512]{1,0:T(8,128)} %copy-done.12) | copy-start | bytes 786436
  60.2 5.9 %collective-permute-start.7 = (f32[8,128]{1,0:T(8,128)S(1)}, f32[8,128]{1,0:T(8,128)S(1)}, u32[]{:S(2)}, u32[]{:S(2)}) collective-permute-start(f32[8,128]{1,0:T(8,128)S(1)} %gather_kernel.1.own), channel_id=1, source_target_pairs={{0,3},{1,2},{2,1},{3,0},{4,7},{5,6},{6,5},{7,4},{8,11},{9,10},{10,... | collective-permute-start | bytes 12296 | tf_op jit(solution)/shard_map/ppermute | solution.py:557
  63.2 5.1 %collective-permute-start.8 = (f32[8,128]{1,0:T(8,128)S(1)}, f32[8,128]{1,0:T(8,128)S(1)}, u32[]{:S(2)}, u32[]{:S(2)}) collective-permute-start(f32[8,128]{1,0:T(8,128)S(1)} %gather_kernel.1.own), channel_id=1, source_target_pairs={{0,2},{1,3},{2,0},{3,1},{4,6},{5,7},{6,4},{7,5},{8,10},{9,11},{10,... | collective-permute-start | bytes 12296 | tf_op jit(solution)/shard_map/ppermute | solution.py:557
  64.9 3.6 %collective-permute-start.9 = (f32[8,128]{1,0:T(8,128)S(1)}, f32[8,128]{1,0:T(8,128)S(1)}, u32[]{:S(2)}, u32[]{:S(2)}) collective-permute-start(f32[8,128]{1,0:T(8,128)S(1)} %gather_kernel.1.own), channel_id=1, source_target_pairs={{0,1},{1,0},{2,3},{3,2},{4,5},{5,4},{6,7},{7,6},{8,9},{9,8},{10,11... | collective-permute-start | bytes 12296 | tf_op jit(solution)/shard_map/ppermute | solution.py:557

commit v11 on v10

--- a/solution.py
+++ b/solution.py
@@ -152,20 +152,18 @@
         copy.wait()
 
 
-def lateral_kernel(rows_in, section, reach_source, last_row, order0, order1, out, source):
+def lateral_kernel(
+    rows_in, section, reach_source, last_row, spread, seats, order0, order1, out, source
+):
     total = rows_in.shape[0]
     tiles = total // CHUNK
     blocks = section.shape[0]
-    slot = iota((total, 1), 0).astype(F32)
-    owner = jnp.floor((slot + 0.5) * (1.0 / CHUNK))
-    within = slot - owner * CHUNK + ID_LANE
     lane = iota((total, LANES), 1).astype(F32)
     extras = rows_in[pl.ds(SLOTS, tiles, CHUNK), :]
     ids_here = iota((tiles, LANES), 1)
     ids_here = (ids_here >= ID_LANE) & (ids_here < ID_LANE + SLOTS)
     ids = jnp.where(ids_here, extras, 0.0).astype(BF16)
-    spread = (iota((total, tiles), 1).astype(F32) == owner).astype(F32).astype(BF16)
-    seat = jnp.where(lane == within, mm(spread, ids), 0.0)
+    seat = seats[...] * mm(spread[...], ids)
     block = mm(seat.astype(BF16), jnp.ones((LANES, LANES), BF16)) - 1.0
     hot = (block == lane).astype(F32).astype(BF16)
     rows = rows_in[...]
@@ -282,7 +280,13 @@
     out[...] = base[...] + column[...] * inflow
 
 
-def hot_kernel(slots, out):
+def hot_kernel(slots, out, spread, seats):
+    total, tiles = spread.shape
+    slot = iota((total, 1), 0).astype(F32)
+    owner = jnp.floor((slot + 0.5) * (1.0 / CHUNK))
+    within = slot - owner * CHUNK + ID_LANE
+    spread[...] = (iota((total, tiles), 1).astype(F32) == owner).astype(F32).astype(BF16)
+    seats[...] = (iota((total, LANES), 1).astype(F32) == within).astype(F32)
     slot_c = jnp.transpose(slots[...])[:, 0:1]
     hot = iota(out.shape, 1).astype(F32) == slot_c
     out[...] = jnp.where(hot, 1.0, 0.0).astype(BF16)
@@ -511,8 +515,16 @@
 
     got_a = lax.ppermute(edge_a, "band", pairs(bands, 0))
     got_b = lax.ppermute(edge_b, "band", pairs(bands, 1))
-    hot = call(
-        hot_kernel, jax.ShapeDtypeStruct((links, total), BF16), [VMEM], flops=10**8, size=10**6
+    hot, spread, seats = call(
+        hot_kernel,
+        (
+            jax.ShapeDtypeStruct((links, total), BF16),
+            jax.ShapeDtypeStruct((total, tiles), BF16),
+            shaped(total, LANES),
+        ),
+        [VMEM],
+        flops=10**8,
+        size=10**6,
     )(slots)
     side_a, side_b = call(
         strips_kernel, (shaped(48, LANES), shaped(48, LANES)), [VMEM] * 7 + [ANY], flops=10**6, size=10**6
@@ -523,10 +535,10 @@
     answer, source = call(
         lateral_kernel,
         (shaped(total, LANES), shaped(blocks, LANES)),
-        [VMEM] * 4 + [ANY] * 2,
+        [VMEM] * 6 + [ANY] * 2,
         flops=10**9,
         size=10**6,
-    )(rows_in.reshape(total, LANES), river_section, reach_source, last_row, col_a, col_b)
+    )(rows_in.reshape(total, LANES), river_section, reach_source, last_row, spread, seats, col_a, col_b)
     returned = lax.all_to_all(
         answer.reshape(tiles, CHUNK, 1, LANES), "tile", split_axis=0, concat_axis=0, tiled=True
     )

time: 69.7 us -> 71.8 us (1.030)
  local copies, waits for them, and re-layouts: 0.85 us -> 3.77 us
  waiting for transfers between devices: 17.6 us -> 16.3 us
    unnamed x30 -> x34, local copies, waits for them, and re-layouts: 0.8 us -> 3.71 us
    ppermute x1, waiting for transfers between devices: 1.35 us -> 0.26 us  [per_device(): got_a = lax.ppermute(edge_a, 'band', pairs(bands, 0))]
where the time goes in v11:
time: 71.8 us; the launch traced here: 71.3 us
  starting transfers between devices  33.2 us (46%)
  Pallas kernels  17.1 us (24%)
  waiting for transfers between devices  16.3 us (23%)
  local copies, waits for them, and re-layouts  3.77 us (5%)
  between operations  0.93 us (1%)
    all_to_all x1, starting transfers between devices, per_device(): lax.all_to_all(payload.reshape(tiles, CHUNK, 1, LANES), 'tile', split_axi...  12.2 us
    all_to_all x1, waiting for transfers between devices, per_device(): lax.all_to_all(payload.reshape(tiles, CHUNK, 1, LANES), 'tile', split_axi...  7.38 us
    all_to_all x1, starting transfers between devices, per_device(): lax.all_to_all(answer.reshape(tiles, CHUNK, 1, LANES), 'tile', split_axis...  5.98 us
    pallas_call x1, Pallas kernels, per_device(): call(flood_kernel, (shaped(height, width),) * 3, [VMEM] * 9, scratch=[plt...  5.85 us
    ppermute x3, starting transfers between devices, per_device(): others = [lax.ppermute(extras, 'band', ring[k]) for k in (3, 2, 1)][::-1]  5.52 us
    ppermute x3, starting transfers between devices, per_device(): lax.ppermute(pushed, 'band', ring[k])  4.74 us
    unnamed x34, local copies, waits for them, and re-layouts  3.71 us
    all_to_all x1, waiting for transfers between devices, per_device(): lax.all_to_all(answer.reshape(tiles, CHUNK, 1, LANES), 'tile', split_axis...  3.21 us
  transfers between devices with their start and end apart: 12, of which 6 were waited for; matrix products, arithmetic and copies ran while one was open for 0% of the time, Pallas kernels for 16%

profile of v11, /device:TPU:2, one launch (start us, length us, event | category | flops | bytes accessed | tf_op | source)
XLA Modules:
  0.0 71.3 jit_solution(7456840572086562785)
XLA Ops:
  0.6 2.9 %pack_kernel.1 = (f32[1088,128]{1,0:T(8,128)}, f32[8,512]{1,0:T(8,128)}, f32[32,128]{1,0:T(8,128)}, f32[40,512]{1,0:T(8,128)}, f32[40,512]{1,0:T(8,128)}) custom-call(f32[128,512]{1,0:T(8,128)} %f0.3, f32[128,512]{1,0:T(8,128)} %f1.3, s32[1,512]{1,0:T(1,128)} %bitcast.17, s32[1,512]{1,0:T(1,128)} %bitcast.18, bf16[32,128,128]{2,1,0:T(8,128)(2,1)} %inverse.1, ...), custom_call_target="tpu_custom_call" | custom-call | flops 1000000000 | bytes 1000000 | tf_op jit(solution)/shard_map/pack_kernel/pallas_call | solution.py:473
  3.6 12.2 %all-to-all-start = ((f32[64,17,1,128]{3,2,1,0:T(1,128)}), f32[64,17,1,128]{3,2,1,0:T(1,128)S(1)}, u32[]{:S(2)}, u32[]{:S(2)}) async-start(f32[64,17,1,128]{3,2,1,0:T(1,128)} %bitcast.16), calls=%async_computation | async-start | bytes 1114112 | tf_op jit(solution)/shard_map/all_to_all | solution.py:508
  15.8 1.7 %collective-permute-start = (f32[40,512]{1,0:T(8,128)}, f32[40,512]{1,0:T(8,128)S(1)}, u32[]{:S(2)}, u32[]{:S(2)}) collective-permute-start(f32[40,512]{1,0:T(8,128)} %get-tuple-element.21), channel_id=1, source_target_pairs={{1,0},{0,1},{3,2},{2,3},{5,4},{4,5},{7,6},{6,7},{9,8},{8,9},{11,10... | collective-permute-start | bytes 245768 | tf_op jit(solution)/shard_map/ppermute | solution.py:516
  17.5 0.7 collective-permute-start.1
  18.1 0.7 copy-done.15
  18.8 0.8 %hot_kernel.1 = (bf16[512,1088]{1,0:T(8,128)(2,1)S(1)}, bf16[1088,64]{1,0:T(8,128)(2,1)S(1)}, f32[1088,128]{1,0:T(8,128)S(1)}) custom-call(f32[8,512]{1,0:T(8,128)S(1)} %copy-done.15), custom_call_target="tpu_custom_call" | custom-call | flops 100000000 | bytes 1000000 | tf_op jit(solution)/shard_map/hot_kernel/pallas_call | solution.py:518
  19.6 0.7 copy-done.13
  20.3 0.3 collective-permute-done.got_a
  20.7 0.2 strips_kernel.1
  20.9 0.2 copy-done.11
  21.1 2.5 %collective-permute-start.3 = (f32[48,128]{1,0:T(8,128)S(1)}, f32[48,128]{1,0:T(8,128)S(1)}, u32[]{:S(2)}, u32[]{:S(2)}) collective-permute-start(f32[48,128]{1,0:T(8,128)S(1)} %get-tuple-element.26), channel_id=1, source_target_pairs={{8,4},{4,8},{16,12},{12,16},{24,20},{20,24},{32,28},{28,32},{40,36... | collective-permute-start | bytes 73736 | tf_op jit(solution)/shard_map/ppermute | solution.py:533
  23.6 3.0 %collective-permute-done.3.col_b.order1 = f32[48,128]{1,0:T(8,128)S(1)} collective-permute-done((f32[48,128]{1,0:T(8,128)S(1)}, f32[48,128]{1,0:T(8,128)S(1)}, u32[]{:S(2)}, u32[]{:S(2)}) %collective-permute-start.3) | collective-permute-done | bytes 24608 | tf_op jit(solution)/shard_map/ppermute | solution.py:533
  26.7 7.4 %all-to-all-done = f32[64,17,1,128]{3,2,1,0:T(1,128)S(1)} async-done(((f32[64,17,1,128]{3,2,1,0:T(1,128)}), f32[64,17,1,128]{3,2,1,0:T(1,128)S(1)}, u32[]{:S(2)}, u32[]{:S(2)}) %all-to-all-start) | async-done | bytes 557088 | tf_op jit(solution)/shard_map/all_to_all | solution.py:508
  34.1 1.0 %copy-done.12 = f32[1088,128]{1,0:T(8,128)S(1)} copy-done((f32[1088,128]{1,0:T(8,128)S(1)}, f32[1088,128]{1,0:T(8,128)}, u32[]{:S(2)}) %copy-start.12) | copy-done | bytes 557080
  35.1 1.0 %copy-done.14 = bf16[1088,64]{1,0:T(8,128)(2,1)S(1)} copy-done((bf16[1088,64]{1,0:T(8,128)(2,1)S(1)}, bf16[1088,64]{1,0:T(8,128)(2,1)}, u32[]{:S(2)}) %copy-start.14) | copy-done | bytes 139288
  36.1 1.6 %lateral_kernel.1 = (f32[1088,128]{1,0:T(8,128)}, f32[32,128]{1,0:T(8,128)S(1)}) custom-call(f32[1088,128]{1,0:T(8,128)S(1)} %bitcast.14, f32[32,128]{1,0:T(8,128)S(1)} %copy-done.9, f32[32,128]{1,0:T(8,128)S(1)} %copy-done.10, f32[32,128]{1,0:T(8,128)S(1)} %copy-done.16, bf16[1088,64]{1,0:T(8,128)(2,1)S(1)} %copy-done.14, f32[1088,128]{1,0:T(8,128)S(1)} %copy-done.12, ...), custom_call_target="tpu_custom_call" | custom-call | flops 1000000000 | bytes 1000000 | tf_op jit(solution)/shard_map/lateral_kernel/pallas_call | solution.py:535
  37.7 6.0 %all-to-all-start.1 = ((f32[64,17,1,128]{3,2,1,0:T(1,128)}), f32[64,17,1,128]{3,2,1,0:T(1,128)S(1)}, u32[]{:S(2)}, u32[]{:S(2)}) async-start(f32[64,17,1,128]{3,2,1,0:T(1,128)} %bitcast.5), calls=%async_computation.1 | async-start | bytes 1114112 | tf_op jit(solution)/shard_map/all_to_all | solution.py:542
  43.7 0.1 copy.24
  43.8 2.7 %collective-permute-start.4 = (f32[64,128]{1,0:T(8,128)S(1)}, f32[64,128]{1,0:T(8,128)S(1)}, u32[]{:S(2)}, u32[]{:S(2)}) collective-permute-start(f32[64,128]{1,0:T(8,128)S(1)} %slice_bitcast_fusion.own), channel_id=1, source_target_pairs={{0,1},{1,0},{2,3},{3,2},{4,5},{5,4},{6,7},{7,6},{8,9},{9,8},{10,11... | collective-permute-start | bytes 98312 | tf_op jit(solution)/shard_map/ppermute | solution.py:561
  46.5 2.1 %collective-permute-start.5 = (f32[64,128]{1,0:T(8,128)S(1)}, f32[64,128]{1,0:T(8,128)S(1)}, u32[]{:S(2)}, u32[]{:S(2)}) collective-permute-start(f32[64,128]{1,0:T(8,128)S(1)} %slice_bitcast_fusion.own), channel_id=1, source_target_pairs={{0,2},{1,3},{2,0},{3,1},{4,6},{5,7},{6,4},{7,5},{8,10},{9,11},{10,... | collective-permute-start | bytes 98312 | tf_op jit(solution)/shard_map/ppermute | solution.py:561
  48.6 0.7 collective-permute-start.6
  49.3 5.8 %flood_kernel.1 = (f32[128,512]{1,0:T(8,128)S(1)}, f32[128,512]{1,0:T(8,128)}, f32[128,512]{1,0:T(8,128)}) custom-call(f32[40,512]{1,0:T(8,128)S(1)} %collective-permute-done.got_a, f32[40,512]{1,0:T(8,128)S(1)} %collective-permute-done.1.got_b, f32[48,128]{1,0:T(8,128)S(1)} %collective-permute-done.2.col_a.order0, f32[48,128]{1,0:T(8,128)S(1)} %copy-done.8, ...), custom_call_target="tpu_custom_call" | custom-call | flops 100000000 | bytes 10000000 | tf_op jit(solution)/shard_map/flood_kernel/pallas_call | solution.py:548
  55.1 0.8 %flow_kernel.1 = (f32[32,128]{1,0:T(8,128)S(1)}, f32[32,128]{1,0:T(8,128)S(1)}) custom-call(f32[32,128]{1,0:T(8,128)S(1)} %get-tuple-element.35.source, bf16[32,128,128]{2,1,0:T(8,128)(2,1)S(1)} %copy-done), custom_call_target="tpu_custom_call" | custom-call | flops 100000000 | bytes 1000000 | tf_op jit(solution)/shard_map/flow_kernel/pallas_call | solution.py:557
  56.0 2.7 %paths_kernel.1.reach = f32[128,2048]{1,0:T(8,128)S(1)} custom-call(f32[64,128]{1,0:T(8,128)S(1)} %slice_bitcast_fusion.own, f32[64,128]{1,0:T(8,128)S(1)} %collective-permute-done.4.one, f32[64,128]{1,0:T(8,128)S(1)} %collective-permute-done.5.two, f32[64,128]{1,0:T(8,128)S(1)} %collective-permute-done.6.three), custom_call_target="tpu_custom_call" | custom-call | flops 1000000000 | bytes 1000000 | tf_op jit(solution)/shard_map/paths_kernel/pallas_call | solution.py:562
  58.7 3.2 %all-to-all-done.1 = f32[64,17,1,128]{3,2,1,0:T(1,128)S(1)} async-done(((f32[64,17,1,128]{3,2,1,0:T(1,128)}), f32[64,17,1,128]{3,2,1,0:T(1,128)S(1)}, u32[]{:S(2)}, u32[]{:S(2)}) %all-to-all-start.1) | async-done | bytes 557088 | tf_op jit(solution)/shard_map/all_to_all | solution.py:542
  61.9 0.3 gather_kernel.1.own
  62.2 3.0 %collective-permute-start.7 = (f32[8,128]{1,0:T(8,128)S(1)}, f32[8,128]{1,0:T(8,128)S(1)}, u32[]{:S(2)}, u32[]{:S(2)}) collective-permute-start(f32[8,128]{1,0:T(8,128)S(1)} %gather_kernel.1.own), channel_id=1, source_target_pairs={{0,3},{1,2},{2,1},{3,0},{4,7},{5,6},{6,5},{7,4},{8,11},{9,10},{10,... | collective-permute-start | bytes 12296 | tf_op jit(solution)/shard_map/ppermute | solution.py:569
  65.2 1.7 %collective-permute-start.8 = (f32[8,128]{1,0:T(8,128)S(1)}, f32[8,128]{1,0:T(8,128)S(1)}, u32[]{:S(2)}, u32[]{:S(2)}) collective-permute-start(f32[8,128]{1,0:T(8,128)S(1)} %gather_kernel.1.own), channel_id=1, source_target_pairs={{0,2},{1,3},{2,0},{3,1},{4,6},{5,7},{6,4},{7,5},{8,10},{9,11},{10,... | collective-permute-start | bytes 12296 | tf_op jit(solution)/shard_map/ppermute | solution.py:569
  66.9 1.2 %final_kernel.1 = f32[128,512]{1,0:T(8,128)} custom-call(f32[128,512]{1,0:T(8,128)S(1)} %get-tuple-element.27.water, f32[1088,128]{1,0:T(8,128)S(1)} %bitcast.13, bf16[512,1088]{1,0:T(8,128)(2,1)S(1)} %get-tuple-element.24.order.hot), custom_call_target="tpu_custom_call" | custom-call | flops 1000000000 | bytes 1000000 | tf_op jit(solution)/shard_map/final_kernel/pallas_call | solution.py:570
  68.2 2.2 %collective-permute-done.8.two = f32[8,128]{1,0:T(8,128)S(1)} collective-permute-done((f32[8,128]{1,0:T(8,128)S(1)}, f32[8,128]{1,0:T(8,128)S(1)}, u32[]{:S(2)}, u32[]{:S(2)}) %collective-permute-start.8) | collective-permute-done | bytes 4128 | tf_op jit(solution)/shard_map/ppermute | solution.py:569
  70.3 0.2 collective-permute-done.9.three
  70.5 0.8 %discharge_kernel.1 = f32[32,128]{1,0:T(8,128)} custom-call(f32[32,128]{1,0:T(8,128)S(1)} %get-tuple-element.36.base, f32[32,128]{1,0:T(8,128)S(1)} %get-tuple-element.37.column, f32[8,128]{1,0:T(8,128)S(1)} %gather_kernel.1.own, f32[8,128]{1,0:T(8,128)S(1)} %collective-permute-done.7.one, f32[8,128]{1,0:T(8,128)S(1)} %collective-permute-done.8.two, ...), custom_call_target="tpu_custom_call" | custom-call | flops 10000 | bytes 10000 | tf_op jit(solution)/shard_map/discharge_kernel/pallas_call | solution.py:573
  (38 shorter events, 0.1 us)
Async XLA Ops:
  3.6 17.0 %copy-start.1 = (f32[128,512]{1,0:T(8,128)S(1)}, f32[128,512]{1,0:T(8,128)}, u32[]{:S(2)}) copy-start(f32[128,512]{1,0:T(8,128)} %f0.3) | copy-start | bytes 786436
  3.6 17.0 %copy-start.2 = (f32[128,512]{1,0:T(8,128)S(1)}, f32[128,512]{1,0:T(8,128)}, u32[]{:S(2)}) copy-start(f32[128,512]{1,0:T(8,128)} %f1.3) | copy-start | bytes 786436
  3.6 17.0 %copy-start.3 = (f32[128,512]{1,0:T(8,128)S(1)}, f32[128,512]{1,0:T(8,128)}, u32[]{:S(2)}) copy-start(f32[128,512]{1,0:T(8,128)} %f2.3) | copy-start | bytes 786436
  3.6 17.0 %copy-start.4 = (f32[128,512]{1,0:T(8,128)S(1)}, f32[128,512]{1,0:T(8,128)}, u32[]{:S(2)}) copy-start(f32[128,512]{1,0:T(8,128)} %f3.3) | copy-start | bytes 786436
  3.6 17.0 %copy-start.5 = (f32[128,512]{1,0:T(8,128)S(1)}, f32[128,512]{1,0:T(8,128)}, u32[]{:S(2)}) copy-start(f32[128,512]{1,0:T(8,128)} %f4.3) | copy-start | bytes 786436
  3.6 30.4 %all-to-all-start = ((f32[64,17,1,128]{3,2,1,0:T(1,128)}), f32[64,17,1,128]{3,2,1,0:T(1,128)S(1)}, u32[]{:S(2)}, u32[]{:S(2)}) async-start(f32[64,17,1,128]{3,2,1,0:T(1,128)} %bitcast.16), calls=%async_computation | async-start | bytes 1114112 | tf_op jit(solution)/shard_map/all_to_all | solution.py:508
  15.8 4.8 %collective-permute-start = (f32[40,512]{1,0:T(8,128)}, f32[40,512]{1,0:T(8,128)S(1)}, u32[]{:S(2)}, u32[]{:S(2)}) collective-permute-start(f32[40,512]{1,0:T(8,128)} %get-tuple-element.21), channel_id=1, source_target_pairs={{1,0},{0,1},{3,2},{2,3},{5,4},{4,5},{7,6},{6,7},{9,8},{8,9},{11,10... | collective-permute-start | bytes 245768 | tf_op jit(solution)/shard_map/ppermute | solution.py:516
  17.5 3.1 %collective-permute-start.1 = (f32[40,512]{1,0:T(8,128)}, f32[40,512]{1,0:T(8,128)S(1)}, u32[]{:S(2)}, u32[]{:S(2)}) collective-permute-start(f32[40,512]{1,0:T(8,128)} %get-tuple-element.22), channel_id=1, source_target_pairs={{2,1},{1,2},{6,5},{5,6},{10,9},{9,10},{14,13},{13,14},{18,17},{17,... | collective-permute-start | bytes 245768 | tf_op jit(solution)/shard_map/ppermute | solution.py:517
  18.1 0.7 %copy-start.15 = (f32[8,512]{1,0:T(8,128)S(1)}, f32[8,512]{1,0:T(8,128)}, u32[]{:S(2)}) copy-start(f32[8,512]{1,0:T(8,128)} %get-tuple-element.23.slots) | copy-start | bytes 49156
  19.6 0.7 copy-start.13
  20.3 0.8 %copy-start.11 = (f32[1088,128]{1,0:T(8,128)}, f32[1088,128]{1,0:T(8,128)S(1)}, u32[]{:S(2)}) copy-start(f32[1088,128]{1,0:T(8,128)S(1)} %get-tuple-element.31.seats) | copy-start | bytes 1671172
  20.6 13.4 %copy-start.9 = (f32[32,128]{1,0:T(8,128)S(1)}, f32[32,128]{1,0:T(8,128)}, u32[]{:S(2)}) copy-start(f32[32,128]{1,0:T(8,128)} %section.1) | copy-start | bytes 49156
  20.6 13.4 %copy-start.10 = (f32[32,128]{1,0:T(8,128)S(1)}, f32[32,128]{1,0:T(8,128)}, u32[]{:S(2)}) copy-start(f32[32,128]{1,0:T(8,128)} %reach_source.1) | copy-start | bytes 49156
  20.7 13.4 %copy-start.16 = (f32[32,128]{1,0:T(8,128)S(1)}, f32[32,128]{1,0:T(8,128)}, u32[]{:S(2)}) copy-start(f32[32,128]{1,0:T(8,128)} %get-tuple-element.29.last_row) | copy-start | bytes 49156
  21.1 2.5 %collective-permute-start.2 = (f32[48,128]{1,0:T(8,128)S(1)}, f32[48,128]{1,0:T(8,128)S(1)}, u32[]{:S(2)}, u32[]{:S(2)}) collective-permute-start(f32[48,128]{1,0:T(8,128)S(1)} %get-tuple-element.25), channel_id=1, source_target_pairs={{4,0},{0,4},{12,8},{8,12},{20,16},{16,20},{28,24},{24,28},{36,32},... | collective-permute-start | bytes 73736 | tf_op jit(solution)/shard_map/ppermute | solution.py:532
  21.1 5.5 %collective-permute-start.3 = (f32[48,128]{1,0:T(8,128)S(1)}, f32[48,128]{1,0:T(8,128)S(1)}, u32[]{:S(2)}, u32[]{:S(2)}) collective-permute-start(f32[48,128]{1,0:T(8,128)S(1)} %get-tuple-element.26), channel_id=1, source_target_pairs={{8,4},{4,8},{16,12},{12,16},{24,20},{20,24},{32,28},{28,32},{40,36... | collective-permute-start | bytes 73736 | tf_op jit(solution)/shard_map/ppermute | solution.py:533
  26.7 11.0 %copy-start.7 = (f32[48,128]{1,0:T(8,128)}, f32[48,128]{1,0:T(8,128)S(1)}, u32[]{:S(2)}) copy-start(f32[48,128]{1,0:T(8,128)S(1)} %collective-permute-done.3.col_b.order1) | copy-start | bytes 73732
  34.1 1.1 %copy-start.12 = (f32[1088,128]{1,0:T(8,128)S(1)}, f32[1088,128]{1,0:T(8,128)}, u32[]{:S(2)}) copy-start(f32[1088,128]{1,0:T(8,128)} %copy-done.11) | copy-start | bytes 1671172
  35.1 1.0 %copy-start.14 = (bf16[1088,64]{1,0:T(8,128)(2,1)S(1)}, bf16[1088,64]{1,0:T(8,128)(2,1)}, u32[]{:S(2)}) copy-start(bf16[1088,64]{1,0:T(8,128)(2,1)} %copy-done.13) | copy-start | bytes 417796
  37.7 24.3 %all-to-all-start.1 = ((f32[64,17,1,128]{3,2,1,0:T(1,128)}), f32[64,17,1,128]{3,2,1,0:T(1,128)S(1)}, u32[]{:S(2)}, u32[]{:S(2)}) async-start(f32[64,17,1,128]{3,2,1,0:T(1,128)} %bitcast.5), calls=%async_computation.1 | async-start | bytes 1114112 | tf_op jit(solution)/shard_map/all_to_all | solution.py:542
  43.7 5.6 %copy-start.6 = (f32[128,512]{1,0:T(8,128)S(1)}, f32[128,512]{1,0:T(8,128)}, u32[]{:S(2)}) copy-start(f32[128,512]{1,0:T(8,128)} %f4.3) | copy-start | bytes 786436
  43.7 5.6 %copy-start.8 = (f32[48,128]{1,0:T(8,128)S(1)}, f32[48,128]{1,0:T(8,128)}, u32[]{:S(2)}) copy-start(f32[48,128]{1,0:T(8,128)} %copy-done.7) | copy-start | bytes 73732
  43.8 11.4 %copy-start = (bf16[32,128,128]{2,1,0:T(8,128)(2,1)S(1)}, bf16[32,128,128]{2,1,0:T(8,128)(2,1)}, u32[]{:S(2)}) copy-start(bf16[32,128,128]{2,1,0:T(8,128)(2,1)} %inverse.1) | copy-start | bytes 3145732
  43.8 12.2 %collective-permute-start.4 = (f32[64,128]{1,0:T(8,128)S(1)}, f32[64,128]{1,0:T(8,128)S(1)}, u32[]{:S(2)}, u32[]{:S(2)}) collective-permute-start(f32[64,128]{1,0:T(8,128)S(1)} %slice_bitcast_fusion.own), channel_id=1, source_target_pairs={{0,1},{1,0},{2,3},{3,2},{4,5},{5,4},{6,7},{7,6},{8,9},{9,8},{10,11... | collective-permute-start | bytes 98312 | tf_op jit(solution)/shard_map/ppermute | solution.py:561
  46.5 9.4 %collective-permute-start.5 = (f32[64,128]{1,0:T(8,128)S(1)}, f32[64,128]{1,0:T(8,128)S(1)}, u32[]{:S(2)}, u32[]{:S(2)}) collective-permute-start(f32[64,128]{1,0:T(8,128)S(1)} %slice_bitcast_fusion.own), channel_id=1, source_target_pairs={{0,2},{1,3},{2,0},{3,1},{4,6},{5,7},{6,4},{7,5},{8,10},{9,11},{10,... | collective-permute-start | bytes 98312 | tf_op jit(solution)/shard_map/ppermute | solution.py:561
  48.6 7.4 %collective-permute-start.6 = (f32[64,128]{1,0:T(8,128)S(1)}, f32[64,128]{1,0:T(8,128)S(1)}, u32[]{:S(2)}, u32[]{:S(2)}) collective-permute-start(f32[64,128]{1,0:T(8,128)S(1)} %slice_bitcast_fusion.own), channel_id=1, source_target_pairs={{0,3},{1,2},{2,1},{3,0},{4,7},{5,6},{6,5},{7,4},{8,11},{9,10},{10,... | collective-permute-start | bytes 98312 | tf_op jit(solution)/shard_map/ppermute | solution.py:561
  62.2 6.0 %collective-permute-start.7 = (f32[8,128]{1,0:T(8,128)S(1)}, f32[8,128]{1,0:T(8,128)S(1)}, u32[]{:S(2)}, u32[]{:S(2)}) collective-permute-start(f32[8,128]{1,0:T(8,128)S(1)} %gather_kernel.1.own), channel_id=1, source_target_pairs={{0,3},{1,2},{2,1},{3,0},{4,7},{5,6},{6,5},{7,4},{8,11},{9,10},{10,... | collective-permute-start | bytes 12296 | tf_op jit(solution)/shard_map/ppermute | solution.py:569
  65.2 5.1 %collective-permute-start.8 = (f32[8,128]{1,0:T(8,128)S(1)}, f32[8,128]{1,0:T(8,128)S(1)}, u32[]{:S(2)}, u32[]{:S(2)}) collective-permute-start(f32[8,128]{1,0:T(8,128)S(1)} %gather_kernel.1.own), channel_id=1, source_target_pairs={{0,2},{1,3},{2,0},{3,1},{4,6},{5,7},{6,4},{7,5},{8,10},{9,11},{10,... | collective-permute-start | bytes 12296 | tf_op jit(solution)/shard_map/ppermute | solution.py:569
  66.9 3.6 %collective-permute-start.9 = (f32[8,128]{1,0:T(8,128)S(1)}, f32[8,128]{1,0:T(8,128)S(1)}, u32[]{:S(2)}, u32[]{:S(2)}) collective-permute-start(f32[8,128]{1,0:T(8,128)S(1)} %gather_kernel.1.own), channel_id=1, source_target_pairs={{0,1},{1,0},{2,3},{3,2},{4,5},{5,4},{6,7},{7,6},{8,9},{9,8},{10,11... | collective-permute-start | bytes 12296 | tf_op jit(solution)/shard_map/ppermute | solution.py:569
